TPU v7x, 128 devices: a whole 4x4x4 slice. The times are simulated.
128 devices in a mesh: rows: 32 (over z, x, core), vec: 4 (over y).
Axes of the slice: x: 4, y: 4, z: 4, core: 2. Of those that a mesh axis runs over, the one named last changes fastest.
Arguments:
- lattice_state: float32 [2, 512, 4096], P(None, 'rows'), may hold values from -0.6 to 0.6
- constant_field: float32 [2, 512, 4096], P(None, 'rows'), may hold values from -0.4 to 0.4
- tangents: float32 [32, 2, 512, 4096], P('vec', None, 'rows'), may hold values from -6 to 6
Outputs:
- next_state: float32 [2, 512, 4096], P(None, 'rows')
- basis: float32 [32, 2, 512, 4096], P('vec', None, 'rows')
- growth: float32 [32], replicated
All inputs are finite; a program needn't handle non-finite values.
Results may differ from a plain program's by a relative error of at most 0.00028.
Values sent between devices are 32-bit elements; how exact they have to be, the bound alone decides.
No kernel may reach another device: no remote copies, remote signals or barrier semaphores. Data moves between devices by JAX's collectives and lax.ppermute only.
A program may use at most 128 MiB of HBM per device.

v0:
```python
import math

import jax
import jax.numpy as jnp
from jax import lax
from jax.sharding import PartitionSpec as P

NV = 32
STEPS = 3


COUPLING = 0.35


def with_halo(block, sides, width):
    for axis, dim in sides:
        count = lax.axis_size(axis)
        forward = [(i, i + 1) for i in range(count - 1)]
        forward.append((count - 1, 0))
        backward = [(target, source) for source, target in forward]
        low = lax.ppermute(
            lax.slice_in_dim(block, block.shape[dim] - width, None, axis=dim), axis, forward
        )
        high = lax.ppermute(lax.slice_in_dim(block, 0, width, axis=dim), axis, backward)
        block = jnp.concatenate([low, block, high], axis=dim)
    return block


def site_terms(current, driven, constant_field):
    real_z = current[0]
    imag_z = current[1]
    map_real = real_z * real_z - imag_z * imag_z + constant_field[0]
    map_imag = 2.0 * real_z * imag_z + constant_field[1]
    real_u = driven[:, 0]
    imag_u = driven[:, 1]
    push_real = 2.0 * (real_z * real_u - imag_z * imag_u)
    push_imag = 2.0 * (real_z * imag_u + imag_z * real_u)
    return jnp.concatenate(
        [jnp.stack([map_real, map_imag])[None], jnp.stack([push_real, push_imag], axis=1)], 0
    )


def mix_rows(padded):
    middle = padded[:, :, 1:-1]
    beside = (
        padded[:, :, :-2] + padded[:, :, 2:] + jnp.roll(middle, 1, -1) + jnp.roll(middle, -1, -1)
    )
    return (1.0 - COUPLING) * middle + COUPLING / 4.0 * beside


def local_gram(vectors):
    return jnp.einsum("jabc,kabc->jk", vectors, vectors, precision=lax.Precision.HIGHEST)


def combine_factor(partial_gram):
    return jnp.linalg.cholesky(lax.psum(partial_gram, ("rows", "vec")))


def per_device(lattice_state, constant_field, tangents):
    stacked = jnp.concatenate([lattice_state[None], tangents], 0)
    for lattice_step in range(STEPS):
        terms = site_terms(stacked[0], stacked[1:], constant_field)
        padded = with_halo(terms, (("rows", 2),), 1)
        stacked = mix_rows(padded)
    next_state = stacked[0]
    advanced = stacked[1:]
    own_count = advanced.shape[0]
    total_rows = advanced.shape[2] * lax.axis_size("rows")
    norm_scale = math.sqrt(2.0 * total_rows * advanced.shape[3])
    identity = jnp.eye(NV, dtype=jnp.float32)
    gathered = lax.all_gather(advanced, "vec", axis=0, tiled=True)
    quarter = gathered.shape[3] // lax.axis_size("vec")
    own_part = lax.dynamic_slice_in_dim(gathered, lax.axis_index("vec") * quarter, quarter, 3)
    factor = combine_factor(local_gram(own_part))
    inverse = jax.scipy.linalg.solve_triangular(factor, identity, lower=True).T
    own_columns = lax.dynamic_slice_in_dim(inverse, lax.axis_index("vec") * own_count, own_count, 1)
    basis = norm_scale * jnp.einsum(
        "jk,jabc->kabc", own_columns, gathered, precision=lax.Precision.HIGHEST
    )
    growth = jnp.log(jnp.diagonal(factor) / norm_scale)
    return (next_state, basis, growth)


def solution(mesh):
    return jax.shard_map(
        per_device,
        mesh=mesh,
        in_specs=(P(None, "rows", None), P(None, "rows", None), P("vec", None, "rows", None)),
        out_specs=(P(None, "rows", None), P("vec", None, "rows", None), P()),
        check_vma=False,
    )
```

profile of v0, /device:TPU:0, one launch (start us, length us, event | category | flops | bytes accessed | tf_op | source)
XLA Modules:
  0.0 369.4 jit_solution(8920721959799482079)
XLA Ops:
  7.2 2.7 fusion.38
  12.0 2.7 subtract_multiply_fusion.2
  17.0 5.8 %collective-permute-start.1 = (f32[9,2,1,4096]{3,0,2,1:T(8,128)}, f32[9,2,1,4096]{3,0,2,1:T(8,128)S(1)}, u32[]{:S(2)}, u32[]{:S(2)}) collective-permute-start(f32[9,2,1,4096]{3,0,2,1:T(8,128)} %get-tuple-element.40), channel_id=1, source_target_pairs={{4,0},{8,4},{12,8},{16,12},{20,16},{24,20},{28,24},{32,28},{36,32}... | collective-permute-start | bytes 884744 | tf_op jit(solution)/shard_map/ppermute | solution.py:24
  23.0 5.1 %fusion.35 = (f32[9,2,16,4095]{3,0,2,1:T(8,128)S(1)}, f32[9,2,16,4095]{3,0,2,1:T(8,128)}) fusion(f32[9,2,16,4096]{3,0,2,1:T(8,128)S(1)} %maximum_maximum_fusion), kind=kLoop, calls=%fused_computation.87 | loop fusion | bytes 18869760 | tf_op jit(solution)/shard_map/jit(_roll_static)/slice | solution.py:46
  28.3 1.4 collective-permute-done.1
  29.7 5.5 %collective-permute-done = f32[9,2,1,4096]{3,0,2,1:T(8,128)} collective-permute-done((f32[9,2,1,4096]{3,0,2,1:T(8,128)}, f32[9,2,1,4096]{3,0,2,1:T(8,128)}, u32[]{:S(2)}, u32[]{:S(2)}) %collective-permute-start) | collective-permute-done | bytes 294944 | tf_op jit(solution)/shard_map/ppermute | solution.py:21
  35.2 12.4 %fusion.14 = f32[9,2,16,4096]{3,0,2,1:T(8,128)S(1)} fusion(f32[9,2,1,4096]{3,0,2,1:T(8,128)S(1)} %collective-permute-done.1, f32[1,2,16,4096]{3,0,2,1:T(1,128)S(1)} %copy.24, f32[8,1,16,4096]{3,0,2,1:T(8,128)S(1)} %get-tuple-element.42, f32[8,1,16,4096]{3,0,2,1:T(8,128)S(1)} %get-tuple-element.41, f32[9,2,1,4096]{3,0,2,1:T(8,128)} %collective-permute-done, ...), kind=kLoop, calls=%fused_computation.28 | loop fusion | flops 18874368 | bytes 19464192 | tf_op jit(solution)/shard_map/add | solution.py:48
  51.3 1.3 maximum_maximum_fusion.1
  54.6 5.1 %fusion.31 = (f32[9,2,16,4095]{3,0,2,1:T(8,128)S(1)}, f32[9,2,16,4095]{3,0,2,1:T(8,128)}) fusion(f32[9,2,16,4096]{3,0,2,1:T(8,128)S(1)} %maximum_maximum_fusion.1), kind=kLoop, calls=%fused_computation.83 | loop fusion | bytes 18869760 | tf_op jit(solution)/shard_map/jit(_roll_static)/slice | solution.py:46
  60.6 5.7 %collective-permute-done.2 = f32[9,2,1,4096]{3,0,2,1:T(8,128)} collective-permute-done((f32[9,2,1,4096]{3,0,2,1:T(8,128)}, f32[9,2,1,4096]{3,0,2,1:T(8,128)}, u32[]{:S(2)}, u32[]{:S(2)}) %collective-permute-start.2) | collective-permute-done | bytes 294944 | tf_op jit(solution)/shard_map/ppermute | solution.py:21
  66.4 12.4 %fusion.9 = f32[9,2,16,4096]{3,0,2,1:T(8,128)S(1)} fusion(f32[9,2,1,4096]{3,0,2,1:T(8,128)S(1)} %collective-permute-done.3, f32[1,2,16,4096]{3,0,2,1:T(1,128)S(1)} %copy.25, f32[8,1,16,4096]{3,0,2,1:T(8,128)S(1)} %get-tuple-element.14, f32[8,1,16,4096]{3,0,2,1:T(8,128)S(1)} %get-tuple-element.13, f32[9,2,1,4096]{3,0,2,1:T(8,128)} %collective-permute-done.2, ...), kind=kLoop, calls=%fused_computation.17 | loop fusion | flops 18874368 | bytes 19464192 | tf_op jit(solution)/shard_map/add | solution.py:48
  85.4 5.1 %fusion.27 = (f32[9,2,16,4095]{3,0,2,1:T(8,128)S(1)}, f32[9,2,16,4095]{3,0,2,1:T(8,128)}) fusion(f32[9,2,16,4096]{3,0,2,1:T(8,128)S(1)} %maximum_maximum_fusion.2), kind=kLoop, calls=%fused_computation.79 | loop fusion | bytes 18869760 | tf_op jit(solution)/shard_map/jit(_roll_static)/slice | solution.py:46
  91.7 5.3 %collective-permute-done.4 = f32[9,2,1,4096]{3,0,2,1:T(8,128)S(1)} collective-permute-done((f32[9,2,1,4096]{3,0,2,1:T(8,128)}, f32[9,2,1,4096]{3,0,2,1:T(8,128)S(1)}, u32[]{:S(2)}, u32[]{:S(2)}) %collective-permute-start.4) | collective-permute-done | bytes 294944 | tf_op jit(solution)/shard_map/ppermute | solution.py:21
  97.0 12.3 %fusion.4 = f32[9,2,16,4096]{3,0,2,1:T(8,128)S(1)} fusion(f32[9,2,1,4096]{3,0,2,1:T(8,128)S(1)} %collective-permute-done.5, f32[1,2,16,4096]{3,0,2,1:T(1,128)S(1)} %copy.26, f32[8,1,16,4096]{3,0,2,1:T(8,128)S(1)} %get-tuple-element.12, f32[8,1,16,4096]{3,0,2,1:T(8,128)S(1)} %get-tuple-element.11, f32[9,2,1,4096]{3,0,2,1:T(8,128)S(1)} %collective-permute-done.4, ...), kind=kLoop, calls=%fused_computation.6 | loop fusion | flops 18874368 | bytes 19464192 | tf_op jit(solution)/shard_map/add | solution.py:48
  109.4 3.2 copy-done
  112.6 2.6 slice.231
  115.2 2.5 slice.230
  118.9 147.0 %all-gather.2.cloned.1.call-done = f32[32,2,16,4096]{3,0,2,1:T(8,128)} async-done(((f32[8,2,16,4096]{3,0,2,1:T(8,128)}), f32[32,2,16,4096]{3,0,2,1:T(8,128)}) %all-gather.2.cloned.1.call-update) | async-done | bytes 16777232 | tf_op jit(solution)/shard_map/all_gather | solution.py:71
  265.9 6.9 %fusion.17 = f32[32,32]{0,1:T(8,128)S(1)} fusion(f32[32,2,16,4096]{3,0,2,1:T(8,128)} %all-gather.2.cloned.1.call-done, s32[]{:T(128)S(6)} %select_n.14), kind=kOutput, calls=%fused_computation.46 | convolution fusion | flops 402653184 | bytes 4198404 | tf_op jit(solution)/shard_map/jabc,kabc->jk/dot_general | solution.py:52
  272.8 66.2 %psum.7 = f32[32,32]{0,1:T(8,128)S(1)} all-reduce(f32[32,32]{0,1:T(8,128)S(1)} %fusion.17), channel_id=1, replica_groups=mesh['rows'=32,'vec'=4] {'rows','vec'}, use_global_device_ids=true, to_apply=%region_0.1 | all-reduce | flops 1024 | bytes 8192 | tf_op jit(solution)/shard_map/psum | solution.py:56
  339.1 2.9 cholesky.14
  343.3 2.4 custom-call.7
  346.0 10.7 %convolution_multiply_fusion = f32[8,2,16,4096]{3,0,2,1:T(8,128)S(1)} fusion(f32[32,2,16,4096]{3,0,2,1:T(8,128)} %all-gather.2.cloned.1.call-done, f32[32,32]{0,1:T(8,128)S(1)} %fusion.20, s32[]{:T(128)S(6)} %select_n.16), kind=kOutput, calls=%fused_computation.37 | convolution fusion | flops 403701760 | bytes 20975620 | tf_op jit(solution)/shard_map/jk,jabc->kabc/dot_general | solution.py:77
  356.7 4.4 %copy.29 = f32[8,2,16,4096]{3,2,1,0:T(8,128)} copy(f32[8,2,16,4096]{3,0,2,1:T(8,128)S(1)} %convolution_multiply_fusion) | data formatting | bytes 8388608
  (50 shorter events, 23.0 us)
Async XLA Ops:
  7.2 2.8 copy-start.1
  7.2 2.8 copy-start.2
  7.2 258.7 %all-gather.2.cloned.1.call-start = ((), (), s32[]{:S(2)}) async-start(), calls=%async_computation | async-start | bytes 20971520 | tf_op jit(solution)/shard_map/all_gather | solution.py:71
  17.0 12.8 %collective-permute-start.1 = (f32[9,2,1,4096]{3,0,2,1:T(8,128)}, f32[9,2,1,4096]{3,0,2,1:T(8,128)S(1)}, u32[]{:S(2)}, u32[]{:S(2)}) collective-permute-start(f32[9,2,1,4096]{3,0,2,1:T(8,128)} %get-tuple-element.40), channel_id=1, source_target_pairs={{4,0},{8,4},{12,8},{16,12},{20,16},{24,20},{28,24},{32,28},{36,32}... | collective-permute-start | bytes 884744 | tf_op jit(solution)/shard_map/ppermute | solution.py:24
  22.7 12.5 %collective-permute-start = (f32[9,2,1,4096]{3,0,2,1:T(8,128)}, f32[9,2,1,4096]{3,0,2,1:T(8,128)}, u32[]{:S(2)}, u32[]{:S(2)}) collective-permute-start(f32[9,2,1,4096]{3,0,2,1:T(8,128)} %get-tuple-element.39), channel_id=1, source_target_pairs={{0,4},{4,8},{8,12},{12,16},{16,20},{20,24},{24,28},{28,32},{32,36}... | collective-permute-start | bytes 884744 | tf_op jit(solution)/shard_map/ppermute | solution.py:21
  53.6 7.0 %collective-permute-start.3 = (f32[9,2,1,4096]{3,0,2,1:T(8,128)}, f32[9,2,1,4096]{3,0,2,1:T(8,128)S(1)}, u32[]{:S(2)}, u32[]{:S(2)}) collective-permute-start(f32[9,2,1,4096]{3,0,2,1:T(8,128)} %get-tuple-element.30), channel_id=1, source_target_pairs={{4,0},{8,4},{12,8},{16,12},{20,16},{24,20},{28,24},{32,28},{36,32}... | collective-permute-start | bytes 884744 | tf_op jit(solution)/shard_map/ppermute | solution.py:24
  53.6 12.7 %collective-permute-start.2 = (f32[9,2,1,4096]{3,0,2,1:T(8,128)}, f32[9,2,1,4096]{3,0,2,1:T(8,128)}, u32[]{:S(2)}, u32[]{:S(2)}) collective-permute-start(f32[9,2,1,4096]{3,0,2,1:T(8,128)} %get-tuple-element.29), channel_id=1, source_target_pairs={{0,4},{4,8},{8,12},{12,16},{16,20},{20,24},{24,28},{28,32},{32,36}... | collective-permute-start | bytes 884744 | tf_op jit(solution)/shard_map/ppermute | solution.py:21
  84.7 7.0 %collective-permute-start.5 = (f32[9,2,1,4096]{3,0,2,1:T(8,128)}, f32[9,2,1,4096]{3,0,2,1:T(8,128)S(1)}, u32[]{:S(2)}, u32[]{:S(2)}) collective-permute-start(f32[9,2,1,4096]{3,0,2,1:T(8,128)} %get-tuple-element.20), channel_id=1, source_target_pairs={{4,0},{8,4},{12,8},{16,12},{20,16},{24,20},{28,24},{32,28},{36,32}... | collective-permute-start | bytes 884744 | tf_op jit(solution)/shard_map/ppermute | solution.py:24
  84.7 12.3 %collective-permute-start.4 = (f32[9,2,1,4096]{3,0,2,1:T(8,128)}, f32[9,2,1,4096]{3,0,2,1:T(8,128)S(1)}, u32[]{:S(2)}, u32[]{:S(2)}) collective-permute-start(f32[9,2,1,4096]{3,0,2,1:T(8,128)} %get-tuple-element.19), channel_id=1, source_target_pairs={{0,4},{4,8},{8,12},{12,16},{16,20},{20,24},{24,28},{28,32},{32,36}... | collective-permute-start | bytes 884744 | tf_op jit(solution)/shard_map/ppermute | solution.py:21
  109.3 3.3 copy-start
Sparse Core Ops, SparseCore 0:
  115.3 150.4 all-gather.1
where the time goes:
time: 375 us; the launch traced here: 369 us
  waiting for transfers between devices  167 us (45%)
  blocking collectives  66.2 us (18%)
  other arithmetic  56.9 us (15%)
  local copies, waits for them, and re-layouts  39.4 us (11%)
  matrix products  17.8 us (5%)
  between operations  14.6 us (4%)
  starting transfers between devices  7.74 us (2%)
    all_gather x1, waiting for transfers between devices, per_device(): gathered = lax.all_gather(advanced, 'vec', axis=0, tiled=True)  147 us
    psum x1, blocking collectives, combine_factor(): return jnp.linalg.cholesky(lax.psum(partial_gram, ('rows', 'vec')))  66.2 us
    add x3, other arithmetic, mix_rows(): return (1.0 - COUPLING) * middle + COUPLING / 4.0 * beside  37.1 us
    ppermute x3, waiting for transfers between devices, with_halo(): lax.ppermute(lax.slice_in_dim(block, block.shape[dim] - width, None, axis...  16.5 us
    slice x6, local copies, waits for them, and re-layouts, mix_rows(): jnp.roll(middle, -1, -1)  15.8 us
    dot_general x1, matrix products, per_device(): jnp.einsum('jk,jabc->kabc', own_columns, gathered, precision=lax.Precisio...  10.7 us
    unnamed x12, local copies, waits for them, and re-layouts  9.43 us
  transfers between devices with their start and end apart: 7, of which 7 were waited for; matrix products, arithmetic and copies ran while one was open for 5% of the time, Pallas kernels for 0%

commit v1 on v0

v1 whole, which is shorter than its diff:
```python
import math

import jax
import jax.numpy as jnp
from jax import lax
from jax.experimental import pallas as pl
from jax.experimental.pallas import tpu as pltpu
from jax.sharding import PartitionSpec as P

NV = 32
STEPS = 3
COUPLING = 0.35
HALO = 4
VMEM = 56 * 1024 * 1024
HIGHEST = lax.Precision.HIGHEST
FULL = pl.BlockSpec(memory_space=pltpu.VMEM)
SMEM = pl.BlockSpec(memory_space=pltpu.SMEM)


def params():
    return pltpu.CompilerParams(vmem_limit_bytes=VMEM)


def neighbours(block):
    count = lax.axis_size("rows")
    forward = [(i, (i + 1) % count) for i in range(count)]
    backward = [(target, source) for source, target in forward]
    last = lax.slice_in_dim(block, block.shape[2] - HALO, None, axis=2)
    first = lax.slice_in_dim(block, 0, HALO, axis=2)
    above = lax.ppermute(last, "rows", forward)
    below = lax.ppermute(first, "rows", backward)
    return below, above


def mix(field):
    rows, columns = field.shape
    beside = (
        pltpu.roll(field, 1, 0)
        + pltpu.roll(field, rows - 1, 0)
        + pltpu.roll(field, 1, 1)
        + pltpu.roll(field, columns - 1, 1)
    )
    return (1.0 - COUPLING) * field + (COUPLING / 4.0) * beside


def ring(block, below, above):
    return jnp.concatenate([block, below, above], axis=0)


def lattice_kernel(z_ref, c_ref, below_ref, above_ref, twice_ref, next_ref):
    real, imag = (ring(z_ref[i], below_ref[0, i], above_ref[0, i]) for i in range(2))
    const_real, const_imag = (ring(c_ref[i], below_ref[1, i], above_ref[1, i]) for i in range(2))
    for step in range(STEPS):
        twice_ref[step, 0] = 2.0 * real
        twice_ref[step, 1] = 2.0 * imag
        map_real = real * real - imag * imag + const_real
        map_imag = 2.0 * real * imag + const_imag
        real, imag = mix(map_real), mix(map_imag)
    rows = z_ref.shape[1]
    next_ref[0] = real[:rows]
    next_ref[1] = imag[:rows]


def tangent_kernel(me_ref, u_ref, below_ref, above_ref, twice_ref, *rest):
    outs, slabs = rest[:-1], rest[-1]
    real, imag = (ring(u_ref[0, i], below_ref[0, i], above_ref[0, i]) for i in range(2))
    for step in range(STEPS):
        z_real, z_imag = twice_ref[step, 0], twice_ref[step, 1]
        push_real = z_real * real - z_imag * imag
        push_imag = z_real * imag + z_imag * real
        real, imag = mix(push_real), mix(push_imag)
    slabs[0] = real[:8]
    slabs[1] = real[8:16]
    slabs[2] = imag[:8]
    slabs[3] = imag[8:16]
    for shift, out in enumerate(outs):
        out[0] = slabs[lax.rem(me_ref[0] + shift, 4)]


def push(me, vectors, halo, twice, start, count):
    columns = vectors.shape[-1]
    return pl.pallas_call(
        tangent_kernel,
        grid=(count,),
        in_specs=[
            SMEM,
            pl.BlockSpec((1, 2, 16, columns), lambda i: (start + i, 0, 0, 0)),
            pl.BlockSpec((1, 2, HALO, columns), lambda i: (i, 0, 0, 0)),
            pl.BlockSpec((1, 2, HALO, columns), lambda i: (i, 0, 0, 0)),
            FULL,
        ],
        out_specs=[pl.BlockSpec((1, 8, columns), lambda i: (i, 0, 0))] * 4,
        out_shape=[jax.ShapeDtypeStruct((count, 8, columns), jnp.float32)] * 4,
        scratch_shapes=[pltpu.VMEM((4, 8, columns), jnp.float32)],
        compiler_params=params(),
        cost_estimate=pl.CostEstimate(
            flops=count * 2_000_000, bytes_accessed=count * 2_000_000, transcendentals=0
        ),
    )(me, vectors, *halo, twice)


def same_row(shape, period):
    return lax.rem(lax.broadcasted_iota(jnp.int32, shape, 0), period) == lax.rem(
        lax.broadcasted_iota(jnp.int32, shape, 1), period
    )


def owner(shape, group):
    row = lax.broadcasted_iota(jnp.int32, shape, 0)
    column = lax.broadcasted_iota(jnp.int32, shape, 1)
    return jnp.where(row == lax.div(column, group), 1.0, 0.0)


def gram_kernel(chunks, me_ref, *refs):
    pieces = refs[: 4 * chunks]
    high_ref, low_ref, gram_ref = refs[4 * chunks :]
    for chunk in range(chunks):
        for shift in range(4):
            piece = pieces[4 * chunk + shift]
            count, rows, columns = piece.shape
            source = lax.rem(me_ref[0] + 4 - shift, 4)
            start = pl.multiple_of(source * 64 + chunk * count * rows, count * rows)
            value = piece[...].reshape(count * rows, columns)
            high = value.astype(jnp.bfloat16)
            low = (value - high.astype(jnp.float32)).astype(jnp.bfloat16)
            high_ref[pl.ds(start, count * rows), :] = high
            low_ref[pl.ds(start, count * rows), :] = low
    high = high_ref[...]
    low = low_ref[...]
    last = (((1,), (1,)), ((), ()))
    main = lax.dot_general(high, high, last, preferred_element_type=jnp.float32)
    rest = lax.dot_general(high, low, last, preferred_element_type=jnp.float32)
    full = main + (rest + rest.T)
    full = jnp.where(same_row(full.shape, 8), full, 0.0)
    left = full.reshape(NV, 8, 8 * NV).sum(1)
    gram_ref[...] = lax.dot_general(
        left, owner((NV, 8 * NV), 8), last, precision=HIGHEST, preferred_element_type=jnp.float32
    )


def inner_products(me, pieces, chunks):
    columns = pieces[0].shape[-1]
    return pl.pallas_call(
        lambda *refs: gram_kernel(chunks, *refs),
        in_specs=[SMEM] + [FULL] * len(pieces),
        out_specs=[FULL] * 3,
        out_shape=[
            jax.ShapeDtypeStruct((8 * NV, columns), jnp.bfloat16),
            jax.ShapeDtypeStruct((8 * NV, columns), jnp.bfloat16),
            jax.ShapeDtypeStruct((NV, NV), jnp.float32),
        ],
        compiler_params=params(),
    )(me, *pieces)


def basis_kernel(scale, me_ref, gram_ref, high_ref, low_ref, growth_ref, *rest):
    outs, w_high, w_low = rest[:-2], rest[-2], rest[-1]
    row = lax.broadcasted_iota(jnp.int32, (NV, 2 * NV), 0)
    column = lax.broadcasted_iota(jnp.int32, (NV, 2 * NV), 1)
    identity = jnp.where(column == row + NV, 1.0, 0.0)
    spread = jnp.where(
        lax.broadcasted_iota(jnp.int32, (NV, 2 * NV), 0)
        == lax.broadcasted_iota(jnp.int32, (NV, 2 * NV), 1),
        1.0,
        0.0,
    )
    last = (((1,), (0,)), ((), ()))
    work = identity + lax.dot_general(
        gram_ref[...], spread, last, precision=HIGHEST, preferred_element_type=jnp.float32
    )
    for k in range(NV):
        pivot_row = work[k : k + 1, :]
        pivot = pivot_row[:, k : k + 1]
        inverse = lax.rsqrt(pivot)
        inverse = inverse * (1.5 - 0.5 * pivot * inverse * inverse)
        scaled = pivot_row * inverse
        factor = work[:, k : k + 1] * inverse
        work = jnp.where(row > k, work - factor * scaled, jnp.where(row == k, scaled, work))
    diagonal = jnp.sum(jnp.where(column == row, work, 0.0), axis=0, keepdims=True)
    growth_ref[...] = jnp.log(diagonal[:, :NV] / scale)
    inverse = work[:, NV:] * scale
    group = owner((NV, 8 * NV), 8)
    wide = lax.dot_general(
        inverse, group, last, precision=HIGHEST, preferred_element_type=jnp.float32
    )
    tall = jnp.broadcast_to(wide[:, None, :], (NV, 8, 8 * NV)).reshape(8 * NV, 8 * NV)
    weights = jnp.where(same_row(tall.shape, 8), tall, 0.0)
    high = weights.astype(jnp.bfloat16)
    w_high[...] = high
    w_low[...] = (weights - high.astype(jnp.float32)).astype(jnp.bfloat16)
    for shift, out in enumerate(outs):
        start = pl.multiple_of(lax.rem(me_ref[0] + shift, 4) * 64, 64)
        own_high = w_high[pl.ds(start, 64), :]
        own_low = w_low[pl.ds(start, 64), :]
        value = jnp.dot(own_high, high_ref[...], preferred_element_type=jnp.float32)
        value += jnp.dot(own_high, low_ref[...], preferred_element_type=jnp.float32)
        value += jnp.dot(own_low, high_ref[...], preferred_element_type=jnp.float32)
        out[...] = value.reshape(out.shape)


def orthonormal(me, gram, high, low, scale):
    columns = high.shape[-1]
    return pl.pallas_call(
        lambda *refs: basis_kernel(scale, *refs),
        in_specs=[SMEM] + [FULL] * 3,
        out_specs=[FULL] * 5,
        out_shape=[jax.ShapeDtypeStruct((1, NV), jnp.float32)]
        + [jax.ShapeDtypeStruct((8, 8, columns), jnp.float32)] * 4,
        scratch_shapes=[pltpu.VMEM((8 * NV, 8 * NV), jnp.bfloat16)] * 2,
        compiler_params=params(),
    )(me, gram, high, low)


def assemble_kernel(me_ref, *refs):
    pieces, out = refs[:-1], refs[-1]
    for shift, piece in enumerate(pieces):
        slab = lax.rem(me_ref[0] + 4 - shift, 4)
        out[:, slab] = piece[...]


def assemble(me, pieces):
    count, rows, columns = pieces[0].shape
    step = 2
    return pl.pallas_call(
        assemble_kernel,
        grid=(count // step,),
        in_specs=[SMEM] + [pl.BlockSpec((step, rows, columns), lambda i: (i, 0, 0))] * 4,
        out_specs=pl.BlockSpec((step, 4, rows, columns), lambda i: (i, 0, 0, 0)),
        out_shape=jax.ShapeDtypeStruct((count, 4, rows, columns), jnp.float32),
        compiler_params=params(),
    )(me, *pieces)


def shifted(block, shift):
    return lax.ppermute(block, "vec", [(i, (i + shift) % 4) for i in range(4)])


def exchange(blocks):
    moved = {shift: shifted(blocks[shift], shift) for shift in (2, 1, 3)}
    return [blocks[0], moved[1], moved[2], moved[3]]


def group_sum(value, axis, stride, members):
    size = lax.axis_size(axis)
    terms = [value] + [
        lax.ppermute(value, axis, [(i, i ^ (k * stride)) for i in range(size)])
        for k in range(1, members)
    ]
    while len(terms) > 1:
        terms = [terms[i] + terms[i + 1] for i in range(0, len(terms), 2)]
    return terms[0]


def total_sum(value):
    value = group_sum(value, "vec", 1, 4)
    value = group_sum(value, "rows", 1, 2)
    value = group_sum(value, "rows", 2, 4)
    return group_sum(value, "rows", 8, 4)


CHUNKS = (4, 4)


def per_device(lattice_state, constant_field, tangents):
    me = lax.axis_index("vec").astype(jnp.int32).reshape(1)
    rows, columns = lattice_state.shape[1:]
    scale = math.sqrt(2.0 * rows * lax.axis_size("rows") * columns)
    fields = jnp.stack([lattice_state, constant_field])
    below, above = neighbours(fields)
    halos, start = [], 0
    for count in CHUNKS:
        halos.append(neighbours(lax.slice_in_dim(tangents, start, start + count, axis=0)))
        start += count
    twice, next_state = pl.pallas_call(
        lattice_kernel,
        in_specs=[FULL] * 4,
        out_specs=[FULL] * 2,
        out_shape=[
            jax.ShapeDtypeStruct((STEPS, 2, rows + 2 * HALO, columns), jnp.float32),
            jax.ShapeDtypeStruct((2, rows, columns), jnp.float32),
        ],
        compiler_params=params(),
    )(lattice_state, constant_field, below, above)
    pieces, start = [], 0
    for count, halo in zip(CHUNKS, halos):
        pieces += exchange(push(me, tangents, halo, twice, start, count))
        start += count
    high, low, partial_gram = inner_products(me, pieces, len(CHUNKS))
    gram = total_sum(partial_gram)
    growth, *parts = orthonormal(me, gram, high, low, scale)
    basis = assemble(me, exchange(parts))
    return (next_state, basis.reshape(tangents.shape), growth.reshape(NV))


def solution(mesh):
    return jax.shard_map(
        per_device,
        mesh=mesh,
        in_specs=(P(None, "rows", None), P(None, "rows", None), P("vec", None, "rows", None)),
        out_specs=(P(None, "rows", None), P("vec", None, "rows", None), P()),
        check_vma=False,
    )
```

time: 375 us -> 177 us (0.47); the launches traced: 369 us -> 177 us
  waiting for transfers between devices: 167 us -> 86.9 us
  blocking collectives: 66.2 us -> 0 us
  other arithmetic: 56.9 us -> 2.23 us
  Pallas kernels: 0 us -> 42.6 us
  local copies, waits for them, and re-layouts: 39.4 us -> 6.41 us
  starting transfers between devices: 7.74 us -> 38.1 us
  matrix products: 17.8 us -> 0 us
  between operations: 14.6 us -> 0.74 us
    all_gather x1 -> x0, waiting for transfers between devices: 147 us -> none  [per_device(): gathered = lax.all_gather(advanced, 'vec', axis=0, tiled=True)]
    ppermute x6 -> x25, waiting for transfers between devices: 19.8 us -> 86.9 us  [the longest x9 72.4 us: shifted(): return lax.ppermute(block, 'vec', [(i, (i + shift) % 4) for i in range(4)])]
    psum x1 -> x0, blocking collectives: 66.2 us -> none  [combine_factor(): return jnp.linalg.cholesky(lax.psum(partial_gram, ('rows', 'vec')))]
    pallas_call x0 -> x6, Pallas kernels: none -> 42.6 us  [the longest x2 17.7 us: push(): pl.pallas_call(tangent_kernel, grid=(count,), in_specs=[SMEM, pl.BlockSpe...]
    add x6 -> x4, other arithmetic: 39.3 us -> 1.34 us  [group_sum(): terms = [terms[i] + terms[i + 1] for i in range(0, len(terms), 2)]]
    ppermute x6 -> x25, starting transfers between devices: 7.7 us -> 38.1 us  [the longest x9 13.9 us: shifted(): return lax.ppermute(block, 'vec', [(i, (i + shift) % 4) for i in range(4)])]
    slice x15 -> x1, local copies, waits for them, and re-layouts: 27.5 us -> 2.67 us  [neighbours(): last = lax.slice_in_dim(block, block.shape[2] - HALO, None, axis=2)]
    dot_general x2 -> x0, matrix products: 17.6 us -> none  [the longest x1 10.7 us: per_device(): jnp.einsum('jk,jabc->kabc', own_columns, gathered, precision=lax.Precisio...]
  transfers between devices with their start and end apart: 7 -> 25, of which waited for: 7 -> 14; matrix products, arithmetic and copies ran while one was open for 5% -> 1% of each run, Pallas kernels for 0% -> 12%
where the time goes in v1:
time: 177 us
  waiting for transfers between devices  86.9 us (49%)
  Pallas kernels  42.6 us (24%)
  starting transfers between devices  38.1 us (22%)
  local copies, waits for them, and re-layouts  6.41 us (4%)
  other arithmetic  2.23 us (1%)
    ppermute x9, waiting for transfers between devices, shifted(): return lax.ppermute(block, 'vec', [(i, (i + shift) % 4) for i in range(4)])  72.4 us
    pallas_call x2, Pallas kernels, push(): pl.pallas_call(tangent_kernel, grid=(count,), in_specs=[SMEM, pl.BlockSpe...  17.7 us
    ppermute x9, starting transfers between devices, shifted(): return lax.ppermute(block, 'vec', [(i, (i + shift) % 4) for i in range(4)])  13.9 us
    ppermute x10, starting transfers between devices, group_sum(): lax.ppermute(value, axis, [(i, i ^ k * stride) for i in range(size)])  12.4 us
    ppermute x3, starting transfers between devices, neighbours(): below = lax.ppermute(first, 'rows', backward)  11.7 us
    pallas_call x1, Pallas kernels, orthonormal(): pl.pallas_call(lambda *refs: basis_kernel(scale, *refs), in_specs=[SMEM]...  10.9 us
    ppermute x10, waiting for transfers between devices, group_sum(): lax.ppermute(value, axis, [(i, i ^ k * stride) for i in range(size)])  10.2 us
    pallas_call x1, Pallas kernels, inner_products(): pl.pallas_call(lambda *refs: gram_kernel(chunks, *refs), in_specs=[SMEM]...  5.35 us
  transfers between devices with their start and end apart: 25, of which 14 were waited for; matrix products, arithmetic and copies ran while one was open for 1% of the time, Pallas kernels for 12%

profile of v1, /device:TPU:0, one launch (start us, length us, event | category | flops | bytes accessed | tf_op | source)
XLA Modules:
  0.0 177.0 jit_solution(6135844581864712736)
XLA Ops:
  0.7 2.7 %fusion = (f32[4,2,4,4096]{3,2,1,0:T(4,128)S(1)}, f32[4,2,4,4096]{3,2,1,0:T(4,128)S(1)}, f32[4,2,4,4096]{3,2,1,0:T(4,128)S(1)}, f32[4,2,4,4096]{3,2,1,0:T(4,128)S(1)}) fusion(f32[8,2,16,4096]{3,2,1,0:T(8,128)} %u_ref.3), kind=kLoop, calls=%fused_computation.5 | loop fusion | bytes 4194304 | tf_op jit(solution)/shard_map/slice | solution.py:28
  3.4 5.8 %collective-permute-start.7 = (f32[4,2,4,4096]{3,2,1,0:T(4,128)S(1)}, f32[4,2,4,4096]{3,2,1,0:T(4,128)}, u32[]{:S(2)}, u32[]{:S(2)}) collective-permute-start(f32[4,2,4,4096]{3,2,1,0:T(4,128)S(1)} %get-tuple-element.40), channel_id=1, source_target_pairs={{4,0},{8,4},{12,8},{16,12},{20,16},{24,20},{28,24},{32,28},{36,32}... | collective-permute-start | bytes 1572872 | tf_op jit(solution)/shard_map/ppermute | solution.py:31
  10.1 5.1 %collective-permute-start = (f32[2,2,4,4096]{3,2,1,0:T(4,128)}, f32[2,2,4,4096]{3,2,1,0:T(4,128)}, u32[]{:S(2)}, u32[]{:S(2)}) collective-permute-start(f32[2,2,4,4096]{3,2,1,0:T(4,128)} %get-tuple-element.44), channel_id=1, source_target_pairs={{4,0},{8,4},{12,8},{16,12},{20,16},{24,20},{28,24},{32,28},{36,32}... | collective-permute-start | bytes 786440 | tf_op jit(solution)/shard_map/ppermute | solution.py:31
  15.2 4.3 %collective-permute-done.1.above_ref = f32[2,2,4,4096]{3,2,1,0:T(4,128)S(1)} collective-permute-done((f32[2,2,4,4096]{3,2,1,0:T(4,128)}, f32[2,2,4,4096]{3,2,1,0:T(4,128)S(1)}, u32[]{:S(2)}, u32[]{:S(2)}) %collective-permute-start.1) | collective-permute-done | bytes 262176 | tf_op jit(solution)/shard_map/ppermute | solution.py:30
  20.3 4.0 %shard_map.58 = (f32[3,2,24,4096]{3,2,1,0:T(8,128)}, f32[2,16,4096]{2,1,0:T(8,128)}) custom-call(f32[2,16,4096]{2,1,0:T(8,128)} %z_ref.1, f32[2,16,4096]{2,1,0:T(8,128)} %c_ref.1, f32[2,2,4,4096]{3,2,1,0:T(4,128)} %collective-permute-done.below_ref, f32[2,2,4,4096]{3,2,1,0:T(4,128)} %copy-done.13), custom_call_target="tpu_custom_call" | custom-call | tf_op jit(solution)/shard_map/pallas_call | solution.py:274
  24.3 8.9 %shard_map.60 = (f32[4,8,4096]{2,1,0:T(8,128)}, f32[4,8,4096]{2,1,0:T(8,128)}, f32[4,8,4096]{2,1,0:T(8,128)}, f32[4,8,4096]{2,1,0:T(8,128)}) custom-call(s32[1]{0:T(128)} %bitcast.2.me_ref.refs_0_, f32[8,2,16,4096]{3,2,1,0:T(8,128)} %u_ref.3, f32[4,2,4,4096]{3,2,1,0:T(4,128)} %collective-permute-done.7.below_ref, ...), custom_call_target="tpu_custom_call" | custom-call | flops 8000000 | bytes 8000000 | tf_op jit(solution)/shard_map/pallas_call | solution.py:82
  33.2 1.6 collective-permute-start.9
  34.7 2.9 %collective-permute-start.10 = (f32[4,8,4096]{2,1,0:T(8,128)}, f32[4,8,4096]{2,1,0:T(8,128)S(1)}, u32[]{:S(2)}, u32[]{:S(2)}) collective-permute-start(f32[4,8,4096]{2,1,0:T(8,128)} %get-tuple-element.29), channel_id=1, source_target_pairs={{0,2},{1,3},{2,0},{3,1},{4,6},{5,7},{6,4},{7,5},{8,10},{9,11},{10,... | collective-permute-start | bytes 1572872 | tf_op jit(solution)/shard_map/ppermute | solution.py:235
  40.6 8.8 %shard_map.59 = (f32[4,8,4096]{2,1,0:T(8,128)}, f32[4,8,4096]{2,1,0:T(8,128)}, f32[4,8,4096]{2,1,0:T(8,128)}, f32[4,8,4096]{2,1,0:T(8,128)}) custom-call(s32[1]{0:T(128)} %bitcast.2.me_ref.refs_0_, f32[8,2,16,4096]{3,2,1,0:T(8,128)} %u_ref.3, f32[4,2,4,4096]{3,2,1,0:T(4,128)} %copy-done.12, f32[4,2,4,4096]{3,2,1,0:T(4,128)} %copy-done.11, ...), custom_call_target="tpu_custom_call" | custom-call | flops 8000000 | bytes 8000000 | tf_op jit(solution)/shard_map/pallas_call | solution.py:82
  50.9 2.0 %collective-permute-start.6 = (f32[4,8,4096]{2,1,0:T(8,128)}, f32[4,8,4096]{2,1,0:T(8,128)S(1)}, u32[]{:S(2)}, u32[]{:S(2)}) collective-permute-start(f32[4,8,4096]{2,1,0:T(8,128)} %get-tuple-element.26), channel_id=1, source_target_pairs={{0,3},{1,0},{2,1},{3,2},{4,7},{5,4},{6,5},{7,6},{8,11},{9,8},{10,9... | collective-permute-start | bytes 1572872 | tf_op jit(solution)/shard_map/ppermute | solution.py:235
  52.9 9.0 %collective-permute-done.10.refs_7_ = f32[4,8,4096]{2,1,0:T(8,128)S(1)} collective-permute-done((f32[4,8,4096]{2,1,0:T(8,128)}, f32[4,8,4096]{2,1,0:T(8,128)S(1)}, u32[]{:S(2)}, u32[]{:S(2)}) %collective-permute-start.10) | collective-permute-done | bytes 524320 | tf_op jit(solution)/shard_map/ppermute | solution.py:235
  61.9 11.1 %collective-permute-done.4.refs_2_ = f32[4,8,4096]{2,1,0:T(8,128)S(1)} collective-permute-done((f32[4,8,4096]{2,1,0:T(8,128)}, f32[4,8,4096]{2,1,0:T(8,128)S(1)}, u32[]{:S(2)}, u32[]{:S(2)}) %collective-permute-start.4) | collective-permute-done | bytes 524320 | tf_op jit(solution)/shard_map/ppermute | solution.py:235
  73.1 10.0 %collective-permute-done.5.refs_3_ = f32[4,8,4096]{2,1,0:T(8,128)S(1)} collective-permute-done((f32[4,8,4096]{2,1,0:T(8,128)}, f32[4,8,4096]{2,1,0:T(8,128)S(1)}, u32[]{:S(2)}, u32[]{:S(2)}) %collective-permute-start.5) | collective-permute-done | bytes 524320 | tf_op jit(solution)/shard_map/ppermute | solution.py:235
  84.1 5.4 %shard_map.61 = (bf16[256,4096]{1,0:T(8,128)(2,1)}, bf16[256,4096]{1,0:T(8,128)(2,1)}, f32[32,32]{1,0:T(8,128)}) custom-call(s32[1]{0:T(128)} %bitcast.2.me_ref.refs_0_, f32[4,8,4096]{2,1,0:T(8,128)} %get-tuple-element.23.refs_1_, f32[4,8,4096]{2,1,0:T(8,128)} %copy-done.8, f32[4,8,4096]{2,1,0:T(8,128)} %copy-done.9, f32[4,8,4096]{2,1,0:T(8,128)} %copy-done.10, ...), custom_call_target="tpu_custom_call" | custom-call | tf_op jit(solution)/shard_map/pallas_call | solution.py:143
  89.5 1.9 %collective-permute-start.14 = (f32[32,32]{1,0:T(8,128)}, f32[32,32]{1,0:T(8,128)S(1)}, u32[]{:S(2)}, u32[]{:S(2)}) collective-permute-start(f32[32,32]{1,0:T(8,128)} %get-tuple-element.31), channel_id=1, source_target_pairs={{0,3},{1,2},{2,1},{3,0},{4,7},{5,6},{6,5},{7,4},{8,11},{9,10},{10,... | collective-permute-start | bytes 12296 | tf_op jit(solution)/shard_map/ppermute | solution.py:246
  94.6 2.2 %collective-permute-done.13 = f32[32,32]{1,0:T(8,128)S(1)} collective-permute-done((f32[32,32]{1,0:T(8,128)}, f32[32,32]{1,0:T(8,128)S(1)}, u32[]{:S(2)}, u32[]{:S(2)}) %collective-permute-start.13) | collective-permute-done | bytes 4128 | tf_op jit(solution)/shard_map/ppermute | solution.py:246
  99.0 3.8 %collective-permute-start.16 = (f32[32,32]{1,0:T(8,128)S(1)}, f32[32,32]{1,0:T(8,128)S(1)}, u32[]{:S(2)}, u32[]{:S(2)}) collective-permute-start(f32[32,32]{1,0:T(8,128)S(1)} %add.33), channel_id=1, source_target_pairs={{0,8},{4,12},{8,0},{12,4},{16,24},{20,28},{24,16},{28,20},{32,40},... | collective-permute-start | bytes 12296 | tf_op jit(solution)/shard_map/ppermute | solution.py:246
  104.7 2.8 %collective-permute-start.21 = (f32[32,32]{1,0:T(8,128)S(1)}, f32[32,32]{1,0:T(8,128)S(1)}, u32[]{:S(2)}, u32[]{:S(2)}) collective-permute-start(f32[32,32]{1,0:T(8,128)S(1)} %add_add_fusion.1), channel_id=1, source_target_pairs={{0,96},{4,100},{8,104},{12,108},{16,112},{20,116},{24,120},{28,124... | collective-permute-start | bytes 12296 | tf_op jit(solution)/shard_map/ppermute | solution.py:246
  109.8 3.0 %collective-permute-done.20 = f32[32,32]{1,0:T(8,128)S(1)} collective-permute-done((f32[32,32]{1,0:T(8,128)S(1)}, f32[32,32]{1,0:T(8,128)S(1)}, u32[]{:S(2)}, u32[]{:S(2)}) %collective-permute-start.20) | collective-permute-done | bytes 4128 | tf_op jit(solution)/shard_map/ppermute | solution.py:246
  113.4 10.9 %shard_map.62 = (f32[1,32]{1,0:T(1,128)}, f32[8,8,4096]{2,1,0:T(8,128)}, f32[8,8,4096]{2,1,0:T(8,128)}, f32[8,8,4096]{2,1,0:T(8,128)}, f32[8,8,4096]{2,1,0:T(8,128)}) custom-call(s32[1]{0:T(128)} %bitcast.2.me_ref.refs_0_, f32[32,32]{1,0:T(8,128)} %add_add_fusion.refs_1_, bf16[256,4096]{1,0:T(8,128)(2,1)} %get-tuple-element.32.refs_2_, ...), custom_call_target="tpu_custom_call" | custom-call | tf_op jit(solution)/shard_map/pallas_call | solution.py:203
  124.3 2.5 %collective-permute-start.23 = (f32[8,8,4096]{2,1,0:T(8,128)}, f32[8,8,4096]{2,1,0:T(8,128)S(1)}, u32[]{:S(2)}, u32[]{:S(2)}) collective-permute-start(f32[8,8,4096]{2,1,0:T(8,128)} %get-tuple-element.36), channel_id=1, source_target_pairs={{0,2},{1,3},{2,0},{3,1},{4,6},{5,7},{6,4},{7,5},{8,10},{9,11},{10,... | collective-permute-start | bytes 3145736 | tf_op jit(solution)/shard_map/ppermute | solution.py:235
  126.8 2.1 %collective-permute-start.24 = (f32[8,8,4096]{2,1,0:T(8,128)}, f32[8,8,4096]{2,1,0:T(8,128)S(1)}, u32[]{:S(2)}, u32[]{:S(2)}) collective-permute-start(f32[8,8,4096]{2,1,0:T(8,128)} %get-tuple-element.37), channel_id=1, source_target_pairs={{0,3},{1,0},{2,1},{3,2},{4,7},{5,4},{6,5},{7,6},{8,11},{9,8},{10,9... | collective-permute-start | bytes 3145736 | tf_op jit(solution)/shard_map/ppermute | solution.py:235
  128.9 41.6 %collective-permute-done.22.refs_1_ = f32[8,8,4096]{2,1,0:T(8,128)S(1)} collective-permute-done((f32[8,8,4096]{2,1,0:T(8,128)}, f32[8,8,4096]{2,1,0:T(8,128)S(1)}, u32[]{:S(2)}, u32[]{:S(2)}) %collective-permute-start.22) | collective-permute-done | bytes 1048608 | tf_op jit(solution)/shard_map/ppermute | solution.py:235
  172.3 4.7 %shard_map.63 = f32[8,4,8,4096]{3,2,1,0:T(8,128)} custom-call(s32[1]{0:T(128)} %bitcast.2.me_ref.refs_0_, f32[8,8,4096]{2,1,0:T(8,128)} %get-tuple-element.34.refs_0_, f32[8,8,4096]{2,1,0:T(8,128)} %copy-done.2, f32[8,8,4096]{2,1,0:T(8,128)} %copy-done.3, f32[8,8,4096]{2,1,0:T(8,128)} %copy-done.4), custom_call_target="tpu_custom_call" | custom-call | tf_op jit(solution)/shard_map/pallas_call | solution.py:224
  (66 shorter events, 19.2 us)
Async XLA Ops:
  3.3 20.9 %collective-permute-start.8 = (f32[4,2,4,4096]{3,2,1,0:T(4,128)S(1)}, f32[4,2,4,4096]{3,2,1,0:T(4,128)}, u32[]{:S(2)}, u32[]{:S(2)}) collective-permute-start(f32[4,2,4,4096]{3,2,1,0:T(4,128)S(1)} %get-tuple-element.39), channel_id=1, source_target_pairs={{0,4},{4,8},{8,12},{12,16},{16,20},{20,24},{24,28},{28,32},{32,36}... | collective-permute-start | bytes 1572872 | tf_op jit(solution)/shard_map/ppermute | solution.py:30
  3.4 20.8 %collective-permute-start.7 = (f32[4,2,4,4096]{3,2,1,0:T(4,128)S(1)}, f32[4,2,4,4096]{3,2,1,0:T(4,128)}, u32[]{:S(2)}, u32[]{:S(2)}) collective-permute-start(f32[4,2,4,4096]{3,2,1,0:T(4,128)S(1)} %get-tuple-element.40), channel_id=1, source_target_pairs={{4,0},{8,4},{12,8},{16,12},{20,16},{24,20},{28,24},{32,28},{36,32}... | collective-permute-start | bytes 1572872 | tf_op jit(solution)/shard_map/ppermute | solution.py:31
  10.1 9.3 %collective-permute-start.1 = (f32[2,2,4,4096]{3,2,1,0:T(4,128)}, f32[2,2,4,4096]{3,2,1,0:T(4,128)S(1)}, u32[]{:S(2)}, u32[]{:S(2)}) collective-permute-start(f32[2,2,4,4096]{3,2,1,0:T(4,128)} %get-tuple-element.43), channel_id=1, source_target_pairs={{0,4},{4,8},{8,12},{12,16},{16,20},{20,24},{24,28},{28,32},{32,36}... | collective-permute-start | bytes 786440 | tf_op jit(solution)/shard_map/ppermute | solution.py:30
  10.1 10.1 %collective-permute-start = (f32[2,2,4,4096]{3,2,1,0:T(4,128)}, f32[2,2,4,4096]{3,2,1,0:T(4,128)}, u32[]{:S(2)}, u32[]{:S(2)}) collective-permute-start(f32[2,2,4,4096]{3,2,1,0:T(4,128)} %get-tuple-element.44), channel_id=1, source_target_pairs={{4,0},{8,4},{12,8},{16,12},{20,16},{24,20},{28,24},{32,28},{36,32}... | collective-permute-start | bytes 786440 | tf_op jit(solution)/shard_map/ppermute | solution.py:31
  15.2 23.8 %collective-permute-start.3 = (f32[4,2,4,4096]{3,2,1,0:T(4,128)S(1)}, f32[4,2,4,4096]{3,2,1,0:T(4,128)S(1)}, u32[]{:S(2)}, u32[]{:S(2)}) collective-permute-start(f32[4,2,4,4096]{3,2,1,0:T(4,128)S(1)} %get-tuple-element.41), channel_id=1, source_target_pairs={{0,4},{4,8},{8,12},{12,16},{16,20},{20,24},{24,28},{28,32},{32,36}... | collective-permute-start | bytes 1572872 | tf_op jit(solution)/shard_map/ppermute | solution.py:30
  19.5 19.5 %collective-permute-start.2 = (f32[4,2,4,4096]{3,2,1,0:T(4,128)S(1)}, f32[4,2,4,4096]{3,2,1,0:T(4,128)S(1)}, u32[]{:S(2)}, u32[]{:S(2)}) collective-permute-start(f32[4,2,4,4096]{3,2,1,0:T(4,128)S(1)} %get-tuple-element.42), channel_id=1, source_target_pairs={{4,0},{8,4},{12,8},{16,12},{20,16},{24,20},{28,24},{32,28},{36,32}... | collective-permute-start | bytes 1572872 | tf_op jit(solution)/shard_map/ppermute | solution.py:31
  33.2 17.8 %collective-permute-start.9 = (f32[4,8,4096]{2,1,0:T(8,128)}, f32[4,8,4096]{2,1,0:T(8,128)S(1)}, u32[]{:S(2)}, u32[]{:S(2)}) collective-permute-start(f32[4,8,4096]{2,1,0:T(8,128)} %get-tuple-element.28), channel_id=1, source_target_pairs={{0,1},{1,2},{2,3},{3,0},{4,5},{5,6},{6,7},{7,4},{8,9},{9,10},{10,1... | collective-permute-start | bytes 1572872 | tf_op jit(solution)/shard_map/ppermute | solution.py:235
  34.7 27.2 %collective-permute-start.10 = (f32[4,8,4096]{2,1,0:T(8,128)}, f32[4,8,4096]{2,1,0:T(8,128)S(1)}, u32[]{:S(2)}, u32[]{:S(2)}) collective-permute-start(f32[4,8,4096]{2,1,0:T(8,128)} %get-tuple-element.29), channel_id=1, source_target_pairs={{0,2},{1,3},{2,0},{3,1},{4,6},{5,7},{6,4},{7,5},{8,10},{9,11},{10,... | collective-permute-start | bytes 1572872 | tf_op jit(solution)/shard_map/ppermute | solution.py:235
  37.6 24.3 %collective-permute-start.11 = (f32[4,8,4096]{2,1,0:T(8,128)}, f32[4,8,4096]{2,1,0:T(8,128)S(1)}, u32[]{:S(2)}, u32[]{:S(2)}) collective-permute-start(f32[4,8,4096]{2,1,0:T(8,128)} %get-tuple-element.30), channel_id=1, source_target_pairs={{0,3},{1,0},{2,1},{3,2},{4,7},{5,4},{6,5},{7,6},{8,11},{9,8},{10,9... | collective-permute-start | bytes 1572872 | tf_op jit(solution)/shard_map/ppermute | solution.py:235
  49.4 23.6 %collective-permute-start.4 = (f32[4,8,4096]{2,1,0:T(8,128)}, f32[4,8,4096]{2,1,0:T(8,128)S(1)}, u32[]{:S(2)}, u32[]{:S(2)}) collective-permute-start(f32[4,8,4096]{2,1,0:T(8,128)} %get-tuple-element.24), channel_id=1, source_target_pairs={{0,1},{1,2},{2,3},{3,0},{4,5},{5,6},{6,7},{7,4},{8,9},{9,10},{10,1... | collective-permute-start | bytes 1572872 | tf_op jit(solution)/shard_map/ppermute | solution.py:235
  50.1 33.0 %collective-permute-start.5 = (f32[4,8,4096]{2,1,0:T(8,128)}, f32[4,8,4096]{2,1,0:T(8,128)S(1)}, u32[]{:S(2)}, u32[]{:S(2)}) collective-permute-start(f32[4,8,4096]{2,1,0:T(8,128)} %get-tuple-element.25), channel_id=1, source_target_pairs={{0,2},{1,3},{2,0},{3,1},{4,6},{5,7},{6,4},{7,5},{8,10},{9,11},{10,... | collective-permute-start | bytes 1572872 | tf_op jit(solution)/shard_map/ppermute | solution.py:235
  50.9 32.2 %collective-permute-start.6 = (f32[4,8,4096]{2,1,0:T(8,128)}, f32[4,8,4096]{2,1,0:T(8,128)S(1)}, u32[]{:S(2)}, u32[]{:S(2)}) collective-permute-start(f32[4,8,4096]{2,1,0:T(8,128)} %get-tuple-element.26), channel_id=1, source_target_pairs={{0,3},{1,0},{2,1},{3,2},{4,7},{5,4},{6,5},{7,6},{8,11},{9,8},{10,9... | collective-permute-start | bytes 1572872 | tf_op jit(solution)/shard_map/ppermute | solution.py:235
  89.5 5.2 %collective-permute-start.14 = (f32[32,32]{1,0:T(8,128)}, f32[32,32]{1,0:T(8,128)S(1)}, u32[]{:S(2)}, u32[]{:S(2)}) collective-permute-start(f32[32,32]{1,0:T(8,128)} %get-tuple-element.31), channel_id=1, source_target_pairs={{0,3},{1,2},{2,1},{3,0},{4,7},{5,6},{6,5},{7,4},{8,11},{9,10},{10,... | collective-permute-start | bytes 12296 | tf_op jit(solution)/shard_map/ppermute | solution.py:246
  91.4 5.5 %collective-permute-start.13 = (f32[32,32]{1,0:T(8,128)}, f32[32,32]{1,0:T(8,128)S(1)}, u32[]{:S(2)}, u32[]{:S(2)}) collective-permute-start(f32[32,32]{1,0:T(8,128)} %get-tuple-element.31), channel_id=1, source_target_pairs={{0,2},{1,3},{2,0},{3,1},{4,6},{5,7},{6,4},{7,5},{8,10},{9,11},{10,... | collective-permute-start | bytes 12296 | tf_op jit(solution)/shard_map/ppermute | solution.py:246
  92.5 4.3 %collective-permute-start.12 = (f32[32,32]{1,0:T(8,128)}, f32[32,32]{1,0:T(8,128)S(1)}, u32[]{:S(2)}, u32[]{:S(2)}) collective-permute-start(f32[32,32]{1,0:T(8,128)} %get-tuple-element.31), channel_id=1, source_target_pairs={{0,1},{1,0},{2,3},{3,2},{4,5},{5,4},{6,7},{7,6},{8,9},{9,8},{10,11... | collective-permute-start | bytes 12296 | tf_op jit(solution)/shard_map/ppermute | solution.py:246
  98.8 4.9 %collective-permute-start.18 = (f32[32,32]{1,0:T(8,128)S(1)}, f32[32,32]{1,0:T(8,128)S(1)}, u32[]{:S(2)}, u32[]{:S(2)}) collective-permute-start(f32[32,32]{1,0:T(8,128)S(1)} %add.33), channel_id=1, source_target_pairs={{0,24},{4,28},{8,16},{12,20},{16,8},{20,12},{24,0},{28,4},{32,56},... | collective-permute-start | bytes 12296 | tf_op jit(solution)/shard_map/ppermute | solution.py:246
  98.8 5.5 %collective-permute-start.17 = (f32[32,32]{1,0:T(8,128)S(1)}, f32[32,32]{1,0:T(8,128)S(1)}, u32[]{:S(2)}, u32[]{:S(2)}) collective-permute-start(f32[32,32]{1,0:T(8,128)S(1)} %add.33), channel_id=1, source_target_pairs={{0,16},{4,20},{8,24},{12,28},{16,0},{20,4},{24,8},{28,12},{32,48},... | collective-permute-start | bytes 12296 | tf_op jit(solution)/shard_map/ppermute | solution.py:246
  99.0 5.7 %collective-permute-start.16 = (f32[32,32]{1,0:T(8,128)S(1)}, f32[32,32]{1,0:T(8,128)S(1)}, u32[]{:S(2)}, u32[]{:S(2)}) collective-permute-start(f32[32,32]{1,0:T(8,128)S(1)} %add.33), channel_id=1, source_target_pairs={{0,8},{4,12},{8,0},{12,4},{16,24},{20,28},{24,16},{28,20},{32,40},... | collective-permute-start | bytes 12296 | tf_op jit(solution)/shard_map/ppermute | solution.py:246
  104.7 5.0 %collective-permute-start.21 = (f32[32,32]{1,0:T(8,128)S(1)}, f32[32,32]{1,0:T(8,128)S(1)}, u32[]{:S(2)}, u32[]{:S(2)}) collective-permute-start(f32[32,32]{1,0:T(8,128)S(1)} %add_add_fusion.1), channel_id=1, source_target_pairs={{0,96},{4,100},{8,104},{12,108},{16,112},{20,116},{24,120},{28,124... | collective-permute-start | bytes 12296 | tf_op jit(solution)/shard_map/ppermute | solution.py:246
  107.5 5.2 %collective-permute-start.20 = (f32[32,32]{1,0:T(8,128)S(1)}, f32[32,32]{1,0:T(8,128)S(1)}, u32[]{:S(2)}, u32[]{:S(2)}) collective-permute-start(f32[32,32]{1,0:T(8,128)S(1)} %add_add_fusion.1), channel_id=1, source_target_pairs={{0,64},{4,68},{8,72},{12,76},{16,80},{20,84},{24,88},{28,92},{32,9... | collective-permute-start | bytes 12296 | tf_op jit(solution)/shard_map/ppermute | solution.py:246
  107.5 5.2 %collective-permute-start.19 = (f32[32,32]{1,0:T(8,128)S(1)}, f32[32,32]{1,0:T(8,128)S(1)}, u32[]{:S(2)}, u32[]{:S(2)}) collective-permute-start(f32[32,32]{1,0:T(8,128)S(1)} %add_add_fusion.1), channel_id=1, source_target_pairs={{0,32},{4,36},{8,40},{12,44},{16,48},{20,52},{24,56},{28,60},{32,0... | collective-permute-start | bytes 12296 | tf_op jit(solution)/shard_map/ppermute | solution.py:246
  124.3 46.3 %collective-permute-start.22 = (f32[8,8,4096]{2,1,0:T(8,128)}, f32[8,8,4096]{2,1,0:T(8,128)S(1)}, u32[]{:S(2)}, u32[]{:S(2)}) collective-permute-start(f32[8,8,4096]{2,1,0:T(8,128)} %get-tuple-element.35), channel_id=1, source_target_pairs={{0,1},{1,2},{2,3},{3,0},{4,5},{5,6},{6,7},{7,4},{8,9},{9,10},{10,1... | collective-permute-start | bytes 3145736 | tf_op jit(solution)/shard_map/ppermute | solution.py:235
  124.3 46.3 %collective-permute-start.23 = (f32[8,8,4096]{2,1,0:T(8,128)}, f32[8,8,4096]{2,1,0:T(8,128)S(1)}, u32[]{:S(2)}, u32[]{:S(2)}) collective-permute-start(f32[8,8,4096]{2,1,0:T(8,128)} %get-tuple-element.36), channel_id=1, source_target_pairs={{0,2},{1,3},{2,0},{3,1},{4,6},{5,7},{6,4},{7,5},{8,10},{9,11},{10,... | collective-permute-start | bytes 3145736 | tf_op jit(solution)/shard_map/ppermute | solution.py:235
  126.8 44.4 %collective-permute-start.24 = (f32[8,8,4096]{2,1,0:T(8,128)}, f32[8,8,4096]{2,1,0:T(8,128)S(1)}, u32[]{:S(2)}, u32[]{:S(2)}) collective-permute-start(f32[8,8,4096]{2,1,0:T(8,128)} %get-tuple-element.37), channel_id=1, source_target_pairs={{0,3},{1,0},{2,1},{3,2},{4,7},{5,4},{6,5},{7,6},{8,11},{9,8},{10,9... | collective-permute-start | bytes 3145736 | tf_op jit(solution)/shard_map/ppermute | solution.py:235
  (15 other events, 110.7 us)

commit v2 on v1

v2 whole, which is shorter than its diff:
```python
import math

import jax
import jax.numpy as jnp
from jax import lax
from jax.experimental import pallas as pl
from jax.experimental.pallas import tpu as pltpu
from jax.sharding import PartitionSpec as P

NV = 32
STEPS = 3
COUPLING = 0.35
HALO = 4
VMEM = 24 * 1024 * 1024
HIGHEST = lax.Precision.HIGHEST
FULL = pl.BlockSpec(memory_space=pltpu.VMEM)
SMEM = pl.BlockSpec(memory_space=pltpu.SMEM)


def params():
    return pltpu.CompilerParams(vmem_limit_bytes=VMEM)


def edges(block):
    last = lax.slice_in_dim(block, block.shape[2] - HALO, None, axis=2)
    return last, lax.slice_in_dim(block, 0, HALO, axis=2)


def neighbours(last, first):
    count = lax.axis_size("rows")
    forward = [(i, (i + 1) % count) for i in range(count)]
    backward = [(target, source) for source, target in forward]
    above = lax.ppermute(last, "rows", forward)
    below = lax.ppermute(first, "rows", backward)
    return below, above


def mix(field):
    rows, columns = field.shape
    beside = (
        pltpu.roll(field, 1, 0)
        + pltpu.roll(field, rows - 1, 0)
        + pltpu.roll(field, 1, 1)
        + pltpu.roll(field, columns - 1, 1)
    )
    return (1.0 - COUPLING) * field + (COUPLING / 4.0) * beside


def ring(block, below, above):
    return jnp.concatenate([block, below, above], axis=0)


def lattice_kernel(z_ref, c_ref, below_ref, above_ref, twice_ref, next_ref):
    real, imag = (ring(z_ref[i], below_ref[0, i], above_ref[0, i]) for i in range(2))
    const_real, const_imag = (ring(c_ref[i], below_ref[1, i], above_ref[1, i]) for i in range(2))
    for step in range(STEPS):
        twice_ref[step, 0] = 2.0 * real
        twice_ref[step, 1] = 2.0 * imag
        map_real = real * real - imag * imag + const_real
        map_imag = 2.0 * real * imag + const_imag
        real, imag = mix(map_real), mix(map_imag)
    rows = z_ref.shape[1]
    next_ref[0] = real[:rows]
    next_ref[1] = imag[:rows]


def tangent_kernel(me_ref, u_ref, below_ref, above_ref, twice_ref, *rest):
    outs, slabs = rest[:-1], rest[-1]
    real, imag = (ring(u_ref[0, i], below_ref[0, i], above_ref[0, i]) for i in range(2))
    for step in range(STEPS):
        z_real, z_imag = twice_ref[step, 0], twice_ref[step, 1]
        push_real = z_real * real - z_imag * imag
        push_imag = z_real * imag + z_imag * real
        real, imag = mix(push_real), mix(push_imag)
    slabs[0] = real[:8]
    slabs[1] = real[8:16]
    slabs[2] = imag[:8]
    slabs[3] = imag[8:16]
    for shift, out in enumerate(outs):
        out[0] = slabs[lax.rem(me_ref[0] + shift, 4)]


def push(me, vectors, halo, twice, start, count):
    columns = vectors.shape[-1]
    skip = halo[0].shape[0] - count
    return pl.pallas_call(
        tangent_kernel,
        grid=(count,),
        in_specs=[
            SMEM,
            pl.BlockSpec((1, 2, 16, columns), lambda i: (start + i, 0, 0, 0)),
            pl.BlockSpec((1, 2, HALO, columns), lambda i: (skip + i, 0, 0, 0)),
            pl.BlockSpec((1, 2, HALO, columns), lambda i: (skip + i, 0, 0, 0)),
            FULL,
        ],
        out_specs=[pl.BlockSpec((1, 8, columns), lambda i: (i, 0, 0))] * 4,
        out_shape=[jax.ShapeDtypeStruct((count, 8, columns), jnp.float32)] * 4,
        scratch_shapes=[pltpu.VMEM((4, 8, columns), jnp.float32)],
        compiler_params=params(),
        cost_estimate=pl.CostEstimate(
            flops=count * 30_000_000, bytes_accessed=count * 6_000_000, transcendentals=0
        ),
    )(me, pltpu.with_memory_space_constraint(vectors, pltpu.HBM), *halo, twice)


def same_row(shape, period):
    return lax.rem(lax.broadcasted_iota(jnp.int32, shape, 0), period) == lax.rem(
        lax.broadcasted_iota(jnp.int32, shape, 1), period
    )


def owner(shape, group):
    row = lax.broadcasted_iota(jnp.int32, shape, 0)
    column = lax.broadcasted_iota(jnp.int32, shape, 1)
    return jnp.where(row == lax.div(column, group), 1.0, 0.0)


def split(value):
    high = value.astype(jnp.bfloat16)
    return high, (value - high.astype(jnp.float32)).astype(jnp.bfloat16)


def gram_kernel(chunks, me_ref, *refs):
    pieces = refs[: 4 * chunks]
    high_ref, low_ref, gram_ref = refs[4 * chunks :]
    offset = 0
    for chunk in range(chunks):
        count, rows, columns = pieces[4 * chunk].shape
        for shift in range(4):
            source = lax.rem(me_ref[0] + 4 - shift, 4)
            start = pl.multiple_of(source * 64 + offset, 16)
            high, low = split(pieces[4 * chunk + shift][...].reshape(count * rows, columns))
            high_ref[pl.ds(start, count * rows), :] = high
            low_ref[pl.ds(start, count * rows), :] = low
        offset += count * rows
    high = high_ref[...]
    low = low_ref[...]
    last = (((1,), (1,)), ((), ()))
    main = lax.dot_general(high, high, last, preferred_element_type=jnp.float32)
    rest = lax.dot_general(high, low, last, preferred_element_type=jnp.float32)
    full = main + (rest + rest.T)
    full = jnp.where(same_row(full.shape, 8), full, 0.0)
    left = full.reshape(NV, 8, 8 * NV).sum(1)
    gram = lax.dot_general(
        left, owner((NV, 8 * NV), 8), last, precision=HIGHEST, preferred_element_type=jnp.float32
    )
    packed = jnp.concatenate([gram[8 * i : 8 * i + 8] for i in range(4)], axis=1)
    copies = gram_ref.shape[0] // 8
    gram_ref[...] = jnp.broadcast_to(packed[None], (copies, 8, 4 * NV)).reshape(gram_ref.shape)


def inner_products(me, pieces, chunks):
    columns = pieces[0].shape[-1]
    devices = lax.axis_size("rows") * lax.axis_size("vec")
    return pl.pallas_call(
        lambda *refs: gram_kernel(chunks, *refs),
        in_specs=[SMEM] + [FULL] * len(pieces),
        out_specs=[FULL] * 3,
        out_shape=[
            jax.ShapeDtypeStruct((8 * NV, columns), jnp.bfloat16),
            jax.ShapeDtypeStruct((8 * NV, columns), jnp.bfloat16),
            jax.ShapeDtypeStruct((8 * devices, 4 * NV), jnp.float32),
        ],
        compiler_params=params(),
    )(me, *pieces)


def factor_kernel(scale, terms_ref, growth_ref, high_ref, low_ref):
    row = lax.broadcasted_iota(jnp.int32, (NV, 2 * NV), 0)
    column = lax.broadcasted_iota(jnp.int32, (NV, 2 * NV), 1)
    spread = jnp.where(row == column, 1.0, 0.0)
    last = (((1,), (0,)), ((), ()))
    packed = jnp.sum(terms_ref[...].reshape(terms_ref.shape[0] // 8, 8, 4 * NV), axis=0)
    gram = jnp.concatenate([packed[:, NV * i : NV * i + NV] for i in range(4)], axis=0)
    work = jnp.where(column == row + NV, 1.0, 0.0) + lax.dot_general(
        gram, spread, last, precision=HIGHEST, preferred_element_type=jnp.float32
    )
    for k in range(NV):
        pivot_row = work[k : k + 1, :]
        pivot = pivot_row[:, k : k + 1]
        inverse = lax.rsqrt(pivot)
        inverse = inverse * (1.5 - 0.5 * pivot * inverse * inverse)
        scaled = pivot_row * inverse
        factor = work[:, k : k + 1] * inverse
        work = jnp.where(row > k, work - factor * scaled, jnp.where(row == k, scaled, work))
    diagonal = jnp.sum(jnp.where(column == row, work, 0.0), axis=0, keepdims=True)
    growth_ref[...] = jnp.log(diagonal[:, :NV] / scale)
    inverse = work[:, NV:] * scale
    wide = lax.dot_general(
        inverse,
        owner((NV, 8 * NV), 8),
        last,
        precision=HIGHEST,
        preferred_element_type=jnp.float32,
    )
    tall = jnp.broadcast_to(wide[:, None, :], (NV, 8, 8 * NV)).reshape(8 * NV, 8 * NV)
    weights = jnp.where(same_row(tall.shape, 8), tall, 0.0)
    high = weights.astype(jnp.bfloat16)
    high_ref[...] = high
    low_ref[...] = (weights - high.astype(jnp.float32)).astype(jnp.bfloat16)


def factorise(terms, scale):
    return pl.pallas_call(
        lambda *refs: factor_kernel(scale, *refs),
        in_specs=[FULL],
        out_specs=[FULL] * 3,
        out_shape=[jax.ShapeDtypeStruct((1, NV), jnp.float32)]
        + [jax.ShapeDtypeStruct((8 * NV, 8 * NV), jnp.bfloat16)] * 2,
        compiler_params=params(),
    )(terms)


def product(w_high, w_low, high, low):
    value = jnp.dot(w_high, high, preferred_element_type=jnp.float32)
    value += jnp.dot(w_high, low, preferred_element_type=jnp.float32)
    return value + jnp.dot(w_low, high, preferred_element_type=jnp.float32)


def send_kernel(me_ref, w_high, w_low, high_ref, low_ref, next_ref, across_ref, previous_ref):
    for shift, out in ((1, next_ref), (2, across_ref), (3, previous_ref)):
        rows = pl.ds(pl.multiple_of(lax.rem(me_ref[0] + shift, 4) * 64, 64), 64)
        value = product(w_high[rows, :], w_low[rows, :], high_ref[...], low_ref[...])
        out[...] = value.reshape(out.shape)


def send_parts(me, w_high, w_low, high, low):
    columns = high.shape[-1]
    return pl.pallas_call(
        send_kernel,
        in_specs=[SMEM] + [FULL] * 4,
        out_specs=[FULL] * 3,
        out_shape=[jax.ShapeDtypeStruct((8, 8, columns), jnp.float32)] * 3,
        compiler_params=params(),
    )(me, w_high, w_low, high, low)


def own_kernel(me_ref, w_high, w_low, high_ref, low_ref, out):
    rows = pl.ds(pl.multiple_of(me_ref[0] * 64, 64), 64)
    value = product(w_high[rows, :], w_low[rows, :], high_ref[...], low_ref[...])
    out[...] = value.reshape(out.shape)


def own_part(me, w_high, w_low, high, low):
    return pl.pallas_call(
        own_kernel,
        in_specs=[SMEM] + [FULL] * 4,
        out_specs=FULL,
        out_shape=jax.ShapeDtypeStruct((8, 8, high.shape[-1]), jnp.float32),
        compiler_params=params(),
    )(me, w_high, w_low, high, low)


def assemble_kernel(me_ref, *refs):
    parts, out = refs[:-1], refs[-1]
    for back, part in enumerate(parts):
        out[:, lax.rem(me_ref[0] + 4 - back, 4)] = part[...]


def assemble(me, *parts):
    count, rows, columns = parts[0].shape
    step = 2
    return pl.pallas_call(
        assemble_kernel,
        grid=(count // step,),
        in_specs=[SMEM] + [pl.BlockSpec((step, rows, columns), lambda i: (i, 0, 0))] * 4,
        out_specs=pl.BlockSpec((step, 4, rows, columns), lambda i: (i, 0, 0, 0)),
        out_shape=jax.ShapeDtypeStruct((count, 4, rows, columns), jnp.float32),
        compiler_params=params(),
    )(me, *parts)


def shifted(block, shift):
    return lax.ppermute(block, "vec", [(i, (i + shift) % 4) for i in range(4)])


def exchange(blocks):
    moved = {shift: shifted(blocks[shift], shift) for shift in (2, 1, 3)}
    return [blocks[0], moved[1], moved[2], moved[3]]


def all_terms(copies):
    return lax.all_to_all(copies, ("rows", "vec"), 0, 0, tiled=True)


CHUNKS = (2, 6)


def per_device(lattice_state, constant_field, tangents):
    me = lax.axis_index("vec").astype(jnp.int32).reshape(1)
    rows, columns = lattice_state.shape[1:]
    scale = math.sqrt(2.0 * rows * lax.axis_size("rows") * columns)
    fields = jnp.stack([lattice_state, constant_field])
    first = jnp.concatenate([fields, tangents[: CHUNKS[0]]], axis=0)
    ahead = neighbours(*edges(first))
    ahead, rest = lax.optimization_barrier((ahead, edges(tangents[CHUNKS[0] :])))
    halos = [ahead, neighbours(*rest)]
    twice, next_state = pl.pallas_call(
        lattice_kernel,
        in_specs=[FULL] * 4,
        out_specs=[FULL] * 2,
        out_shape=[
            jax.ShapeDtypeStruct((STEPS, 2, rows + 2 * HALO, columns), jnp.float32),
            jax.ShapeDtypeStruct((2, rows, columns), jnp.float32),
        ],
        compiler_params=params(),
    )(lattice_state, constant_field, *halos[0])
    pieces, start = [], 0
    for count, halo in zip(CHUNKS, halos):
        if pieces:
            halo, blocks = lax.optimization_barrier((halo, blocks))
        blocks = push(me, tangents, halo, twice, start, count)
        if pieces:
            blocks, pieces = lax.optimization_barrier((blocks, pieces))
        pieces += exchange(blocks)
        start += count
    high, low, copies = inner_products(me, pieces, len(CHUNKS))
    growth, w_high, w_low = factorise(all_terms(copies), scale)
    following, across, previous = send_parts(me, w_high, w_low, high, low)
    across = shifted(across, 2)
    before = shifted(following, 1)
    after = shifted(previous, 3)
    own = own_part(me, w_high, w_low, high, low)
    basis = assemble(me, own, before, across, after)
    return (next_state, basis.reshape(tangents.shape), growth.reshape(NV))


def solution(mesh):
    return jax.shard_map(
        per_device,
        mesh=mesh,
        in_specs=(P(None, "rows", None), P(None, "rows", None), P("vec", None, "rows", None)),
        out_specs=(P(None, "rows", None), P("vec", None, "rows", None), P()),
        check_vma=False,
    )
```

time: 177 us -> 163 us (0.921)
  blocking collectives: 0 us -> 24.4 us
  waiting for transfers between devices: 86.9 us -> 74.3 us
  Pallas kernels: 42.6 us -> 30.5 us
  starting transfers between devices: 38.1 us -> 27 us
    all_to_all x0 -> x1, blocking collectives: none -> 24.4 us  [all_terms(): return lax.all_to_all(copies, ('rows', 'vec'), 0, 0, tiled=True)]
    ppermute x10 -> x0, starting transfers between devices: 12.4 us -> none  [group_sum(): lax.ppermute(value, axis, [(i, i ^ k * stride) for i in range(size)])]
    ppermute x10 -> x0, waiting for transfers between devices: 10.2 us -> none  [group_sum(): lax.ppermute(value, axis, [(i, i ^ k * stride) for i in range(size)])]
    ppermute x9, waiting for transfers between devices: 72.4 us -> 68.4 us  [shifted(): return lax.ppermute(block, 'vec', [(i, (i + shift) % 4) for i in range(4)])]
    unnamed x28 -> x4, local copies, waits for them, and re-layouts: 3.74 us -> 0.01 us
    pallas_call x1, Pallas kernels: 5.35 us -> 1.86 us  [inner_products(): pl.pallas_call(lambda *refs: gram_kernel(chunks, *refs), in_specs=[SMEM]...]
    pallas_call x1 -> x3, Pallas kernels: 10.9 us -> 8.24 us  [the longest x1 3.67 us: factorise(): pl.pallas_call(lambda *refs: factor_kernel(scale, *refs), in_specs=[FULL]...]
    pallas_call x1, Pallas kernels: 4.67 us -> 2.43 us  [assemble(): pl.pallas_call(assemble_kernel, grid=(count // step,), in_specs=[SMEM] +...]
  transfers between devices with their start and end apart: 25 -> 13, of which waited for: 14 -> 6; matrix products, arithmetic and copies ran while one was open for 1% -> 2% of each run, Pallas kernels for 12% -> 12%
where the time goes in v2:
time: 163 us
  waiting for transfers between devices  74.3 us (46%)
  Pallas kernels  30.5 us (19%)
  starting transfers between devices  27 us (17%)
  blocking collectives  24.4 us (15%)
  local copies, waits for them, and re-layouts  4.73 us (3%)
    ppermute x9, waiting for transfers between devices, shifted(): return lax.ppermute(block, 'vec', [(i, (i + shift) % 4) for i in range(4)])  68.4 us
    all_to_all x1, blocking collectives, all_terms(): return lax.all_to_all(copies, ('rows', 'vec'), 0, 0, tiled=True)  24.4 us
    ppermute x9, starting transfers between devices, shifted(): return lax.ppermute(block, 'vec', [(i, (i + shift) % 4) for i in range(4)])  16 us
    pallas_call x2, Pallas kernels, push(): pl.pallas_call(tangent_kernel, grid=(count,), in_specs=[SMEM, pl.BlockSpe...  15.8 us
    ppermute x2, starting transfers between devices, neighbours(): below = lax.ppermute(first, 'rows', backward)  11 us
    ppermute x2, waiting for transfers between devices, neighbours(): above = lax.ppermute(last, 'rows', forward)  5.93 us
    pallas_call x1, Pallas kernels, factorise(): pl.pallas_call(lambda *refs: factor_kernel(scale, *refs), in_specs=[FULL]...  3.67 us
    pallas_call x1, Pallas kernels, send_parts(): pl.pallas_call(send_kernel, in_specs=[SMEM] + [FULL] * 4, out_specs=[FULL...  3.38 us
  transfers between devices with their start and end apart: 13, of which 6 were waited for; matrix products, arithmetic and copies ran while one was open for 2% of the time, Pallas kernels for 12%

profile of v2, /device:TPU:0, one launch (start us, length us, event | category | flops | bytes accessed | tf_op | source)
XLA Modules:
  0.0 163.1 jit_solution(9031144643102441664)
XLA Ops:
  0.7 1.4 slice.18
  2.0 1.4 pad_maximum_fusion
  3.5 5.8 %collective-permute-start = (f32[4,2,4,4096]{3,2,1,0:T(4,128)S(1)}, f32[4,2,4,4096]{3,2,1,0:T(4,128)S(1)}, u32[]{:S(2)}, u32[]{:S(2)}) collective-permute-start(f32[4,2,4,4096]{3,2,1,0:T(4,128)S(1)} %get-tuple-element.72), channel_id=1, source_target_pairs={{4,0},{8,4},{12,8},{16,12},{20,16},{24,20},{28,24},{32,28},{36,32}... | collective-permute-start | bytes 1572872 | tf_op jit(solution)/shard_map/ppermute | solution.py:34
  9.4 3.3 %fusion = (f32[6,2,4,4096]{3,2,1,0:T(4,128)}, f32[6,2,4,4096]{3,2,1,0:T(4,128)}) fusion(f32[8,2,16,4096]{3,2,1,0:T(8,128)} %u_ref.3), kind=kLoop, calls=%fused_computation.3 | loop fusion | bytes 3145728 | tf_op jit(solution)/shard_map/slice | solution.py:26
  12.7 3.5 %collective-permute-done.1.above_ref = f32[4,2,4,4096]{3,2,1,0:T(4,128)S(1)} collective-permute-done((f32[4,2,4,4096]{3,2,1,0:T(4,128)S(1)}, f32[4,2,4,4096]{3,2,1,0:T(4,128)S(1)}, u32[]{:S(2)}, u32[]{:S(2)}) %collective-permute-start.1) | collective-permute-done | bytes 524320 | tf_op jit(solution)/shard_map/ppermute | solution.py:33
  16.1 5.1 %collective-permute-start.2 = (f32[6,2,4,4096]{3,2,1,0:T(4,128)}, f32[6,2,4,4096]{3,2,1,0:T(4,128)S(1)}, u32[]{:S(2)}, u32[]{:S(2)}) collective-permute-start(f32[6,2,4,4096]{3,2,1,0:T(4,128)} %get-tuple-element.39), channel_id=1, source_target_pairs={{4,0},{8,4},{12,8},{16,12},{20,16},{24,20},{28,24},{32,28},{36,32}... | collective-permute-start | bytes 2359304 | tf_op jit(solution)/shard_map/ppermute | solution.py:34
  21.3 2.2 %shard_map.58 = (f32[3,2,24,4096]{3,2,1,0:T(8,128)S(1)}, f32[2,16,4096]{2,1,0:T(8,128)}) custom-call(f32[2,16,4096]{2,1,0:T(8,128)S(1)} %copy-done, f32[2,16,4096]{2,1,0:T(8,128)S(1)} %copy-done.1, f32[4,2,4,4096]{3,2,1,0:T(4,128)S(1)} %collective-permute-done.below_ref, f32[4,2,4,4096]{3,2,1,0:T(4,128)S(1)} %collective-permute-done.1.above_ref), custom_call_target="tpu_custom_call" | custom-call | tf_op jit(solution)/shard_map/pallas_call | solution.py:298
  23.5 4.5 %shard_map.59 = (f32[2,8,4096]{2,1,0:T(8,128)S(1)}, f32[2,8,4096]{2,1,0:T(8,128)S(1)}, f32[2,8,4096]{2,1,0:T(8,128)S(1)}, f32[2,8,4096]{2,1,0:T(8,128)S(1)}) custom-call(s32[1]{0:T(128)} %bitcast.2.me_ref.refs_0_, f32[8,2,16,4096]{3,2,1,0:T(8,128)} %u_ref.3, f32[4,2,4,4096]{3,2,1,0:T(4,128)S(1)} %collective-permute-done.below_ref, ...), custom_call_target="tpu_custom_call" | custom-call | flops 60000000 | bytes 12000000 | tf_op jit(solution)/shard_map/pallas_call | solution.py:86
  28.0 1.6 %collective-permute-start.4 = (f32[2,8,4096]{2,1,0:T(8,128)S(1)}, f32[2,8,4096]{2,1,0:T(8,128)S(1)}, u32[]{:S(2)}, u32[]{:S(2)}) collective-permute-start(f32[2,8,4096]{2,1,0:T(8,128)S(1)} %get-tuple-element.43), channel_id=1, source_target_pairs={{0,1},{1,2},{2,3},{3,0},{4,5},{5,6},{6,7},{7,4},{8,9},{9,10},{10,1... | collective-permute-start | bytes 786440 | tf_op jit(solution)/shard_map/ppermute | solution.py:274
  29.6 2.9 %collective-permute-start.5 = (f32[2,8,4096]{2,1,0:T(8,128)S(1)}, f32[2,8,4096]{2,1,0:T(8,128)S(1)}, u32[]{:S(2)}, u32[]{:S(2)}) collective-permute-start(f32[2,8,4096]{2,1,0:T(8,128)S(1)} %get-tuple-element.44), channel_id=1, source_target_pairs={{0,2},{1,3},{2,0},{3,1},{4,6},{5,7},{6,4},{7,5},{8,10},{9,11},{10,... | collective-permute-start | bytes 786440 | tf_op jit(solution)/shard_map/ppermute | solution.py:274
  32.5 1.3 collective-permute-start.6
  33.9 2.5 %collective-permute-done.3.above_ref = f32[6,2,4,4096]{3,2,1,0:T(4,128)} collective-permute-done((f32[6,2,4,4096]{3,2,1,0:T(4,128)}, f32[6,2,4,4096]{3,2,1,0:T(4,128)}, u32[]{:S(2)}, u32[]{:S(2)}) %collective-permute-start.3) | collective-permute-done | bytes 786464 | tf_op jit(solution)/shard_map/ppermute | solution.py:33
  36.3 11.3 %shard_map.60 = (f32[6,8,4096]{2,1,0:T(8,128)S(1)}, f32[6,8,4096]{2,1,0:T(8,128)S(1)}, f32[6,8,4096]{2,1,0:T(8,128)S(1)}, f32[6,8,4096]{2,1,0:T(8,128)S(1)}) custom-call(s32[1]{0:T(128)} %bitcast.2.me_ref.refs_0_, f32[8,2,16,4096]{3,2,1,0:T(8,128)} %u_ref.3, f32[6,2,4,4096]{3,2,1,0:T(4,128)S(1)} %collective-permute-done.2.below_ref, ...), custom_call_target="tpu_custom_call" | custom-call | flops 180000000 | bytes 36000000 | tf_op jit(solution)/shard_map/pallas_call | solution.py:86
  47.7 1.7 %collective-permute-start.7 = (f32[6,8,4096]{2,1,0:T(8,128)S(1)}, f32[6,8,4096]{2,1,0:T(8,128)S(1)}, u32[]{:S(2)}, u32[]{:S(2)}) collective-permute-start(f32[6,8,4096]{2,1,0:T(8,128)S(1)} %get-tuple-element.57), channel_id=1, source_target_pairs={{0,1},{1,2},{2,3},{3,0},{4,5},{5,6},{6,7},{7,4},{8,9},{9,10},{10,1... | collective-permute-start | bytes 2359304 | tf_op jit(solution)/shard_map/ppermute | solution.py:274
  49.4 2.9 %collective-permute-start.8 = (f32[6,8,4096]{2,1,0:T(8,128)S(1)}, f32[6,8,4096]{2,1,0:T(8,128)S(1)}, u32[]{:S(2)}, u32[]{:S(2)}) collective-permute-start(f32[6,8,4096]{2,1,0:T(8,128)S(1)} %get-tuple-element.58), channel_id=1, source_target_pairs={{0,2},{1,3},{2,0},{3,1},{4,6},{5,7},{6,4},{7,5},{8,10},{9,11},{10,... | collective-permute-start | bytes 2359304 | tf_op jit(solution)/shard_map/ppermute | solution.py:274
  53.6 23.7 %collective-permute-done.7.refs_6_ = f32[6,8,4096]{2,1,0:T(8,128)S(1)} collective-permute-done((f32[6,8,4096]{2,1,0:T(8,128)S(1)}, f32[6,8,4096]{2,1,0:T(8,128)S(1)}, u32[]{:S(2)}, u32[]{:S(2)}) %collective-permute-start.7) | collective-permute-done | bytes 786464 | tf_op jit(solution)/shard_map/ppermute | solution.py:274
  78.0 1.9 %shard_map.61 = (bf16[256,4096]{1,0:T(8,128)(2,1)S(1)}, bf16[256,4096]{1,0:T(8,128)(2,1)S(1)}, f32[1024,128]{1,0:T(8,128)S(1)}) custom-call(s32[1]{0:T(128)} %bitcast.2.me_ref.refs_0_, f32[2,8,4096]{2,1,0:T(8,128)S(1)} %get-tuple-element.52.refs_1_, f32[2,8,4096]{2,1,0:T(8,128)S(1)} %collective-permute-done.4.refs_2_, ...), custom_call_target="tpu_custom_call" | custom-call | tf_op jit(solution)/shard_map/pallas_call | solution.py:155
  79.8 24.4 %all_to_all.11 = f32[128,8,128]{2,1,0:T(8,128)S(1)} all-to-all(f32[128,8,128]{2,1,0:T(8,128)S(1)} %bitcast.10), channel_id=1, replica_groups=mesh['rows'=32,'vec'=4] {'rows','vec'}, dimensions={0} | all-to-all | bytes 1048576 | tf_op jit(solution)/shard_map/all_to_all | solution.py:283
  104.3 3.7 %shard_map.62 = (f32[1,32]{1,0:T(1,128)}, bf16[256,256]{1,0:T(8,128)(2,1)S(1)}, bf16[256,256]{1,0:T(8,128)(2,1)S(1)}) custom-call(f32[1024,128]{1,0:T(8,128)S(1)} %bitcast.7), custom_call_target="tpu_custom_call" | custom-call | tf_op jit(solution)/shard_map/pallas_call | solution.py:204
  107.9 3.4 %shard_map.64 = (f32[8,8,4096]{2,1,0:T(8,128)S(1)}, f32[8,8,4096]{2,1,0:T(8,128)S(1)}, f32[8,8,4096]{2,1,0:T(8,128)S(1)}) custom-call(s32[1]{0:T(128)} %bitcast.2.me_ref.refs_0_, bf16[256,256]{1,0:T(8,128)(2,1)S(1)} %get-tuple-element.61.w_high, bf16[256,256]{1,0:T(8,128)(2,1)S(1)} %get-tuple-element.62.w_low, ...), custom_call_target="tpu_custom_call" | custom-call | tf_op jit(solution)/shard_map/pallas_call | solution.py:229
  112.0 1.9 %collective-permute-start.11 = (f32[8,8,4096]{2,1,0:T(8,128)S(1)}, f32[8,8,4096]{2,1,0:T(8,128)S(1)}, u32[]{:S(2)}, u32[]{:S(2)}) collective-permute-start(f32[8,8,4096]{2,1,0:T(8,128)S(1)} %get-tuple-element.66), channel_id=1, source_target_pairs={{0,2},{1,3},{2,0},{3,1},{4,6},{5,7},{6,4},{7,5},{8,10},{9,11},{10,... | collective-permute-start | bytes 3145736 | tf_op jit(solution)/shard_map/ppermute | solution.py:274
  113.9 1.6 collective-permute-start.12
  116.7 43.4 %collective-permute-done.10.refs_1_ = f32[8,8,4096]{2,1,0:T(8,128)S(1)} collective-permute-done((f32[8,8,4096]{2,1,0:T(8,128)S(1)}, f32[8,8,4096]{2,1,0:T(8,128)S(1)}, u32[]{:S(2)}, u32[]{:S(2)}) %collective-permute-start.10) | collective-permute-done | bytes 1048608 | tf_op jit(solution)/shard_map/ppermute | solution.py:274
  160.7 2.4 %shard_map.65 = f32[8,4,8,4096]{3,2,1,0:T(8,128)} custom-call(s32[1]{0:T(128)} %bitcast.2.me_ref.refs_0_, f32[8,8,4096]{2,1,0:T(8,128)S(1)} %shard_map.63.refs_0_, f32[8,8,4096]{2,1,0:T(8,128)S(1)} %collective-permute-done.10.refs_1_, f32[8,8,4096]{2,1,0:T(8,128)S(1)} %collective-permute-done.11.refs_2_, f32[8,8,4096]{2,1,0:T(8,128)S(1)} %collective-permute-done.12.refs_3_), custom_call_target="tpu_custom_call" | custom-call | tf_op jit(solution)/shard_map/pallas_call | solution.py:263
  (18 shorter events, 4.6 us)
Async XLA Ops:
  0.6 20.7 %copy-start = (f32[2,16,4096]{2,1,0:T(8,128)S(1)}, f32[2,16,4096]{2,1,0:T(8,128)}, u32[]{:S(2)}) copy-start(f32[2,16,4096]{2,1,0:T(8,128)} %z_ref.1) | copy-start | bytes 1572868
  0.6 20.7 %copy-start.1 = (f32[2,16,4096]{2,1,0:T(8,128)S(1)}, f32[2,16,4096]{2,1,0:T(8,128)}, u32[]{:S(2)}) copy-start(f32[2,16,4096]{2,1,0:T(8,128)} %c_ref.1) | copy-start | bytes 1572868
  3.5 12.7 %collective-permute-start.1 = (f32[4,2,4,4096]{3,2,1,0:T(4,128)S(1)}, f32[4,2,4,4096]{3,2,1,0:T(4,128)S(1)}, u32[]{:S(2)}, u32[]{:S(2)}) collective-permute-start(f32[4,2,4,4096]{3,2,1,0:T(4,128)S(1)} %get-tuple-element.71), channel_id=1, source_target_pairs={{0,4},{4,8},{8,12},{12,16},{16,20},{20,24},{24,28},{28,32},{32,36}... | collective-permute-start | bytes 1572872 | tf_op jit(solution)/shard_map/ppermute | solution.py:33
  3.5 12.6 %collective-permute-start = (f32[4,2,4,4096]{3,2,1,0:T(4,128)S(1)}, f32[4,2,4,4096]{3,2,1,0:T(4,128)S(1)}, u32[]{:S(2)}, u32[]{:S(2)}) collective-permute-start(f32[4,2,4,4096]{3,2,1,0:T(4,128)S(1)} %get-tuple-element.72), channel_id=1, source_target_pairs={{4,0},{8,4},{12,8},{16,12},{20,16},{24,20},{28,24},{32,28},{36,32}... | collective-permute-start | bytes 1572872 | tf_op jit(solution)/shard_map/ppermute | solution.py:34
  16.1 17.7 %collective-permute-start.2 = (f32[6,2,4,4096]{3,2,1,0:T(4,128)}, f32[6,2,4,4096]{3,2,1,0:T(4,128)S(1)}, u32[]{:S(2)}, u32[]{:S(2)}) collective-permute-start(f32[6,2,4,4096]{3,2,1,0:T(4,128)} %get-tuple-element.39), channel_id=1, source_target_pairs={{4,0},{8,4},{12,8},{16,12},{20,16},{24,20},{28,24},{32,28},{36,32}... | collective-permute-start | bytes 2359304 | tf_op jit(solution)/shard_map/ppermute | solution.py:34
  21.3 15.1 %collective-permute-start.3 = (f32[6,2,4,4096]{3,2,1,0:T(4,128)}, f32[6,2,4,4096]{3,2,1,0:T(4,128)}, u32[]{:S(2)}, u32[]{:S(2)}) collective-permute-start(f32[6,2,4,4096]{3,2,1,0:T(4,128)} %get-tuple-element.40), channel_id=1, source_target_pairs={{0,4},{4,8},{8,12},{12,16},{16,20},{20,24},{24,28},{28,32},{32,36}... | collective-permute-start | bytes 2359304 | tf_op jit(solution)/shard_map/ppermute | solution.py:33
  28.0 19.7 %collective-permute-start.4 = (f32[2,8,4096]{2,1,0:T(8,128)S(1)}, f32[2,8,4096]{2,1,0:T(8,128)S(1)}, u32[]{:S(2)}, u32[]{:S(2)}) collective-permute-start(f32[2,8,4096]{2,1,0:T(8,128)S(1)} %get-tuple-element.43), channel_id=1, source_target_pairs={{0,1},{1,2},{2,3},{3,0},{4,5},{5,6},{6,7},{7,4},{8,9},{9,10},{10,1... | collective-permute-start | bytes 786440 | tf_op jit(solution)/shard_map/ppermute | solution.py:274
  29.6 18.1 %collective-permute-start.5 = (f32[2,8,4096]{2,1,0:T(8,128)S(1)}, f32[2,8,4096]{2,1,0:T(8,128)S(1)}, u32[]{:S(2)}, u32[]{:S(2)}) collective-permute-start(f32[2,8,4096]{2,1,0:T(8,128)S(1)} %get-tuple-element.44), channel_id=1, source_target_pairs={{0,2},{1,3},{2,0},{3,1},{4,6},{5,7},{6,4},{7,5},{8,10},{9,11},{10,... | collective-permute-start | bytes 786440 | tf_op jit(solution)/shard_map/ppermute | solution.py:274
  32.5 15.2 %collective-permute-start.6 = (f32[2,8,4096]{2,1,0:T(8,128)S(1)}, f32[2,8,4096]{2,1,0:T(8,128)S(1)}, u32[]{:S(2)}, u32[]{:S(2)}) collective-permute-start(f32[2,8,4096]{2,1,0:T(8,128)S(1)} %get-tuple-element.45), channel_id=1, source_target_pairs={{0,3},{1,0},{2,1},{3,2},{4,7},{5,4},{6,5},{7,6},{8,11},{9,8},{10,9... | collective-permute-start | bytes 786440 | tf_op jit(solution)/shard_map/ppermute | solution.py:274
  47.7 29.6 %collective-permute-start.7 = (f32[6,8,4096]{2,1,0:T(8,128)S(1)}, f32[6,8,4096]{2,1,0:T(8,128)S(1)}, u32[]{:S(2)}, u32[]{:S(2)}) collective-permute-start(f32[6,8,4096]{2,1,0:T(8,128)S(1)} %get-tuple-element.57), channel_id=1, source_target_pairs={{0,1},{1,2},{2,3},{3,0},{4,5},{5,6},{6,7},{7,4},{8,9},{9,10},{10,1... | collective-permute-start | bytes 2359304 | tf_op jit(solution)/shard_map/ppermute | solution.py:274
  49.4 28.0 %collective-permute-start.8 = (f32[6,8,4096]{2,1,0:T(8,128)S(1)}, f32[6,8,4096]{2,1,0:T(8,128)S(1)}, u32[]{:S(2)}, u32[]{:S(2)}) collective-permute-start(f32[6,8,4096]{2,1,0:T(8,128)S(1)} %get-tuple-element.58), channel_id=1, source_target_pairs={{0,2},{1,3},{2,0},{3,1},{4,6},{5,7},{6,4},{7,5},{8,10},{9,11},{10,... | collective-permute-start | bytes 2359304 | tf_op jit(solution)/shard_map/ppermute | solution.py:274
  52.3 25.7 %collective-permute-start.9 = (f32[6,8,4096]{2,1,0:T(8,128)S(1)}, f32[6,8,4096]{2,1,0:T(8,128)S(1)}, u32[]{:S(2)}, u32[]{:S(2)}) collective-permute-start(f32[6,8,4096]{2,1,0:T(8,128)S(1)} %get-tuple-element.59), channel_id=1, source_target_pairs={{0,3},{1,0},{2,1},{3,2},{4,7},{5,4},{6,5},{7,6},{8,11},{9,8},{10,9... | collective-permute-start | bytes 2359304 | tf_op jit(solution)/shard_map/ppermute | solution.py:274
  111.3 48.8 %collective-permute-start.10 = (f32[8,8,4096]{2,1,0:T(8,128)S(1)}, f32[8,8,4096]{2,1,0:T(8,128)S(1)}, u32[]{:S(2)}, u32[]{:S(2)}) collective-permute-start(f32[8,8,4096]{2,1,0:T(8,128)S(1)} %get-tuple-element.65), channel_id=1, source_target_pairs={{0,1},{1,2},{2,3},{3,0},{4,5},{5,6},{6,7},{7,4},{8,9},{9,10},{10,1... | collective-permute-start | bytes 3145736 | tf_op jit(solution)/shard_map/ppermute | solution.py:274
  112.0 48.1 %collective-permute-start.11 = (f32[8,8,4096]{2,1,0:T(8,128)S(1)}, f32[8,8,4096]{2,1,0:T(8,128)S(1)}, u32[]{:S(2)}, u32[]{:S(2)}) collective-permute-start(f32[8,8,4096]{2,1,0:T(8,128)S(1)} %get-tuple-element.66), channel_id=1, source_target_pairs={{0,2},{1,3},{2,0},{3,1},{4,6},{5,7},{6,4},{7,5},{8,10},{9,11},{10,... | collective-permute-start | bytes 3145736 | tf_op jit(solution)/shard_map/ppermute | solution.py:274
  113.9 46.8 %collective-permute-start.12 = (f32[8,8,4096]{2,1,0:T(8,128)S(1)}, f32[8,8,4096]{2,1,0:T(8,128)S(1)}, u32[]{:S(2)}, u32[]{:S(2)}) collective-permute-start(f32[8,8,4096]{2,1,0:T(8,128)S(1)} %get-tuple-element.67), channel_id=1, source_target_pairs={{0,3},{1,0},{2,1},{3,2},{4,7},{5,4},{6,5},{7,6},{8,11},{9,8},{10,9... | collective-permute-start | bytes 3145736 | tf_op jit(solution)/shard_map/ppermute | solution.py:274

commit v3 on v2

--- a/solution.py
+++ b/solution.py
@@ -220,7 +220,8 @@
 def send_kernel(me_ref, w_high, w_low, high_ref, low_ref, next_ref, across_ref, previous_ref):
     for shift, out in ((1, next_ref), (2, across_ref), (3, previous_ref)):
         rows = pl.ds(pl.multiple_of(lax.rem(me_ref[0] + shift, 4) * 64, 64), 64)
-        value = product(w_high[rows, :], w_low[rows, :], high_ref[...], low_ref[...])
+        skip = high_ref.shape[1] - out.shape[2]
+        value = product(w_high[rows, :], w_low[rows, :], high_ref[:, skip:], low_ref[:, skip:])
         out[...] = value.reshape(out.shape)
 
 
@@ -230,40 +231,61 @@
         send_kernel,
         in_specs=[SMEM] + [FULL] * 4,
         out_specs=[FULL] * 3,
-        out_shape=[jax.ShapeDtypeStruct((8, 8, columns), jnp.float32)] * 3,
+        out_shape=[
+            jax.ShapeDtypeStruct((8, 8, width), jnp.float32)
+            for width in (columns, columns - NEAR, columns)
+        ],
         compiler_params=params(),
     )(me, w_high, w_low, high, low)
 
 
-def own_kernel(me_ref, w_high, w_low, high_ref, low_ref, out):
-    rows = pl.ds(pl.multiple_of(me_ref[0] * 64, 64), 64)
-    value = product(w_high[rows, :], w_low[rows, :], high_ref[...], low_ref[...])
-    out[...] = value.reshape(out.shape)
-
-
-def own_part(me, w_high, w_low, high, low):
+def own_kernel(me_ref, w_high, w_low, high_ref, low_ref, *refs):
+    pieces, (own_ref, far_ref, far_high, far_low) = refs[:-4], refs[-4:]
+    me = me_ref[0]
+    for back, piece in enumerate(pieces):
+        start = pl.multiple_of(lax.rem(me + 4 - back, 4) * 64, 64)
+        high, low = split(piece[...].reshape(64, piece.shape[2]))
+        far_high[pl.ds(start, 64), :] = high
+        far_low[pl.ds(start, 64), :] = low
+    rows = pl.ds(pl.multiple_of(me * 64, 64), 64)
+    own_high, own_low = w_high[rows, :], w_low[rows, :]
+    own_ref[...] = product(own_high, own_low, high_ref[...], low_ref[...]).reshape(own_ref.shape)
+    far_ref[...] = product(own_high, own_low, far_high[...], far_low[...]).reshape(far_ref.shape)
+
+
+def own_parts(me, w_high, w_low, high, low, pieces):
+    columns = high.shape[-1]
     return pl.pallas_call(
         own_kernel,
-        in_specs=[SMEM] + [FULL] * 4,
-        out_specs=FULL,
-        out_shape=jax.ShapeDtypeStruct((8, 8, high.shape[-1]), jnp.float32),
-        compiler_params=params(),
-    )(me, w_high, w_low, high, low)
-
-
-def assemble_kernel(me_ref, *refs):
-    parts, out = refs[:-1], refs[-1]
-    for back, part in enumerate(parts):
-        out[:, lax.rem(me_ref[0] + 4 - back, 4)] = part[...]
-
-
-def assemble(me, *parts):
-    count, rows, columns = parts[0].shape
+        in_specs=[SMEM] + [FULL] * (4 + len(pieces)),
+        out_specs=[FULL] * 2,
+        out_shape=[
+            jax.ShapeDtypeStruct((8, 8, width), jnp.float32) for width in (columns, NEAR)
+        ],
+        scratch_shapes=[pltpu.VMEM((8 * NV, NEAR), jnp.bfloat16)] * 2,
+        compiler_params=params(),
+    )(me, w_high, w_low, high, low, *pieces)
+
+
+def assemble_kernel(me_ref, own_ref, far_ref, before_ref, across_ref, after_ref, out):
+    me = me_ref[0]
+    opposite_slab = lax.rem(me + 2, 4)
+    out[:, me] = own_ref[...]
+    out[:, opposite_slab, :, :NEAR] = far_ref[...]
+    out[:, opposite_slab, :, NEAR:] = across_ref[...]
+    out[:, lax.rem(me + 3, 4)] = before_ref[...]
+    out[:, lax.rem(me + 1, 4)] = after_ref[...]
+
+
+def assemble(me, own, before, across, after):
+    parts = (*own, before, across, after)
+    count, rows, columns = before.shape
     step = 2
     return pl.pallas_call(
         assemble_kernel,
         grid=(count // step,),
-        in_specs=[SMEM] + [pl.BlockSpec((step, rows, columns), lambda i: (i, 0, 0))] * 4,
+        in_specs=[SMEM]
+        + [pl.BlockSpec((step, rows, part.shape[2]), lambda i: (i, 0, 0)) for part in parts],
         out_specs=pl.BlockSpec((step, 4, rows, columns), lambda i: (i, 0, 0, 0)),
         out_shape=jax.ShapeDtypeStruct((count, 4, rows, columns), jnp.float32),
         compiler_params=params(),
@@ -279,11 +301,19 @@
     return [blocks[0], moved[1], moved[2], moved[3]]
 
 
+def opposite(blocks):
+    one = lax.ppermute(blocks[3], "vec", [(0, 1), (1, 2), (2, 3)])
+    two = lax.ppermute(blocks[0], "vec", [(0, 2), (1, 3)])
+    three = lax.ppermute(blocks[1], "vec", [(0, 3)])
+    return [blocks[2], one, two, three]
+
+
 def all_terms(copies):
     return lax.all_to_all(copies, ("rows", "vec"), 0, 0, tiled=True)
 
 
 CHUNKS = (2, 6)
+NEAR = 2048
 
 
 def per_device(lattice_state, constant_field, tangents):
@@ -305,22 +335,30 @@
         ],
         compiler_params=params(),
     )(lattice_state, constant_field, *halos[0])
-    pieces, start = [], 0
+    pieces, local, start = [], [], 0
     for count, halo in zip(CHUNKS, halos):
         if pieces:
             halo, blocks = lax.optimization_barrier((halo, blocks))
         blocks = push(me, tangents, halo, twice, start, count)
         if pieces:
             blocks, pieces = lax.optimization_barrier((blocks, pieces))
+        local.append(blocks)
         pieces += exchange(blocks)
         start += count
+    slabs = [
+        jnp.concatenate([blocks[shift][:, :, :NEAR] for blocks in local], axis=0)
+        for shift in range(4)
+    ]
+    slabs, pieces[5] = lax.optimization_barrier((slabs, pieces[5]))
+    far = opposite(slabs)
     high, low, copies = inner_products(me, pieces, len(CHUNKS))
-    growth, w_high, w_low = factorise(all_terms(copies), scale)
+    terms, far = lax.optimization_barrier((all_terms(copies), far))
+    growth, w_high, w_low = factorise(terms, scale)
     following, across, previous = send_parts(me, w_high, w_low, high, low)
     across = shifted(across, 2)
     before = shifted(following, 1)
     after = shifted(previous, 3)
-    own = own_part(me, w_high, w_low, high, low)
+    own = own_parts(me, w_high, w_low, high, low, far)
     basis = assemble(me, own, before, across, after)
     return (next_state, basis.reshape(tangents.shape), growth.reshape(NV))
 

time: 163 us -> 159 us (0.975); the launches traced: 163 us -> 157 us
  waiting for transfers between devices: 74.3 us -> 57.8 us
  starting transfers between devices: 27 us -> 42.5 us
  blocking collectives: 24.4 us -> 18.8 us
    ppermute x9, waiting for transfers between devices: 68.4 us -> 52 us  [shifted(): return lax.ppermute(block, 'vec', [(i, (i + shift) % 4) for i in range(4)])]
    ppermute x0 -> x3, starting transfers between devices: none -> 16.1 us  [the longest x1 10.2 us: opposite(): one = lax.ppermute(blocks[3], 'vec', [(0, 1), (1, 2), (2, 3)])]
    all_to_all x1, blocking collectives: 24.4 us -> 18.8 us  [all_terms(): return lax.all_to_all(copies, ('rows', 'vec'), 0, 0, tiled=True)]
  transfers between devices with their start and end apart: 13 -> 16, of which waited for: 6 -> 6; matrix products, arithmetic and copies ran while one was open for 2% -> 2% of each run, Pallas kernels for 12% -> 14%
where the time goes in v3:
time: 159 us; the launch traced here: 157 us
  waiting for transfers between devices  57.8 us (36%)
  starting transfers between devices  42.5 us (27%)
  Pallas kernels  30.8 us (19%)
  blocking collectives  18.8 us (12%)
  local copies, waits for them, and re-layouts  4.87 us (3%)
    ppermute x9, waiting for transfers between devices, shifted(): return lax.ppermute(block, 'vec', [(i, (i + shift) % 4) for i in range(4)])  52 us
    all_to_all x1, blocking collectives, all_terms(): return lax.all_to_all(copies, ('rows', 'vec'), 0, 0, tiled=True)  18.8 us
    pallas_call x2, Pallas kernels, push(): pl.pallas_call(tangent_kernel, grid=(count,), in_specs=[SMEM, pl.BlockSpe...  15.8 us
    ppermute x9, starting transfers between devices, shifted(): return lax.ppermute(block, 'vec', [(i, (i + shift) % 4) for i in range(4)])  15.4 us
    ppermute x2, starting transfers between devices, neighbours(): below = lax.ppermute(first, 'rows', backward)  11 us
    ppermute x1, starting transfers between devices, opposite(): one = lax.ppermute(blocks[3], 'vec', [(0, 1), (1, 2), (2, 3)])  10.2 us
    ppermute x2, waiting for transfers between devices, neighbours(): above = lax.ppermute(last, 'rows', forward)  5.86 us
    ppermute x1, starting transfers between devices, opposite(): two = lax.ppermute(blocks[0], 'vec', [(0, 2), (1, 3)])  4.58 us
  transfers between devices with their start and end apart: 16, of which 6 were waited for; matrix products, arithmetic and copies ran while one was open for 2% of the time, Pallas kernels for 14%

profile of v3, /device:TPU:0, one launch (start us, length us, event | category | flops | bytes accessed | tf_op | source)
XLA Modules:
  0.0 157.2 jit_solution(6053237850157201277)
XLA Ops:
  3.5 5.8 %collective-permute-start = (f32[4,2,4,4096]{3,2,1,0:T(4,128)S(1)}, f32[4,2,4,4096]{3,2,1,0:T(4,128)S(1)}, u32[]{:S(2)}, u32[]{:S(2)}) collective-permute-start(f32[4,2,4,4096]{3,2,1,0:T(4,128)S(1)} %get-tuple-element.96), channel_id=1, source_target_pairs={{4,0},{8,4},{12,8},{16,12},{20,16},{24,20},{28,24},{32,28},{36,32}... | collective-permute-start | bytes 1572872 | tf_op jit(solution)/shard_map/ppermute | solution.py:34
  9.4 3.3 %fusion = (f32[6,2,4,4096]{3,2,1,0:T(4,128)}, f32[6,2,4,4096]{3,2,1,0:T(4,128)}) fusion(f32[8,2,16,4096]{3,2,1,0:T(8,128)} %u_ref.3), kind=kLoop, calls=%fused_computation.7 | loop fusion | bytes 3145728 | tf_op jit(solution)/shard_map/slice | solution.py:26
  12.7 3.5 %collective-permute-done.1.above_ref = f32[4,2,4,4096]{3,2,1,0:T(4,128)S(1)} collective-permute-done((f32[4,2,4,4096]{3,2,1,0:T(4,128)S(1)}, f32[4,2,4,4096]{3,2,1,0:T(4,128)S(1)}, u32[]{:S(2)}, u32[]{:S(2)}) %collective-permute-start.1) | collective-permute-done | bytes 524320 | tf_op jit(solution)/shard_map/ppermute | solution.py:33
  16.1 5.1 %collective-permute-start.2 = (f32[6,2,4,4096]{3,2,1,0:T(4,128)}, f32[6,2,4,4096]{3,2,1,0:T(4,128)S(1)}, u32[]{:S(2)}, u32[]{:S(2)}) collective-permute-start(f32[6,2,4,4096]{3,2,1,0:T(4,128)} %get-tuple-element.51), channel_id=1, source_target_pairs={{4,0},{8,4},{12,8},{16,12},{20,16},{24,20},{28,24},{32,28},{36,32}... | collective-permute-start | bytes 2359304 | tf_op jit(solution)/shard_map/ppermute | solution.py:34
  21.3 2.2 %shard_map.58 = (f32[3,2,24,4096]{3,2,1,0:T(8,128)S(1)}, f32[2,16,4096]{2,1,0:T(8,128)}) custom-call(f32[2,16,4096]{2,1,0:T(8,128)S(1)} %copy-done, f32[2,16,4096]{2,1,0:T(8,128)S(1)} %copy-done.1, f32[4,2,4,4096]{3,2,1,0:T(4,128)S(1)} %collective-permute-done.below_ref, f32[4,2,4,4096]{3,2,1,0:T(4,128)S(1)} %collective-permute-done.1.above_ref), custom_call_target="tpu_custom_call" | custom-call | tf_op jit(solution)/shard_map/pallas_call | solution.py:328
  23.5 4.5 %shard_map.59 = (f32[2,8,4096]{2,1,0:T(8,128)S(1)}, f32[2,8,4096]{2,1,0:T(8,128)S(1)}, f32[2,8,4096]{2,1,0:T(8,128)S(1)}, f32[2,8,4096]{2,1,0:T(8,128)S(1)}) custom-call(s32[1]{0:T(128)} %bitcast.2.me_ref.refs_0_, f32[8,2,16,4096]{3,2,1,0:T(8,128)} %u_ref.3, f32[4,2,4,4096]{3,2,1,0:T(4,128)S(1)} %collective-permute-done.below_ref, ...), custom_call_target="tpu_custom_call" | custom-call | flops 60000000 | bytes 12000000 | tf_op jit(solution)/shard_map/pallas_call | solution.py:86
  28.0 1.6 %collective-permute-start.4 = (f32[2,8,4096]{2,1,0:T(8,128)S(1)}, f32[2,8,4096]{2,1,0:T(8,128)S(1)}, u32[]{:S(2)}, u32[]{:S(2)}) collective-permute-start(f32[2,8,4096]{2,1,0:T(8,128)S(1)} %get-tuple-element.55), channel_id=1, source_target_pairs={{0,1},{1,2},{2,3},{3,0},{4,5},{5,6},{6,7},{7,4},{8,9},{9,10},{10,1... | collective-permute-start | bytes 786440 | tf_op jit(solution)/shard_map/ppermute | solution.py:296
  29.6 2.9 %collective-permute-start.5 = (f32[2,8,4096]{2,1,0:T(8,128)S(1)}, f32[2,8,4096]{2,1,0:T(8,128)S(1)}, u32[]{:S(2)}, u32[]{:S(2)}) collective-permute-start(f32[2,8,4096]{2,1,0:T(8,128)S(1)} %get-tuple-element.56), channel_id=1, source_target_pairs={{0,2},{1,3},{2,0},{3,1},{4,6},{5,7},{6,4},{7,5},{8,10},{9,11},{10,... | collective-permute-start | bytes 786440 | tf_op jit(solution)/shard_map/ppermute | solution.py:296
  33.9 2.4 %collective-permute-done.3.above_ref = f32[6,2,4,4096]{3,2,1,0:T(4,128)} collective-permute-done((f32[6,2,4,4096]{3,2,1,0:T(4,128)}, f32[6,2,4,4096]{3,2,1,0:T(4,128)}, u32[]{:S(2)}, u32[]{:S(2)}) %collective-permute-start.3) | collective-permute-done | bytes 786464 | tf_op jit(solution)/shard_map/ppermute | solution.py:33
  36.3 11.3 %shard_map.60 = (f32[6,8,4096]{2,1,0:T(8,128)S(1)}, f32[6,8,4096]{2,1,0:T(8,128)S(1)}, f32[6,8,4096]{2,1,0:T(8,128)S(1)}, f32[6,8,4096]{2,1,0:T(8,128)S(1)}) custom-call(s32[1]{0:T(128)} %bitcast.2.me_ref.refs_0_, f32[8,2,16,4096]{3,2,1,0:T(8,128)} %u_ref.3, f32[6,2,4,4096]{3,2,1,0:T(4,128)S(1)} %collective-permute-done.2.below_ref, ...), custom_call_target="tpu_custom_call" | custom-call | flops 180000000 | bytes 36000000 | tf_op jit(solution)/shard_map/pallas_call | solution.py:86
  47.8 1.7 %collective-permute-start.7 = (f32[6,8,4096]{2,1,0:T(8,128)S(1)}, f32[6,8,4096]{2,1,0:T(8,128)S(1)}, u32[]{:S(2)}, u32[]{:S(2)}) collective-permute-start(f32[6,8,4096]{2,1,0:T(8,128)S(1)} %get-tuple-element.69), channel_id=1, source_target_pairs={{0,1},{1,2},{2,3},{3,0},{4,5},{5,6},{6,7},{7,4},{8,9},{9,10},{10,1... | collective-permute-start | bytes 2359304 | tf_op jit(solution)/shard_map/ppermute | solution.py:296
  49.4 2.9 %collective-permute-start.8 = (f32[6,8,4096]{2,1,0:T(8,128)S(1)}, f32[6,8,4096]{2,1,0:T(8,128)S(1)}, u32[]{:S(2)}, u32[]{:S(2)}) collective-permute-start(f32[6,8,4096]{2,1,0:T(8,128)S(1)} %get-tuple-element.70), channel_id=1, source_target_pairs={{0,2},{1,3},{2,0},{3,1},{4,6},{5,7},{6,4},{7,5},{8,10},{9,11},{10,... | collective-permute-start | bytes 2359304 | tf_op jit(solution)/shard_map/ppermute | solution.py:296
  53.9 15.1 %collective-permute-done.7.refs_6_ = f32[6,8,4096]{2,1,0:T(8,128)S(1)} collective-permute-done((f32[6,8,4096]{2,1,0:T(8,128)S(1)}, f32[6,8,4096]{2,1,0:T(8,128)S(1)}, u32[]{:S(2)}, u32[]{:S(2)}) %collective-permute-start.7) | collective-permute-done | bytes 786464 | tf_op jit(solution)/shard_map/ppermute | solution.py:296
  69.1 10.2 %collective-permute-start.10 = (f32[8,8,2048]{2,1,0:T(8,128)S(1)}, f32[8,8,2048]{2,1,0:T(8,128)S(1)}, u32[]{:S(2)}, u32[]{:S(2)}) collective-permute-start(f32[8,8,2048]{2,1,0:T(8,128)S(1)} %pad_maximum_fusion.6), channel_id=1, source_target_pairs={{0,1},{1,2},{2,3},{4,5},{5,6},{6,7},{8,9},{9,10},{10,11},{12,13},{... | collective-permute-start | bytes 1572872 | tf_op jit(solution)/shard_map/ppermute | solution.py:305
  79.2 4.6 %collective-permute-start.11 = (f32[8,8,2048]{2,1,0:T(8,128)S(1)}, f32[8,8,2048]{2,1,0:T(8,128)S(1)}, u32[]{:S(2)}, u32[]{:S(2)}) collective-permute-start(f32[8,8,2048]{2,1,0:T(8,128)S(1)} %pad_maximum_fusion.3), channel_id=1, source_target_pairs={{0,2},{1,3},{4,6},{5,7},{8,10},{9,11},{12,14},{13,15},{16,18},{17,... | collective-permute-start | bytes 1572872 | tf_op jit(solution)/shard_map/ppermute | solution.py:306
  85.2 4.9 %collective-permute-done.9.refs_8_ = f32[6,8,4096]{2,1,0:T(8,128)S(1)} collective-permute-done((f32[6,8,4096]{2,1,0:T(8,128)S(1)}, f32[6,8,4096]{2,1,0:T(8,128)S(1)}, u32[]{:S(2)}, u32[]{:S(2)}) %collective-permute-start.9) | collective-permute-done | bytes 786464 | tf_op jit(solution)/shard_map/ppermute | solution.py:296
  90.1 1.9 %shard_map.61 = (bf16[256,4096]{1,0:T(8,128)(2,1)S(1)}, bf16[256,4096]{1,0:T(8,128)(2,1)S(1)}, f32[1024,128]{1,0:T(8,128)S(1)}) custom-call(s32[1]{0:T(128)} %bitcast.2.me_ref.refs_0_, f32[2,8,4096]{2,1,0:T(8,128)S(1)} %get-tuple-element.64.refs_1_, f32[2,8,4096]{2,1,0:T(8,128)S(1)} %collective-permute-done.4.refs_2_, ...), custom_call_target="tpu_custom_call" | custom-call | tf_op jit(solution)/shard_map/pallas_call | solution.py:155
  91.9 18.8 %all_to_all.12 = f32[128,8,128]{2,1,0:T(8,128)S(1)} all-to-all(f32[128,8,128]{2,1,0:T(8,128)S(1)} %bitcast.10), channel_id=1, replica_groups=mesh['rows'=32,'vec'=4] {'rows','vec'}, dimensions={0} | all-to-all | bytes 1048576 | tf_op jit(solution)/shard_map/all_to_all | solution.py:312
  110.7 3.7 %shard_map.62 = (f32[1,32]{1,0:T(1,128)}, bf16[256,256]{1,0:T(8,128)(2,1)S(1)}, bf16[256,256]{1,0:T(8,128)(2,1)S(1)}) custom-call(f32[1024,128]{1,0:T(8,128)S(1)} %bitcast.7), custom_call_target="tpu_custom_call" | custom-call | tf_op jit(solution)/shard_map/pallas_call | solution.py:204
  114.4 2.8 %shard_map.64 = (f32[8,8,4096]{2,1,0:T(8,128)S(1)}, f32[8,8,2048]{2,1,0:T(8,128)S(1)}, f32[8,8,4096]{2,1,0:T(8,128)S(1)}) custom-call(s32[1]{0:T(128)} %bitcast.2.me_ref.refs_0_, bf16[256,256]{1,0:T(8,128)(2,1)S(1)} %get-tuple-element.79.w_high, bf16[256,256]{1,0:T(8,128)(2,1)S(1)} %get-tuple-element.80.w_low, ...), custom_call_target="tpu_custom_call" | custom-call | tf_op jit(solution)/shard_map/pallas_call | solution.py:230
  117.9 2.6 %collective-permute-start.15 = (f32[8,8,4096]{2,1,0:T(8,128)S(1)}, f32[8,8,4096]{2,1,0:T(8,128)S(1)}, u32[]{:S(2)}, u32[]{:S(2)}) collective-permute-start(f32[8,8,4096]{2,1,0:T(8,128)S(1)} %get-tuple-element.91), channel_id=1, source_target_pairs={{0,3},{1,0},{2,1},{3,2},{4,7},{5,4},{6,5},{7,6},{8,11},{9,8},{10,9... | collective-permute-start | bytes 3145736 | tf_op jit(solution)/shard_map/ppermute | solution.py:296
  120.8 2.1 %shard_map.63 = (f32[8,8,4096]{2,1,0:T(8,128)S(1)}, f32[8,8,2048]{2,1,0:T(8,128)S(1)}) custom-call(s32[1]{0:T(128)} %bitcast.2.me_ref.refs_0_, bf16[256,256]{1,0:T(8,128)(2,1)S(1)} %get-tuple-element.79.w_high, bf16[256,256]{1,0:T(8,128)(2,1)S(1)} %get-tuple-element.80.w_low, bf16[256,4096]{1,0:T(8,128)(2,1)S(1)} %get-tuple-element.81.high_ref, ...), custom_call_target="tpu_custom_call" | custom-call | tf_op jit(solution)/shard_map/pallas_call | solution.py:258
  122.9 31.6 %collective-permute-done.14.across_ref = f32[8,8,2048]{2,1,0:T(8,128)S(1)} collective-permute-done((f32[8,8,2048]{2,1,0:T(8,128)S(1)}, f32[8,8,2048]{2,1,0:T(8,128)S(1)}, u32[]{:S(2)}, u32[]{:S(2)}) %collective-permute-start.14) | collective-permute-done | bytes 524320 | tf_op jit(solution)/shard_map/ppermute | solution.py:296
  154.8 2.4 %shard_map.65 = f32[8,4,8,4096]{3,2,1,0:T(8,128)} custom-call(s32[1]{0:T(128)} %bitcast.2.me_ref.refs_0_, f32[8,8,4096]{2,1,0:T(8,128)S(1)} %get-tuple-element.87.own_ref, f32[8,8,2048]{2,1,0:T(8,128)S(1)} %get-tuple-element.88.far_ref, f32[8,8,4096]{2,1,0:T(8,128)S(1)} %collective-permute-done.13.before_ref, ...), custom_call_target="tpu_custom_call" | custom-call | tf_op jit(solution)/shard_map/pallas_call | solution.py:284
  (36 shorter events, 8.6 us)
Async XLA Ops:
  0.6 20.7 %copy-start = (f32[2,16,4096]{2,1,0:T(8,128)S(1)}, f32[2,16,4096]{2,1,0:T(8,128)}, u32[]{:S(2)}) copy-start(f32[2,16,4096]{2,1,0:T(8,128)} %z_ref.1) | copy-start | bytes 1572868
  0.6 20.7 %copy-start.1 = (f32[2,16,4096]{2,1,0:T(8,128)S(1)}, f32[2,16,4096]{2,1,0:T(8,128)}, u32[]{:S(2)}) copy-start(f32[2,16,4096]{2,1,0:T(8,128)} %c_ref.1) | copy-start | bytes 1572868
  3.5 12.7 %collective-permute-start.1 = (f32[4,2,4,4096]{3,2,1,0:T(4,128)S(1)}, f32[4,2,4,4096]{3,2,1,0:T(4,128)S(1)}, u32[]{:S(2)}, u32[]{:S(2)}) collective-permute-start(f32[4,2,4,4096]{3,2,1,0:T(4,128)S(1)} %get-tuple-element.95), channel_id=1, source_target_pairs={{0,4},{4,8},{8,12},{12,16},{16,20},{20,24},{24,28},{28,32},{32,36}... | collective-permute-start | bytes 1572872 | tf_op jit(solution)/shard_map/ppermute | solution.py:33
  3.5 12.6 %collective-permute-start = (f32[4,2,4,4096]{3,2,1,0:T(4,128)S(1)}, f32[4,2,4,4096]{3,2,1,0:T(4,128)S(1)}, u32[]{:S(2)}, u32[]{:S(2)}) collective-permute-start(f32[4,2,4,4096]{3,2,1,0:T(4,128)S(1)} %get-tuple-element.96), channel_id=1, source_target_pairs={{4,0},{8,4},{12,8},{16,12},{20,16},{24,20},{28,24},{32,28},{36,32}... | collective-permute-start | bytes 1572872 | tf_op jit(solution)/shard_map/ppermute | solution.py:34
  16.1 17.8 %collective-permute-start.2 = (f32[6,2,4,4096]{3,2,1,0:T(4,128)}, f32[6,2,4,4096]{3,2,1,0:T(4,128)S(1)}, u32[]{:S(2)}, u32[]{:S(2)}) collective-permute-start(f32[6,2,4,4096]{3,2,1,0:T(4,128)} %get-tuple-element.51), channel_id=1, source_target_pairs={{4,0},{8,4},{12,8},{16,12},{20,16},{24,20},{28,24},{32,28},{36,32}... | collective-permute-start | bytes 2359304 | tf_op jit(solution)/shard_map/ppermute | solution.py:34
  21.3 15.1 %collective-permute-start.3 = (f32[6,2,4,4096]{3,2,1,0:T(4,128)}, f32[6,2,4,4096]{3,2,1,0:T(4,128)}, u32[]{:S(2)}, u32[]{:S(2)}) collective-permute-start(f32[6,2,4,4096]{3,2,1,0:T(4,128)} %get-tuple-element.52), channel_id=1, source_target_pairs={{0,4},{4,8},{8,12},{12,16},{16,20},{20,24},{24,28},{28,32},{32,36}... | collective-permute-start | bytes 2359304 | tf_op jit(solution)/shard_map/ppermute | solution.py:33
  28.0 19.7 %collective-permute-start.4 = (f32[2,8,4096]{2,1,0:T(8,128)S(1)}, f32[2,8,4096]{2,1,0:T(8,128)S(1)}, u32[]{:S(2)}, u32[]{:S(2)}) collective-permute-start(f32[2,8,4096]{2,1,0:T(8,128)S(1)} %get-tuple-element.55), channel_id=1, source_target_pairs={{0,1},{1,2},{2,3},{3,0},{4,5},{5,6},{6,7},{7,4},{8,9},{9,10},{10,1... | collective-permute-start | bytes 786440 | tf_op jit(solution)/shard_map/ppermute | solution.py:296
  29.6 18.1 %collective-permute-start.5 = (f32[2,8,4096]{2,1,0:T(8,128)S(1)}, f32[2,8,4096]{2,1,0:T(8,128)S(1)}, u32[]{:S(2)}, u32[]{:S(2)}) collective-permute-start(f32[2,8,4096]{2,1,0:T(8,128)S(1)} %get-tuple-element.56), channel_id=1, source_target_pairs={{0,2},{1,3},{2,0},{3,1},{4,6},{5,7},{6,4},{7,5},{8,10},{9,11},{10,... | collective-permute-start | bytes 786440 | tf_op jit(solution)/shard_map/ppermute | solution.py:296
  32.5 15.2 %collective-permute-start.6 = (f32[2,8,4096]{2,1,0:T(8,128)S(1)}, f32[2,8,4096]{2,1,0:T(8,128)S(1)}, u32[]{:S(2)}, u32[]{:S(2)}) collective-permute-start(f32[2,8,4096]{2,1,0:T(8,128)S(1)} %get-tuple-element.57), channel_id=1, source_target_pairs={{0,3},{1,0},{2,1},{3,2},{4,7},{5,4},{6,5},{7,6},{8,11},{9,8},{10,9... | collective-permute-start | bytes 786440 | tf_op jit(solution)/shard_map/ppermute | solution.py:296
  47.8 21.3 %collective-permute-start.7 = (f32[6,8,4096]{2,1,0:T(8,128)S(1)}, f32[6,8,4096]{2,1,0:T(8,128)S(1)}, u32[]{:S(2)}, u32[]{:S(2)}) collective-permute-start(f32[6,8,4096]{2,1,0:T(8,128)S(1)} %get-tuple-element.69), channel_id=1, source_target_pairs={{0,1},{1,2},{2,3},{3,0},{4,5},{5,6},{6,7},{7,4},{8,9},{9,10},{10,1... | collective-permute-start | bytes 2359304 | tf_op jit(solution)/shard_map/ppermute | solution.py:296
  49.4 35.7 %collective-permute-start.8 = (f32[6,8,4096]{2,1,0:T(8,128)S(1)}, f32[6,8,4096]{2,1,0:T(8,128)S(1)}, u32[]{:S(2)}, u32[]{:S(2)}) collective-permute-start(f32[6,8,4096]{2,1,0:T(8,128)S(1)} %get-tuple-element.70), channel_id=1, source_target_pairs={{0,2},{1,3},{2,0},{3,1},{4,6},{5,7},{6,4},{7,5},{8,10},{9,11},{10,... | collective-permute-start | bytes 2359304 | tf_op jit(solution)/shard_map/ppermute | solution.py:296
  52.3 37.7 %collective-permute-start.9 = (f32[6,8,4096]{2,1,0:T(8,128)S(1)}, f32[6,8,4096]{2,1,0:T(8,128)S(1)}, u32[]{:S(2)}, u32[]{:S(2)}) collective-permute-start(f32[6,8,4096]{2,1,0:T(8,128)S(1)} %get-tuple-element.71), channel_id=1, source_target_pairs={{0,3},{1,0},{2,1},{3,2},{4,7},{5,4},{6,5},{7,6},{8,11},{9,8},{10,9... | collective-permute-start | bytes 2359304 | tf_op jit(solution)/shard_map/ppermute | solution.py:296
  69.1 41.7 %collective-permute-start.10 = (f32[8,8,2048]{2,1,0:T(8,128)S(1)}, f32[8,8,2048]{2,1,0:T(8,128)S(1)}, u32[]{:S(2)}, u32[]{:S(2)}) collective-permute-start(f32[8,8,2048]{2,1,0:T(8,128)S(1)} %pad_maximum_fusion.6), channel_id=1, source_target_pairs={{0,1},{1,2},{2,3},{4,5},{5,6},{6,7},{8,9},{9,10},{10,11},{12,13},{... | collective-permute-start | bytes 1572872 | tf_op jit(solution)/shard_map/ppermute | solution.py:305
  79.2 31.5 %collective-permute-start.11 = (f32[8,8,2048]{2,1,0:T(8,128)S(1)}, f32[8,8,2048]{2,1,0:T(8,128)S(1)}, u32[]{:S(2)}, u32[]{:S(2)}) collective-permute-start(f32[8,8,2048]{2,1,0:T(8,128)S(1)} %pad_maximum_fusion.3), channel_id=1, source_target_pairs={{0,2},{1,3},{4,6},{5,7},{8,10},{9,11},{12,14},{13,15},{16,18},{17,... | collective-permute-start | bytes 1572872 | tf_op jit(solution)/shard_map/ppermute | solution.py:306
  83.8 26.9 %collective-permute-start.12 = (f32[8,8,2048]{2,1,0:T(8,128)S(1)}, f32[8,8,2048]{2,1,0:T(8,128)S(1)}, u32[]{:S(2)}, u32[]{:S(2)}) collective-permute-start(f32[8,8,2048]{2,1,0:T(8,128)S(1)} %pad_maximum_fusion.4), channel_id=1, source_target_pairs={{0,3},{4,7},{8,11},{12,15},{16,19},{20,23},{24,27},{28,31},{32,35}... | collective-permute-start | bytes 1572872 | tf_op jit(solution)/shard_map/ppermute | solution.py:307
  117.2 37.6 %collective-permute-start.13 = (f32[8,8,4096]{2,1,0:T(8,128)S(1)}, f32[8,8,4096]{2,1,0:T(8,128)S(1)}, u32[]{:S(2)}, u32[]{:S(2)}) collective-permute-start(f32[8,8,4096]{2,1,0:T(8,128)S(1)} %get-tuple-element.89), channel_id=1, source_target_pairs={{0,1},{1,2},{2,3},{3,0},{4,5},{5,6},{6,7},{7,4},{8,9},{9,10},{10,1... | collective-permute-start | bytes 3145736 | tf_op jit(solution)/shard_map/ppermute | solution.py:296
  117.9 36.9 %collective-permute-start.15 = (f32[8,8,4096]{2,1,0:T(8,128)S(1)}, f32[8,8,4096]{2,1,0:T(8,128)S(1)}, u32[]{:S(2)}, u32[]{:S(2)}) collective-permute-start(f32[8,8,4096]{2,1,0:T(8,128)S(1)} %get-tuple-element.91), channel_id=1, source_target_pairs={{0,3},{1,0},{2,1},{3,2},{4,7},{5,4},{6,5},{7,6},{8,11},{9,8},{10,9... | collective-permute-start | bytes 3145736 | tf_op jit(solution)/shard_map/ppermute | solution.py:296
  120.5 33.9 %collective-permute-start.14 = (f32[8,8,2048]{2,1,0:T(8,128)S(1)}, f32[8,8,2048]{2,1,0:T(8,128)S(1)}, u32[]{:S(2)}, u32[]{:S(2)}) collective-permute-start(f32[8,8,2048]{2,1,0:T(8,128)S(1)} %get-tuple-element.90), channel_id=1, source_target_pairs={{0,2},{1,3},{2,0},{3,1},{4,6},{5,7},{6,4},{7,5},{8,10},{9,11},{10,... | collective-permute-start | bytes 1572872 | tf_op jit(solution)/shard_map/ppermute | solution.py:296

commit v4 on v3

--- a/solution.py
+++ b/solution.py
@@ -15,6 +15,7 @@
 HIGHEST = lax.Precision.HIGHEST
 FULL = pl.BlockSpec(memory_space=pltpu.VMEM)
 SMEM = pl.BlockSpec(memory_space=pltpu.SMEM)
+HBM = pl.BlockSpec(memory_space=pltpu.HBM)
 
 
 def params():
@@ -165,7 +166,19 @@
     )(me, *pieces)
 
 
-def factor_kernel(scale, terms_ref, growth_ref, high_ref, low_ref):
+def factor_kernel(
+    scale,
+    me_ref,
+    terms_ref,
+    high_ref,
+    low_ref,
+    growth_ref,
+    w_high,
+    w_low,
+    next_ref,
+    across_ref,
+    previous_ref,
+):
     row = lax.broadcasted_iota(jnp.int32, (NV, 2 * NV), 0)
     column = lax.broadcasted_iota(jnp.int32, (NV, 2 * NV), 1)
     spread = jnp.where(row == column, 1.0, 0.0)
@@ -196,28 +209,8 @@
     tall = jnp.broadcast_to(wide[:, None, :], (NV, 8, 8 * NV)).reshape(8 * NV, 8 * NV)
     weights = jnp.where(same_row(tall.shape, 8), tall, 0.0)
     high = weights.astype(jnp.bfloat16)
-    high_ref[...] = high
-    low_ref[...] = (weights - high.astype(jnp.float32)).astype(jnp.bfloat16)
-
-
-def factorise(terms, scale):
-    return pl.pallas_call(
-        lambda *refs: factor_kernel(scale, *refs),
-        in_specs=[FULL],
-        out_specs=[FULL] * 3,
-        out_shape=[jax.ShapeDtypeStruct((1, NV), jnp.float32)]
-        + [jax.ShapeDtypeStruct((8 * NV, 8 * NV), jnp.bfloat16)] * 2,
-        compiler_params=params(),
-    )(terms)
-
-
-def product(w_high, w_low, high, low):
-    value = jnp.dot(w_high, high, preferred_element_type=jnp.float32)
-    value += jnp.dot(w_high, low, preferred_element_type=jnp.float32)
-    return value + jnp.dot(w_low, high, preferred_element_type=jnp.float32)
-
-
-def send_kernel(me_ref, w_high, w_low, high_ref, low_ref, next_ref, across_ref, previous_ref):
+    w_high[...] = high
+    w_low[...] = (weights - high.astype(jnp.float32)).astype(jnp.bfloat16)
     for shift, out in ((1, next_ref), (2, across_ref), (3, previous_ref)):
         rows = pl.ds(pl.multiple_of(lax.rem(me_ref[0] + shift, 4) * 64, 64), 64)
         skip = high_ref.shape[1] - out.shape[2]
@@ -225,22 +218,30 @@
         out[...] = value.reshape(out.shape)
 
 
-def send_parts(me, w_high, w_low, high, low):
+def factorise(me, terms, high, low, scale):
     columns = high.shape[-1]
     return pl.pallas_call(
-        send_kernel,
-        in_specs=[SMEM] + [FULL] * 4,
-        out_specs=[FULL] * 3,
-        out_shape=[
+        lambda *refs: factor_kernel(scale, *refs),
+        in_specs=[SMEM] + [FULL] * 3,
+        out_specs=[FULL] * 6,
+        out_shape=[jax.ShapeDtypeStruct((1, NV), jnp.float32)]
+        + [jax.ShapeDtypeStruct((8 * NV, 8 * NV), jnp.bfloat16)] * 2
+        + [
             jax.ShapeDtypeStruct((8, 8, width), jnp.float32)
             for width in (columns, columns - NEAR, columns)
         ],
         compiler_params=params(),
-    )(me, w_high, w_low, high, low)
+    )(me, terms, high, low)
+
+
+def product(w_high, w_low, high, low):
+    value = jnp.dot(w_high, high, preferred_element_type=jnp.float32)
+    value += jnp.dot(w_high, low, preferred_element_type=jnp.float32)
+    return value + jnp.dot(w_low, high, preferred_element_type=jnp.float32)
 
 
 def own_kernel(me_ref, w_high, w_low, high_ref, low_ref, *refs):
-    pieces, (own_ref, far_ref, far_high, far_low) = refs[:-4], refs[-4:]
+    pieces, (out, own_ref, far_ref, far_high, far_low, sems) = refs[:-6], refs[-6:]
     me = me_ref[0]
     for back, piece in enumerate(pieces):
         start = pl.multiple_of(lax.rem(me + 4 - back, 4) * 64, 64)
@@ -250,7 +251,15 @@
     rows = pl.ds(pl.multiple_of(me * 64, 64), 64)
     own_high, own_low = w_high[rows, :], w_low[rows, :]
     own_ref[...] = product(own_high, own_low, high_ref[...], low_ref[...]).reshape(own_ref.shape)
+    own_copy = pltpu.make_async_copy(own_ref, out.at[:, me], sems.at[0])
+    own_copy.start()
     far_ref[...] = product(own_high, own_low, far_high[...], far_low[...]).reshape(far_ref.shape)
+    far_copy = pltpu.make_async_copy(
+        far_ref, out.at[:, lax.rem(me + 2, 4), :, pl.ds(0, NEAR)], sems.at[1]
+    )
+    far_copy.start()
+    own_copy.wait()
+    far_copy.wait()
 
 
 def own_parts(me, w_high, w_low, high, low, pieces):
@@ -258,38 +267,44 @@
     return pl.pallas_call(
         own_kernel,
         in_specs=[SMEM] + [FULL] * (4 + len(pieces)),
-        out_specs=[FULL] * 2,
-        out_shape=[
-            jax.ShapeDtypeStruct((8, 8, width), jnp.float32) for width in (columns, NEAR)
-        ],
-        scratch_shapes=[pltpu.VMEM((8 * NV, NEAR), jnp.bfloat16)] * 2,
+        out_specs=HBM,
+        out_shape=jax.ShapeDtypeStruct((8, 4, 8, columns), jnp.float32),
+        scratch_shapes=[
+            pltpu.VMEM((8, 8, columns), jnp.float32),
+            pltpu.VMEM((8, 8, NEAR), jnp.float32),
+            pltpu.VMEM((8 * NV, NEAR), jnp.bfloat16),
+            pltpu.VMEM((8 * NV, NEAR), jnp.bfloat16),
+            pltpu.SemaphoreType.DMA((2,)),
+        ],
         compiler_params=params(),
     )(me, w_high, w_low, high, low, *pieces)
 
 
-def assemble_kernel(me_ref, own_ref, far_ref, before_ref, across_ref, after_ref, out):
+def assemble_kernel(me_ref, own_ref, before_ref, across_ref, after_ref, out, sems):
     me = me_ref[0]
-    opposite_slab = lax.rem(me + 2, 4)
-    out[:, me] = own_ref[...]
-    out[:, opposite_slab, :, :NEAR] = far_ref[...]
-    out[:, opposite_slab, :, NEAR:] = across_ref[...]
-    out[:, lax.rem(me + 3, 4)] = before_ref[...]
-    out[:, lax.rem(me + 1, 4)] = after_ref[...]
+    width = across_ref.shape[2]
+    far = out.at[:, lax.rem(me + 2, 4), :, pl.ds(out.shape[3] - width, width)]
+    copies = [
+        pltpu.make_async_copy(before_ref, out.at[:, lax.rem(me + 3, 4)], sems.at[0]),
+        pltpu.make_async_copy(after_ref, out.at[:, lax.rem(me + 1, 4)], sems.at[1]),
+        pltpu.make_async_copy(across_ref, far, sems.at[2]),
+    ]
+    for copy in copies:
+        copy.start()
+    for copy in copies:
+        copy.wait()
 
 
 def assemble(me, own, before, across, after):
-    parts = (*own, before, across, after)
-    count, rows, columns = before.shape
-    step = 2
     return pl.pallas_call(
         assemble_kernel,
-        grid=(count // step,),
-        in_specs=[SMEM]
-        + [pl.BlockSpec((step, rows, part.shape[2]), lambda i: (i, 0, 0)) for part in parts],
-        out_specs=pl.BlockSpec((step, 4, rows, columns), lambda i: (i, 0, 0, 0)),
-        out_shape=jax.ShapeDtypeStruct((count, 4, rows, columns), jnp.float32),
-        compiler_params=params(),
-    )(me, *parts)
+        in_specs=[SMEM, HBM] + [pl.BlockSpec(memory_space=pl.ANY)] * 3,
+        out_specs=HBM,
+        out_shape=jax.ShapeDtypeStruct(own.shape, own.dtype),
+        scratch_shapes=[pltpu.SemaphoreType.DMA((3,))],
+        input_output_aliases={1: 0},
+        compiler_params=params(),
+    )(me, own, before, across, after)
 
 
 def shifted(block, shift):
@@ -320,9 +335,10 @@
     me = lax.axis_index("vec").astype(jnp.int32).reshape(1)
     rows, columns = lattice_state.shape[1:]
     scale = math.sqrt(2.0 * rows * lax.axis_size("rows") * columns)
-    fields = jnp.stack([lattice_state, constant_field])
-    first = jnp.concatenate([fields, tangents[: CHUNKS[0]]], axis=0)
-    ahead = neighbours(*edges(first))
+    sources = (lattice_state[None], constant_field[None], tangents[: CHUNKS[0]])
+    ahead = neighbours(
+        *(jnp.concatenate(parts, axis=0) for parts in zip(*(edges(part) for part in sources)))
+    )
     ahead, rest = lax.optimization_barrier((ahead, edges(tangents[CHUNKS[0] :])))
     halos = [ahead, neighbours(*rest)]
     twice, next_state = pl.pallas_call(
@@ -353,8 +369,7 @@
     far = opposite(slabs)
     high, low, copies = inner_products(me, pieces, len(CHUNKS))
     terms, far = lax.optimization_barrier((all_terms(copies), far))
-    growth, w_high, w_low = factorise(terms, scale)
-    following, across, previous = send_parts(me, w_high, w_low, high, low)
+    growth, w_high, w_low, following, across, previous = factorise(me, terms, high, low, scale)
     across = shifted(across, 2)
     before = shifted(following, 1)
     after = shifted(previous, 3)

time: 159 us -> 158 us (level)
  starting transfers between devices: 42.5 us -> 39.2 us
  blocking collectives: 18.8 us -> 20.8 us
  waiting for transfers between devices: 57.8 us -> 59.5 us
    ppermute x2, starting transfers between devices: 11 us -> 5.83 us  [neighbours(): below = lax.ppermute(first, 'rows', backward)]
    ppermute x2, waiting for transfers between devices: 0.01 us -> 3.16 us  [neighbours(): below = lax.ppermute(first, 'rows', backward)]
    ppermute x9, waiting for transfers between devices: 52 us -> 49 us  [shifted(): return lax.ppermute(block, 'vec', [(i, (i + shift) % 4) for i in range(4)])]
    all_to_all x1, blocking collectives: 18.8 us -> 20.8 us  [all_terms(): return lax.all_to_all(copies, ('rows', 'vec'), 0, 0, tiled=True)]
    ppermute x9, starting transfers between devices: 15.4 us -> 17 us  [shifted(): return lax.ppermute(block, 'vec', [(i, (i + shift) % 4) for i in range(4)])]
    pallas_call x3 -> x2, Pallas kernels: 8.93 us -> 7.77 us  [the longest x1 6.26 us: factorise(): pl.pallas_call(lambda *refs: factor_kernel(scale, *refs), in_specs=[SMEM]...]
where the time goes in v4:
time: 158 us
  waiting for transfers between devices  59.5 us (38%)
  starting transfers between devices  39.2 us (25%)
  Pallas kernels  30.5 us (19%)
  blocking collectives  20.8 us (13%)
  local copies, waits for them, and re-layouts  6.15 us (4%)
    ppermute x9, waiting for transfers between devices, shifted(): return lax.ppermute(block, 'vec', [(i, (i + shift) % 4) for i in range(4)])  49 us
    all_to_all x1, blocking collectives, all_terms(): return lax.all_to_all(copies, ('rows', 'vec'), 0, 0, tiled=True)  20.8 us
    ppermute x9, starting transfers between devices, shifted(): return lax.ppermute(block, 'vec', [(i, (i + shift) % 4) for i in range(4)])  17 us
    pallas_call x2, Pallas kernels, push(): pl.pallas_call(tangent_kernel, grid=(count,), in_specs=[SMEM, pl.BlockSpe...  15.8 us
    ppermute x1, starting transfers between devices, opposite(): one = lax.ppermute(blocks[3], 'vec', [(0, 1), (1, 2), (2, 3)])  9.53 us
    ppermute x2, waiting for transfers between devices, neighbours(): above = lax.ppermute(last, 'rows', forward)  7.33 us
    pallas_call x1, Pallas kernels, factorise(): pl.pallas_call(lambda *refs: factor_kernel(scale, *refs), in_specs=[SMEM]...  6.26 us
    ppermute x2, starting transfers between devices, neighbours(): below = lax.ppermute(first, 'rows', backward)  5.83 us
  transfers between devices with their start and end apart: 16, of which 6 were waited for; matrix products, arithmetic and copies ran while one was open for 2% of the time, Pallas kernels for 14%

profile of v4, /device:TPU:0, one launch (start us, length us, event | category | flops | bytes accessed | tf_op | source)
XLA Modules:
  0.0 157.6 jit_solution(8479481257215548875)
XLA Ops:
  3.5 5.8 %collective-permute-start = (f32[4,2,4,4096]{3,2,1,0:T(4,128)S(1)}, f32[4,2,4,4096]{3,2,1,0:T(4,128)S(1)}, u32[]{:S(2)}, u32[]{:S(2)}) collective-permute-start(f32[4,2,4,4096]{3,2,1,0:T(4,128)S(1)} %pad_maximum_fusion), channel_id=1, source_target_pairs={{4,0},{8,4},{12,8},{16,12},{20,16},{24,20},{28,24},{32,28},{36,32}... | collective-permute-start | bytes 1572872 | tf_op jit(solution)/shard_map/ppermute | solution.py:35
  9.5 3.3 %fusion = (f32[6,2,4,4096]{3,2,1,0:T(4,128)}, f32[6,2,4,4096]{3,2,1,0:T(4,128)}) fusion(f32[8,2,16,4096]{3,2,1,0:T(8,128)} %u_ref.3), kind=kLoop, calls=%fused_computation.6 | loop fusion | bytes 3145728 | tf_op jit(solution)/shard_map/slice | solution.py:27
  12.8 3.2 %collective-permute-done.below_ref = f32[4,2,4,4096]{3,2,1,0:T(4,128)S(1)} collective-permute-done((f32[4,2,4,4096]{3,2,1,0:T(4,128)S(1)}, f32[4,2,4,4096]{3,2,1,0:T(4,128)S(1)}, u32[]{:S(2)}, u32[]{:S(2)}) %collective-permute-start) | collective-permute-done | bytes 524320 | tf_op jit(solution)/shard_map/ppermute | solution.py:35
  16.0 5.4 %collective-permute-done.1.above_ref = f32[4,2,4,4096]{3,2,1,0:T(4,128)S(1)} collective-permute-done((f32[4,2,4,4096]{3,2,1,0:T(4,128)S(1)}, f32[4,2,4,4096]{3,2,1,0:T(4,128)S(1)}, u32[]{:S(2)}, u32[]{:S(2)}) %collective-permute-start.1) | collective-permute-done | bytes 524320 | tf_op jit(solution)/shard_map/ppermute | solution.py:34
  21.9 2.2 %shard_map.58 = (f32[3,2,24,4096]{3,2,1,0:T(8,128)S(1)}, f32[2,16,4096]{2,1,0:T(8,128)}) custom-call(f32[2,16,4096]{2,1,0:T(8,128)S(1)} %copy-done, f32[2,16,4096]{2,1,0:T(8,128)S(1)} %copy-done.1, f32[4,2,4,4096]{3,2,1,0:T(4,128)S(1)} %collective-permute-done.below_ref, f32[4,2,4,4096]{3,2,1,0:T(4,128)S(1)} %collective-permute-done.1.above_ref), custom_call_target="tpu_custom_call" | custom-call | tf_op jit(solution)/shard_map/pallas_call | solution.py:344
  24.1 4.5 %shard_map.59 = (f32[2,8,4096]{2,1,0:T(8,128)S(1)}, f32[2,8,4096]{2,1,0:T(8,128)S(1)}, f32[2,8,4096]{2,1,0:T(8,128)S(1)}, f32[2,8,4096]{2,1,0:T(8,128)S(1)}) custom-call(s32[1]{0:T(128)} %bitcast.2.me_ref.refs_0_, f32[8,2,16,4096]{3,2,1,0:T(8,128)} %u_ref.3, f32[4,2,4,4096]{3,2,1,0:T(4,128)S(1)} %collective-permute-done.below_ref, ...), custom_call_target="tpu_custom_call" | custom-call | flops 60000000 | bytes 12000000 | tf_op jit(solution)/shard_map/pallas_call | solution.py:87
  28.6 1.6 %collective-permute-start.4 = (f32[2,8,4096]{2,1,0:T(8,128)S(1)}, f32[2,8,4096]{2,1,0:T(8,128)S(1)}, u32[]{:S(2)}, u32[]{:S(2)}) collective-permute-start(f32[2,8,4096]{2,1,0:T(8,128)S(1)} %get-tuple-element.53), channel_id=1, source_target_pairs={{0,1},{1,2},{2,3},{3,0},{4,5},{5,6},{6,7},{7,4},{8,9},{9,10},{10,1... | collective-permute-start | bytes 786440 | tf_op jit(solution)/shard_map/ppermute | solution.py:311
  30.2 2.9 %collective-permute-start.5 = (f32[2,8,4096]{2,1,0:T(8,128)S(1)}, f32[2,8,4096]{2,1,0:T(8,128)S(1)}, u32[]{:S(2)}, u32[]{:S(2)}) collective-permute-start(f32[2,8,4096]{2,1,0:T(8,128)S(1)} %get-tuple-element.54), channel_id=1, source_target_pairs={{0,2},{1,3},{2,0},{3,1},{4,6},{5,7},{6,4},{7,5},{8,10},{9,11},{10,... | collective-permute-start | bytes 786440 | tf_op jit(solution)/shard_map/ppermute | solution.py:311
  34.6 1.9 %collective-permute-done.3.above_ref = f32[6,2,4,4096]{3,2,1,0:T(4,128)} collective-permute-done((f32[6,2,4,4096]{3,2,1,0:T(4,128)}, f32[6,2,4,4096]{3,2,1,0:T(4,128)}, u32[]{:S(2)}, u32[]{:S(2)}) %collective-permute-start.3) | collective-permute-done | bytes 786464 | tf_op jit(solution)/shard_map/ppermute | solution.py:34
  36.5 11.3 %shard_map.60 = (f32[6,8,4096]{2,1,0:T(8,128)S(1)}, f32[6,8,4096]{2,1,0:T(8,128)S(1)}, f32[6,8,4096]{2,1,0:T(8,128)S(1)}, f32[6,8,4096]{2,1,0:T(8,128)S(1)}) custom-call(s32[1]{0:T(128)} %bitcast.2.me_ref.refs_0_, f32[8,2,16,4096]{3,2,1,0:T(8,128)} %u_ref.3, f32[6,2,4,4096]{3,2,1,0:T(4,128)S(1)} %collective-permute-done.2.below_ref, ...), custom_call_target="tpu_custom_call" | custom-call | flops 180000000 | bytes 36000000 | tf_op jit(solution)/shard_map/pallas_call | solution.py:87
  47.9 1.7 %collective-permute-start.7 = (f32[6,8,4096]{2,1,0:T(8,128)S(1)}, f32[6,8,4096]{2,1,0:T(8,128)S(1)}, u32[]{:S(2)}, u32[]{:S(2)}) collective-permute-start(f32[6,8,4096]{2,1,0:T(8,128)S(1)} %get-tuple-element.67), channel_id=1, source_target_pairs={{0,1},{1,2},{2,3},{3,0},{4,5},{5,6},{6,7},{7,4},{8,9},{9,10},{10,1... | collective-permute-start | bytes 2359304 | tf_op jit(solution)/shard_map/ppermute | solution.py:311
  49.5 2.9 %collective-permute-start.8 = (f32[6,8,4096]{2,1,0:T(8,128)S(1)}, f32[6,8,4096]{2,1,0:T(8,128)S(1)}, u32[]{:S(2)}, u32[]{:S(2)}) collective-permute-start(f32[6,8,4096]{2,1,0:T(8,128)S(1)} %get-tuple-element.68), channel_id=1, source_target_pairs={{0,2},{1,3},{2,0},{3,1},{4,6},{5,7},{6,4},{7,5},{8,10},{9,11},{10,... | collective-permute-start | bytes 2359304 | tf_op jit(solution)/shard_map/ppermute | solution.py:311
  54.1 16.4 %collective-permute-done.7.refs_6_ = f32[6,8,4096]{2,1,0:T(8,128)S(1)} collective-permute-done((f32[6,8,4096]{2,1,0:T(8,128)S(1)}, f32[6,8,4096]{2,1,0:T(8,128)S(1)}, u32[]{:S(2)}, u32[]{:S(2)}) %collective-permute-start.7) | collective-permute-done | bytes 786464 | tf_op jit(solution)/shard_map/ppermute | solution.py:311
  70.5 9.5 %collective-permute-start.10 = (f32[8,8,2048]{2,1,0:T(8,128)S(1)}, f32[8,8,2048]{2,1,0:T(8,128)S(1)}, u32[]{:S(2)}, u32[]{:S(2)}) collective-permute-start(f32[8,8,2048]{2,1,0:T(8,128)S(1)} %pad_maximum_fusion.5), channel_id=1, source_target_pairs={{0,1},{1,2},{2,3},{4,5},{5,6},{6,7},{8,9},{9,10},{10,11},{12,13},{... | collective-permute-start | bytes 1572872 | tf_op jit(solution)/shard_map/ppermute | solution.py:320
  80.0 4.9 %collective-permute-start.11 = (f32[8,8,2048]{2,1,0:T(8,128)S(1)}, f32[8,8,2048]{2,1,0:T(8,128)S(1)}, u32[]{:S(2)}, u32[]{:S(2)}) collective-permute-start(f32[8,8,2048]{2,1,0:T(8,128)S(1)} %pad_maximum_fusion.2), channel_id=1, source_target_pairs={{0,2},{1,3},{4,6},{5,7},{8,10},{9,11},{12,14},{13,15},{16,18},{17,... | collective-permute-start | bytes 1572872 | tf_op jit(solution)/shard_map/ppermute | solution.py:321
  86.3 1.5 collective-permute-done.8.refs_7_
  87.8 1.9 %shard_map.61 = (bf16[256,4096]{1,0:T(8,128)(2,1)S(1)}, bf16[256,4096]{1,0:T(8,128)(2,1)S(1)}, f32[1024,128]{1,0:T(8,128)S(1)}) custom-call(s32[1]{0:T(128)} %bitcast.2.me_ref.refs_0_, f32[2,8,4096]{2,1,0:T(8,128)S(1)} %get-tuple-element.62.refs_1_, f32[2,8,4096]{2,1,0:T(8,128)S(1)} %collective-permute-done.4.refs_2_, ...), custom_call_target="tpu_custom_call" | custom-call | tf_op jit(solution)/shard_map/pallas_call | solution.py:156
  89.6 20.8 %all_to_all.12 = f32[128,8,128]{2,1,0:T(8,128)S(1)} all-to-all(f32[128,8,128]{2,1,0:T(8,128)S(1)} %bitcast.10), channel_id=1, replica_groups=mesh['rows'=32,'vec'=4] {'rows','vec'}, dimensions={0} | all-to-all | bytes 1048576 | tf_op jit(solution)/shard_map/all_to_all | solution.py:327
  110.4 6.3 %shard_map.62 = (f32[1,32]{1,0:T(1,128)}, bf16[256,256]{1,0:T(8,128)(2,1)S(1)}, bf16[256,256]{1,0:T(8,128)(2,1)S(1)}, f32[8,8,4096]{2,1,0:T(8,128)S(1)}, f32[8,8...) custom-call(s32[1]{0:T(128)} %bitcast.2.me_ref.refs_0_, f32[1024,128]{1,0:T(8,128)S(1)} %bitcast.7, ...), custom_call_target="tpu_custom_call" | custom-call | tf_op jit(solution)/shard_map/pallas_call | solution.py:223
  116.8 3.7 %collective-permute-start.15 = (f32[8,8,4096]{2,1,0:T(8,128)S(1)}, f32[8,8,4096]{2,1,0:T(8,128)S(1)}, u32[]{:S(2)}, u32[]{:S(2)}) collective-permute-start(f32[8,8,4096]{2,1,0:T(8,128)S(1)} %get-tuple-element.87), channel_id=1, source_target_pairs={{0,3},{1,0},{2,1},{3,2},{4,7},{5,4},{6,5},{7,6},{8,11},{9,8},{10,9... | collective-permute-start | bytes 3145736 | tf_op jit(solution)/shard_map/ppermute | solution.py:311
  120.5 1.4 collective-permute-start.14
  121.9 2.9 %shard_map.63.own_ref = f32[8,4,8,4096]{3,2,1,0:T(8,128)} custom-call(s32[1]{0:T(128)} %bitcast.2.me_ref.refs_0_, bf16[256,256]{1,0:T(8,128)(2,1)S(1)} %get-tuple-element.79.w_high, bf16[256,256]{1,0:T(8,128)(2,1)S(1)} %get-tuple-element.80.w_low, bf16[256,4096]{1,0:T(8,128)(2,1)S(1)} %get-tuple-element.77.refs_2_.high_ref, ...), custom_call_target="tpu_custom_call" | custom-call | tf_op jit(solution)/shard_map/pallas_call | solution.py:267
  124.8 31.1 %collective-permute-done.14.across_ref = f32[8,8,2048]{2,1,0:T(8,128)S(1)} collective-permute-done((f32[8,8,2048]{2,1,0:T(8,128)S(1)}, f32[8,8,2048]{2,1,0:T(8,128)S(1)}, u32[]{:S(2)}, u32[]{:S(2)}) %collective-permute-start.14) | collective-permute-done | bytes 524320 | tf_op jit(solution)/shard_map/ppermute | solution.py:311
  155.9 1.5 shard_map.64
  (37 shorter events, 7.9 us)
Async XLA Ops:
  0.6 21.3 %copy-start = (f32[2,16,4096]{2,1,0:T(8,128)S(1)}, f32[2,16,4096]{2,1,0:T(8,128)}, u32[]{:S(2)}) copy-start(f32[2,16,4096]{2,1,0:T(8,128)} %z_ref.1) | copy-start | bytes 1572868
  0.6 21.3 %copy-start.1 = (f32[2,16,4096]{2,1,0:T(8,128)S(1)}, f32[2,16,4096]{2,1,0:T(8,128)}, u32[]{:S(2)}) copy-start(f32[2,16,4096]{2,1,0:T(8,128)} %c_ref.1) | copy-start | bytes 1572868
  3.5 12.5 %collective-permute-start = (f32[4,2,4,4096]{3,2,1,0:T(4,128)S(1)}, f32[4,2,4,4096]{3,2,1,0:T(4,128)S(1)}, u32[]{:S(2)}, u32[]{:S(2)}) collective-permute-start(f32[4,2,4,4096]{3,2,1,0:T(4,128)S(1)} %pad_maximum_fusion), channel_id=1, source_target_pairs={{4,0},{8,4},{12,8},{16,12},{20,16},{24,20},{28,24},{32,28},{36,32}... | collective-permute-start | bytes 1572872 | tf_op jit(solution)/shard_map/ppermute | solution.py:35
  9.4 12.0 %collective-permute-start.1 = (f32[4,2,4,4096]{3,2,1,0:T(4,128)S(1)}, f32[4,2,4,4096]{3,2,1,0:T(4,128)S(1)}, u32[]{:S(2)}, u32[]{:S(2)}) collective-permute-start(f32[4,2,4,4096]{3,2,1,0:T(4,128)S(1)} %pad_maximum_fusion.1), channel_id=1, source_target_pairs={{0,4},{4,8},{8,12},{12,16},{16,20},{20,24},{24,28},{28,32},{32,36}... | collective-permute-start | bytes 1572872 | tf_op jit(solution)/shard_map/ppermute | solution.py:34
  21.4 13.1 %collective-permute-start.2 = (f32[6,2,4,4096]{3,2,1,0:T(4,128)}, f32[6,2,4,4096]{3,2,1,0:T(4,128)S(1)}, u32[]{:S(2)}, u32[]{:S(2)}) collective-permute-start(f32[6,2,4,4096]{3,2,1,0:T(4,128)} %get-tuple-element.49), channel_id=1, source_target_pairs={{4,0},{8,4},{12,8},{16,12},{20,16},{24,20},{28,24},{32,28},{36,32}... | collective-permute-start | bytes 2359304 | tf_op jit(solution)/shard_map/ppermute | solution.py:35
  21.4 15.1 %collective-permute-start.3 = (f32[6,2,4,4096]{3,2,1,0:T(4,128)}, f32[6,2,4,4096]{3,2,1,0:T(4,128)}, u32[]{:S(2)}, u32[]{:S(2)}) collective-permute-start(f32[6,2,4,4096]{3,2,1,0:T(4,128)} %get-tuple-element.50), channel_id=1, source_target_pairs={{0,4},{4,8},{8,12},{12,16},{16,20},{20,24},{24,28},{28,32},{32,36}... | collective-permute-start | bytes 2359304 | tf_op jit(solution)/shard_map/ppermute | solution.py:34
  28.6 19.2 %collective-permute-start.4 = (f32[2,8,4096]{2,1,0:T(8,128)S(1)}, f32[2,8,4096]{2,1,0:T(8,128)S(1)}, u32[]{:S(2)}, u32[]{:S(2)}) collective-permute-start(f32[2,8,4096]{2,1,0:T(8,128)S(1)} %get-tuple-element.53), channel_id=1, source_target_pairs={{0,1},{1,2},{2,3},{3,0},{4,5},{5,6},{6,7},{7,4},{8,9},{9,10},{10,1... | collective-permute-start | bytes 786440 | tf_op jit(solution)/shard_map/ppermute | solution.py:311
  30.2 17.6 %collective-permute-start.5 = (f32[2,8,4096]{2,1,0:T(8,128)S(1)}, f32[2,8,4096]{2,1,0:T(8,128)S(1)}, u32[]{:S(2)}, u32[]{:S(2)}) collective-permute-start(f32[2,8,4096]{2,1,0:T(8,128)S(1)} %get-tuple-element.54), channel_id=1, source_target_pairs={{0,2},{1,3},{2,0},{3,1},{4,6},{5,7},{6,4},{7,5},{8,10},{9,11},{10,... | collective-permute-start | bytes 786440 | tf_op jit(solution)/shard_map/ppermute | solution.py:311
  33.1 14.7 %collective-permute-start.6 = (f32[2,8,4096]{2,1,0:T(8,128)S(1)}, f32[2,8,4096]{2,1,0:T(8,128)S(1)}, u32[]{:S(2)}, u32[]{:S(2)}) collective-permute-start(f32[2,8,4096]{2,1,0:T(8,128)S(1)} %get-tuple-element.55), channel_id=1, source_target_pairs={{0,3},{1,0},{2,1},{3,2},{4,7},{5,4},{6,5},{7,6},{8,11},{9,8},{10,9... | collective-permute-start | bytes 786440 | tf_op jit(solution)/shard_map/ppermute | solution.py:311
  47.9 22.6 %collective-permute-start.7 = (f32[6,8,4096]{2,1,0:T(8,128)S(1)}, f32[6,8,4096]{2,1,0:T(8,128)S(1)}, u32[]{:S(2)}, u32[]{:S(2)}) collective-permute-start(f32[6,8,4096]{2,1,0:T(8,128)S(1)} %get-tuple-element.67), channel_id=1, source_target_pairs={{0,1},{1,2},{2,3},{3,0},{4,5},{5,6},{6,7},{7,4},{8,9},{9,10},{10,1... | collective-permute-start | bytes 2359304 | tf_op jit(solution)/shard_map/ppermute | solution.py:311
  49.5 38.2 %collective-permute-start.8 = (f32[6,8,4096]{2,1,0:T(8,128)S(1)}, f32[6,8,4096]{2,1,0:T(8,128)S(1)}, u32[]{:S(2)}, u32[]{:S(2)}) collective-permute-start(f32[6,8,4096]{2,1,0:T(8,128)S(1)} %get-tuple-element.68), channel_id=1, source_target_pairs={{0,2},{1,3},{2,0},{3,1},{4,6},{5,7},{6,4},{7,5},{8,10},{9,11},{10,... | collective-permute-start | bytes 2359304 | tf_op jit(solution)/shard_map/ppermute | solution.py:311
  52.4 35.3 %collective-permute-start.9 = (f32[6,8,4096]{2,1,0:T(8,128)S(1)}, f32[6,8,4096]{2,1,0:T(8,128)S(1)}, u32[]{:S(2)}, u32[]{:S(2)}) collective-permute-start(f32[6,8,4096]{2,1,0:T(8,128)S(1)} %get-tuple-element.69), channel_id=1, source_target_pairs={{0,3},{1,0},{2,1},{3,2},{4,7},{5,4},{6,5},{7,6},{8,11},{9,8},{10,9... | collective-permute-start | bytes 2359304 | tf_op jit(solution)/shard_map/ppermute | solution.py:311
  70.5 39.9 %collective-permute-start.10 = (f32[8,8,2048]{2,1,0:T(8,128)S(1)}, f32[8,8,2048]{2,1,0:T(8,128)S(1)}, u32[]{:S(2)}, u32[]{:S(2)}) collective-permute-start(f32[8,8,2048]{2,1,0:T(8,128)S(1)} %pad_maximum_fusion.5), channel_id=1, source_target_pairs={{0,1},{1,2},{2,3},{4,5},{5,6},{6,7},{8,9},{9,10},{10,11},{12,13},{... | collective-permute-start | bytes 1572872 | tf_op jit(solution)/shard_map/ppermute | solution.py:320
  80.0 30.4 %collective-permute-start.11 = (f32[8,8,2048]{2,1,0:T(8,128)S(1)}, f32[8,8,2048]{2,1,0:T(8,128)S(1)}, u32[]{:S(2)}, u32[]{:S(2)}) collective-permute-start(f32[8,8,2048]{2,1,0:T(8,128)S(1)} %pad_maximum_fusion.2), channel_id=1, source_target_pairs={{0,2},{1,3},{4,6},{5,7},{8,10},{9,11},{12,14},{13,15},{16,18},{17,... | collective-permute-start | bytes 1572872 | tf_op jit(solution)/shard_map/ppermute | solution.py:321
  85.0 25.5 %collective-permute-start.12 = (f32[8,8,2048]{2,1,0:T(8,128)S(1)}, f32[8,8,2048]{2,1,0:T(8,128)S(1)}, u32[]{:S(2)}, u32[]{:S(2)}) collective-permute-start(f32[8,8,2048]{2,1,0:T(8,128)S(1)} %pad_maximum_fusion.3), channel_id=1, source_target_pairs={{0,3},{4,7},{8,11},{12,15},{16,19},{20,23},{24,27},{28,31},{32,35}... | collective-permute-start | bytes 1572872 | tf_op jit(solution)/shard_map/ppermute | solution.py:322
  116.7 39.2 %collective-permute-start.13 = (f32[8,8,4096]{2,1,0:T(8,128)S(1)}, f32[8,8,4096]{2,1,0:T(8,128)S(1)}, u32[]{:S(2)}, u32[]{:S(2)}) collective-permute-start(f32[8,8,4096]{2,1,0:T(8,128)S(1)} %get-tuple-element.85), channel_id=1, source_target_pairs={{0,1},{1,2},{2,3},{3,0},{4,5},{5,6},{6,7},{7,4},{8,9},{9,10},{10,1... | collective-permute-start | bytes 3145736 | tf_op jit(solution)/shard_map/ppermute | solution.py:311
  116.8 39.2 %collective-permute-start.15 = (f32[8,8,4096]{2,1,0:T(8,128)S(1)}, f32[8,8,4096]{2,1,0:T(8,128)S(1)}, u32[]{:S(2)}, u32[]{:S(2)}) collective-permute-start(f32[8,8,4096]{2,1,0:T(8,128)S(1)} %get-tuple-element.87), channel_id=1, source_target_pairs={{0,3},{1,0},{2,1},{3,2},{4,7},{5,4},{6,5},{7,6},{8,11},{9,8},{10,9... | collective-permute-start | bytes 3145736 | tf_op jit(solution)/shard_map/ppermute | solution.py:311
  120.5 35.4 %collective-permute-start.14 = (f32[8,8,2048]{2,1,0:T(8,128)S(1)}, f32[8,8,2048]{2,1,0:T(8,128)S(1)}, u32[]{:S(2)}, u32[]{:S(2)}) collective-permute-start(f32[8,8,2048]{2,1,0:T(8,128)S(1)} %get-tuple-element.86), channel_id=1, source_target_pairs={{0,2},{1,3},{2,0},{3,1},{4,6},{5,7},{6,4},{7,5},{8,10},{9,11},{10,... | collective-permute-start | bytes 1572872 | tf_op jit(solution)/shard_map/ppermute | solution.py:311

commit v5 on v4

--- a/solution.py
+++ b/solution.py
@@ -79,6 +79,65 @@
     slabs[3] = imag[8:16]
     for shift, out in enumerate(outs):
         out[0] = slabs[lax.rem(me_ref[0] + shift, 4)]
+
+
+def first_kernel(
+    me_ref,
+    u_ref,
+    below_ref,
+    above_ref,
+    z_ref,
+    c_ref,
+    fields_below,
+    fields_above,
+    *rest,
+):
+    outs, twice_ref, next_ref, slabs = rest[:-3], *rest[-3:]
+
+    @pl.when(pl.program_id(0) == 0)
+    def _():
+        lattice_kernel(z_ref, c_ref, fields_below, fields_above, twice_ref, next_ref)
+
+    tangent_kernel(me_ref, u_ref, below_ref, above_ref, twice_ref, *outs, slabs)
+
+
+def push_first(me, lattice_state, constant_field, vectors, halo, count):
+    rows, columns = lattice_state.shape[1:]
+    edge = pl.BlockSpec((1, 2, HALO, columns), lambda i: (2 + i, 0, 0, 0))
+    fields = pl.BlockSpec((2, 2, HALO, columns), lambda i: (0, 0, 0, 0))
+    *blocks, twice, next_state = pl.pallas_call(
+        first_kernel,
+        grid=(count,),
+        in_specs=[
+            SMEM,
+            pl.BlockSpec((1, 2, rows, columns), lambda i: (i, 0, 0, 0)),
+            edge,
+            edge,
+            FULL,
+            FULL,
+            fields,
+            fields,
+        ],
+        out_specs=[pl.BlockSpec((1, 8, columns), lambda i: (i, 0, 0))] * 4 + [FULL] * 2,
+        out_shape=[jax.ShapeDtypeStruct((count, 8, columns), jnp.float32)] * 4
+        + [
+            jax.ShapeDtypeStruct((STEPS, 2, rows + 2 * HALO, columns), jnp.float32),
+            jax.ShapeDtypeStruct((2, rows, columns), jnp.float32),
+        ],
+        scratch_shapes=[pltpu.VMEM((4, 8, columns), jnp.float32)],
+        compiler_params=params(),
+        cost_estimate=pl.CostEstimate(
+            flops=count * 45_000_000, bytes_accessed=count * 9_000_000, transcendentals=0
+        ),
+    )(
+        me,
+        pltpu.with_memory_space_constraint(vectors, pltpu.HBM),
+        *halo,
+        lattice_state,
+        constant_field,
+        *halo,
+    )
+    return blocks, twice, next_state
 
 
 def push(me, vectors, halo, twice, start, count):
@@ -341,21 +400,15 @@
     )
     ahead, rest = lax.optimization_barrier((ahead, edges(tangents[CHUNKS[0] :])))
     halos = [ahead, neighbours(*rest)]
-    twice, next_state = pl.pallas_call(
-        lattice_kernel,
-        in_specs=[FULL] * 4,
-        out_specs=[FULL] * 2,
-        out_shape=[
-            jax.ShapeDtypeStruct((STEPS, 2, rows + 2 * HALO, columns), jnp.float32),
-            jax.ShapeDtypeStruct((2, rows, columns), jnp.float32),
-        ],
-        compiler_params=params(),
-    )(lattice_state, constant_field, *halos[0])
     pieces, local, start = [], [], 0
     for count, halo in zip(CHUNKS, halos):
         if pieces:
             halo, blocks = lax.optimization_barrier((halo, blocks))
-        blocks = push(me, tangents, halo, twice, start, count)
+            blocks = push(me, tangents, halo, twice, start, count)
+        else:
+            blocks, twice, next_state = push_first(
+                me, lattice_state, constant_field, tangents, halo, count
+            )
         if pieces:
             blocks, pieces = lax.optimization_barrier((blocks, pieces))
         local.append(blocks)

time: 158 us -> 158 us (level)
    pallas_call x2 -> x1, Pallas kernels: 15.8 us -> 11.3 us  [push(): pl.pallas_call(tangent_kernel, grid=(count,), in_specs=[SMEM, pl.BlockSpe...]
    pallas_call x1, Pallas kernels: 2.2 us -> 6.42 us  [push_first(): pl.pallas_call(first_kernel, grid=(count,), in_specs=[SMEM, pl.BlockSpec(...]
where the time goes in v5:
time: 158 us; the launch traced here: 157 us
  waiting for transfers between devices  59.9 us (38%)
  starting transfers between devices  39 us (25%)
  Pallas kernels  30.3 us (19%)
  blocking collectives  20.5 us (13%)
  local copies, waits for them, and re-layouts  6.15 us (4%)
    ppermute x9, waiting for transfers between devices, shifted(): return lax.ppermute(block, 'vec', [(i, (i + shift) % 4) for i in range(4)])  49.1 us
    all_to_all x1, blocking collectives, all_terms(): return lax.all_to_all(copies, ('rows', 'vec'), 0, 0, tiled=True)  20.5 us
    ppermute x9, starting transfers between devices, shifted(): return lax.ppermute(block, 'vec', [(i, (i + shift) % 4) for i in range(4)])  16.9 us
    pallas_call x1, Pallas kernels, push(): pl.pallas_call(tangent_kernel, grid=(count,), in_specs=[SMEM, pl.BlockSpe...  11.3 us
    ppermute x1, starting transfers between devices, opposite(): one = lax.ppermute(blocks[3], 'vec', [(0, 1), (1, 2), (2, 3)])  9.42 us
    ppermute x2, waiting for transfers between devices, neighbours(): above = lax.ppermute(last, 'rows', forward)  7.64 us
    pallas_call x1, Pallas kernels, push_first(): pl.pallas_call(first_kernel, grid=(count,), in_specs=[SMEM, pl.BlockSpec(...  6.42 us
    pallas_call x1, Pallas kernels, factorise(): pl.pallas_call(lambda *refs: factor_kernel(scale, *refs), in_specs=[SMEM]...  6.27 us
  transfers between devices with their start and end apart: 16, of which 6 were waited for; matrix products, arithmetic and copies ran while one was open for 2% of the time, Pallas kernels for 14%

profile of v5, /device:TPU:0, one launch (start us, length us, event | category | flops | bytes accessed | tf_op | source)
XLA Modules:
  0.0 157.3 jit_solution(12933312789148155969)
XLA Ops:
  0.7 1.4 fusion.1
  3.5 5.8 %collective-permute-start = (f32[4,2,4,4096]{3,2,1,0:T(4,128)S(1)}, f32[4,2,4,4096]{3,2,1,0:T(4,128)S(1)}, u32[]{:S(2)}, u32[]{:S(2)}) collective-permute-start(f32[4,2,4,4096]{3,2,1,0:T(4,128)S(1)} %pad_maximum_fusion), channel_id=1, source_target_pairs={{4,0},{8,4},{12,8},{16,12},{20,16},{24,20},{28,24},{32,28},{36,32}... | collective-permute-start | bytes 1572872 | tf_op jit(solution)/shard_map/ppermute | solution.py:35
  9.5 3.3 %fusion = (f32[6,2,4,4096]{3,2,1,0:T(4,128)}, f32[6,2,4,4096]{3,2,1,0:T(4,128)}) fusion(f32[8,2,16,4096]{3,2,1,0:T(8,128)} %u_ref.3), kind=kLoop, calls=%fused_computation.6 | loop fusion | bytes 3145728 | tf_op jit(solution)/shard_map/slice | solution.py:27
  12.8 3.2 %collective-permute-done.below_ref.fields_below = f32[4,2,4,4096]{3,2,1,0:T(4,128)S(1)} collective-permute-done((f32[4,2,4,4096]{3,2,1,0:T(4,128)S(1)}, f32[4,2,4,4096]{3,2,1,0:T(4,128)S(1)}, u32[]{:S(2)}, u32[]{:S(2)}) %collective-permute-start) | collective-permute-done | bytes 524320 | tf_op jit(solution)/shard_map/ppermute | solution.py:35
  16.0 5.4 %collective-permute-done.1.above_ref.fields_above = f32[4,2,4,4096]{3,2,1,0:T(4,128)S(1)} collective-permute-done((f32[4,2,4,4096]{3,2,1,0:T(4,128)S(1)}, f32[4,2,4,4096]{3,2,1,0:T(4,128)S(1)}, u32[]{:S(2)}, u32[]{:S(2)}) %collective-permute-start.1) | collective-permute-done | bytes 524320 | tf_op jit(solution)/shard_map/ppermute | solution.py:34
  21.9 6.4 %shard_map.58 = (f32[2,8,4096]{2,1,0:T(8,128)S(1)}, f32[2,8,4096]{2,1,0:T(8,128)S(1)}, f32[2,8,4096]{2,1,0:T(8,128)S(1)}, f32[2,8,4096]{2,1,0:T(8,128)S(1)}, f32...) custom-call(s32[1]{0:T(128)} %bitcast.me_ref.refs_0_, f32[8,2,16,4096]{3,2,1,0:T(8,128)} %u_ref.3, ...), custom_call_target="tpu_custom_call" | custom-call | flops 90000000 | bytes 18000000 | tf_op jit(solution)/shard_map/pallas_call | solution.py:108
  28.4 1.6 %collective-permute-start.4 = (f32[2,8,4096]{2,1,0:T(8,128)S(1)}, f32[2,8,4096]{2,1,0:T(8,128)S(1)}, u32[]{:S(2)}, u32[]{:S(2)}) collective-permute-start(f32[2,8,4096]{2,1,0:T(8,128)S(1)} %get-tuple-element.52), channel_id=1, source_target_pairs={{0,1},{1,2},{2,3},{3,0},{4,5},{5,6},{6,7},{7,4},{8,9},{9,10},{10,1... | collective-permute-start | bytes 786440 | tf_op jit(solution)/shard_map/ppermute | solution.py:370
  29.9 2.9 %collective-permute-start.5 = (f32[2,8,4096]{2,1,0:T(8,128)S(1)}, f32[2,8,4096]{2,1,0:T(8,128)S(1)}, u32[]{:S(2)}, u32[]{:S(2)}) collective-permute-start(f32[2,8,4096]{2,1,0:T(8,128)S(1)} %get-tuple-element.53), channel_id=1, source_target_pairs={{0,2},{1,3},{2,0},{3,1},{4,6},{5,7},{6,4},{7,5},{8,10},{9,11},{10,... | collective-permute-start | bytes 786440 | tf_op jit(solution)/shard_map/ppermute | solution.py:370
  34.3 2.2 %collective-permute-done.3.above_ref = f32[6,2,4,4096]{3,2,1,0:T(4,128)} collective-permute-done((f32[6,2,4,4096]{3,2,1,0:T(4,128)}, f32[6,2,4,4096]{3,2,1,0:T(4,128)}, u32[]{:S(2)}, u32[]{:S(2)}) %collective-permute-start.3) | collective-permute-done | bytes 786464 | tf_op jit(solution)/shard_map/ppermute | solution.py:34
  36.5 11.3 %shard_map.59 = (f32[6,8,4096]{2,1,0:T(8,128)S(1)}, f32[6,8,4096]{2,1,0:T(8,128)S(1)}, f32[6,8,4096]{2,1,0:T(8,128)S(1)}, f32[6,8,4096]{2,1,0:T(8,128)S(1)}) custom-call(s32[1]{0:T(128)} %bitcast.me_ref.refs_0_, f32[8,2,16,4096]{3,2,1,0:T(8,128)} %u_ref.3, f32[6,2,4,4096]{3,2,1,0:T(4,128)S(1)} %collective-permute-done.2.below_ref, ...), custom_call_target="tpu_custom_call" | custom-call | flops 180000000 | bytes 36000000 | tf_op jit(solution)/shard_map/pallas_call | solution.py:146
  47.9 1.7 %collective-permute-start.7 = (f32[6,8,4096]{2,1,0:T(8,128)S(1)}, f32[6,8,4096]{2,1,0:T(8,128)S(1)}, u32[]{:S(2)}, u32[]{:S(2)}) collective-permute-start(f32[6,8,4096]{2,1,0:T(8,128)S(1)} %get-tuple-element.67), channel_id=1, source_target_pairs={{0,1},{1,2},{2,3},{3,0},{4,5},{5,6},{6,7},{7,4},{8,9},{9,10},{10,1... | collective-permute-start | bytes 2359304 | tf_op jit(solution)/shard_map/ppermute | solution.py:370
  49.5 2.9 %collective-permute-start.8 = (f32[6,8,4096]{2,1,0:T(8,128)S(1)}, f32[6,8,4096]{2,1,0:T(8,128)S(1)}, u32[]{:S(2)}, u32[]{:S(2)}) collective-permute-start(f32[6,8,4096]{2,1,0:T(8,128)S(1)} %get-tuple-element.68), channel_id=1, source_target_pairs={{0,2},{1,3},{2,0},{3,1},{4,6},{5,7},{6,4},{7,5},{8,10},{9,11},{10,... | collective-permute-start | bytes 2359304 | tf_op jit(solution)/shard_map/ppermute | solution.py:370
  54.1 16.6 %collective-permute-done.7.refs_6_ = f32[6,8,4096]{2,1,0:T(8,128)S(1)} collective-permute-done((f32[6,8,4096]{2,1,0:T(8,128)S(1)}, f32[6,8,4096]{2,1,0:T(8,128)S(1)}, u32[]{:S(2)}, u32[]{:S(2)}) %collective-permute-start.7) | collective-permute-done | bytes 786464 | tf_op jit(solution)/shard_map/ppermute | solution.py:370
  70.7 9.4 %collective-permute-start.10 = (f32[8,8,2048]{2,1,0:T(8,128)S(1)}, f32[8,8,2048]{2,1,0:T(8,128)S(1)}, u32[]{:S(2)}, u32[]{:S(2)}) collective-permute-start(f32[8,8,2048]{2,1,0:T(8,128)S(1)} %pad_maximum_fusion.5), channel_id=1, source_target_pairs={{0,1},{1,2},{2,3},{4,5},{5,6},{6,7},{8,9},{9,10},{10,11},{12,13},{... | collective-permute-start | bytes 1572872 | tf_op jit(solution)/shard_map/ppermute | solution.py:379
  80.1 4.9 %collective-permute-start.11 = (f32[8,8,2048]{2,1,0:T(8,128)S(1)}, f32[8,8,2048]{2,1,0:T(8,128)S(1)}, u32[]{:S(2)}, u32[]{:S(2)}) collective-permute-start(f32[8,8,2048]{2,1,0:T(8,128)S(1)} %pad_maximum_fusion.2), channel_id=1, source_target_pairs={{0,2},{1,3},{4,6},{5,7},{8,10},{9,11},{12,14},{13,15},{16,18},{17,... | collective-permute-start | bytes 1572872 | tf_op jit(solution)/shard_map/ppermute | solution.py:380
  86.4 1.4 collective-permute-done.8.refs_7_
  87.8 1.9 %shard_map.60 = (bf16[256,4096]{1,0:T(8,128)(2,1)S(1)}, bf16[256,4096]{1,0:T(8,128)(2,1)S(1)}, f32[1024,128]{1,0:T(8,128)S(1)}) custom-call(s32[1]{0:T(128)} %bitcast.me_ref.refs_0_, f32[2,8,4096]{2,1,0:T(8,128)S(1)} %get-tuple-element.62.refs_1_, f32[2,8,4096]{2,1,0:T(8,128)S(1)} %collective-permute-done.4.refs_2_, ...), custom_call_target="tpu_custom_call" | custom-call | tf_op jit(solution)/shard_map/pallas_call | solution.py:215
  89.6 20.5 %all_to_all.12 = f32[128,8,128]{2,1,0:T(8,128)S(1)} all-to-all(f32[128,8,128]{2,1,0:T(8,128)S(1)} %bitcast.10), channel_id=1, replica_groups=mesh['rows'=32,'vec'=4] {'rows','vec'}, dimensions={0} | all-to-all | bytes 1048576 | tf_op jit(solution)/shard_map/all_to_all | solution.py:386
  110.1 6.3 %shard_map.61 = (f32[1,32]{1,0:T(1,128)}, bf16[256,256]{1,0:T(8,128)(2,1)S(1)}, bf16[256,256]{1,0:T(8,128)(2,1)S(1)}, f32[8,8,4096]{2,1,0:T(8,128)S(1)}, f32[8,8...) custom-call(s32[1]{0:T(128)} %bitcast.me_ref.refs_0_, f32[1024,128]{1,0:T(8,128)S(1)} %bitcast.7, ...), custom_call_target="tpu_custom_call" | custom-call | tf_op jit(solution)/shard_map/pallas_call | solution.py:282
  116.5 3.7 %collective-permute-start.15 = (f32[8,8,4096]{2,1,0:T(8,128)S(1)}, f32[8,8,4096]{2,1,0:T(8,128)S(1)}, u32[]{:S(2)}, u32[]{:S(2)}) collective-permute-start(f32[8,8,4096]{2,1,0:T(8,128)S(1)} %get-tuple-element.87), channel_id=1, source_target_pairs={{0,3},{1,0},{2,1},{3,2},{4,7},{5,4},{6,5},{7,6},{8,11},{9,8},{10,9... | collective-permute-start | bytes 3145736 | tf_op jit(solution)/shard_map/ppermute | solution.py:370
  120.2 1.4 collective-permute-start.14
  121.6 2.9 %shard_map.62.own_ref = f32[8,4,8,4096]{3,2,1,0:T(8,128)} custom-call(s32[1]{0:T(128)} %bitcast.me_ref.refs_0_, bf16[256,256]{1,0:T(8,128)(2,1)S(1)} %get-tuple-element.79.w_high, bf16[256,256]{1,0:T(8,128)(2,1)S(1)} %get-tuple-element.80.w_low, bf16[256,4096]{1,0:T(8,128)(2,1)S(1)} %get-tuple-element.77.refs_2_.high_ref, ...), custom_call_target="tpu_custom_call" | custom-call | tf_op jit(solution)/shard_map/pallas_call | solution.py:326
  124.5 31.1 %collective-permute-done.14.across_ref = f32[8,8,2048]{2,1,0:T(8,128)S(1)} collective-permute-done((f32[8,8,2048]{2,1,0:T(8,128)S(1)}, f32[8,8,2048]{2,1,0:T(8,128)S(1)}, u32[]{:S(2)}, u32[]{:S(2)}) %collective-permute-start.14) | collective-permute-done | bytes 524320 | tf_op jit(solution)/shard_map/ppermute | solution.py:370
  155.6 1.5 shard_map.63
  (36 shorter events, 6.6 us)
Async XLA Ops:
  0.6 21.3 %copy-start = (f32[2,16,4096]{2,1,0:T(8,128)S(1)}, f32[2,16,4096]{2,1,0:T(8,128)}, u32[]{:S(2)}) copy-start(f32[2,16,4096]{2,1,0:T(8,128)} %z_ref.1) | copy-start | bytes 1572868
  0.6 21.3 %copy-start.1 = (f32[2,16,4096]{2,1,0:T(8,128)S(1)}, f32[2,16,4096]{2,1,0:T(8,128)}, u32[]{:S(2)}) copy-start(f32[2,16,4096]{2,1,0:T(8,128)} %c_ref.1) | copy-start | bytes 1572868
  3.5 12.5 %collective-permute-start = (f32[4,2,4,4096]{3,2,1,0:T(4,128)S(1)}, f32[4,2,4,4096]{3,2,1,0:T(4,128)S(1)}, u32[]{:S(2)}, u32[]{:S(2)}) collective-permute-start(f32[4,2,4,4096]{3,2,1,0:T(4,128)S(1)} %pad_maximum_fusion), channel_id=1, source_target_pairs={{4,0},{8,4},{12,8},{16,12},{20,16},{24,20},{28,24},{32,28},{36,32}... | collective-permute-start | bytes 1572872 | tf_op jit(solution)/shard_map/ppermute | solution.py:35
  9.4 12.0 %collective-permute-start.1 = (f32[4,2,4,4096]{3,2,1,0:T(4,128)S(1)}, f32[4,2,4,4096]{3,2,1,0:T(4,128)S(1)}, u32[]{:S(2)}, u32[]{:S(2)}) collective-permute-start(f32[4,2,4,4096]{3,2,1,0:T(4,128)S(1)} %pad_maximum_fusion.1), channel_id=1, source_target_pairs={{0,4},{4,8},{8,12},{12,16},{16,20},{20,24},{24,28},{28,32},{32,36}... | collective-permute-start | bytes 1572872 | tf_op jit(solution)/shard_map/ppermute | solution.py:34
  21.4 12.8 %collective-permute-start.2 = (f32[6,2,4,4096]{3,2,1,0:T(4,128)}, f32[6,2,4,4096]{3,2,1,0:T(4,128)S(1)}, u32[]{:S(2)}, u32[]{:S(2)}) collective-permute-start(f32[6,2,4,4096]{3,2,1,0:T(4,128)} %get-tuple-element.49), channel_id=1, source_target_pairs={{4,0},{8,4},{12,8},{16,12},{20,16},{24,20},{28,24},{32,28},{36,32}... | collective-permute-start | bytes 2359304 | tf_op jit(solution)/shard_map/ppermute | solution.py:35
  21.4 15.1 %collective-permute-start.3 = (f32[6,2,4,4096]{3,2,1,0:T(4,128)}, f32[6,2,4,4096]{3,2,1,0:T(4,128)}, u32[]{:S(2)}, u32[]{:S(2)}) collective-permute-start(f32[6,2,4,4096]{3,2,1,0:T(4,128)} %get-tuple-element.50), channel_id=1, source_target_pairs={{0,4},{4,8},{8,12},{12,16},{16,20},{20,24},{24,28},{28,32},{32,36}... | collective-permute-start | bytes 2359304 | tf_op jit(solution)/shard_map/ppermute | solution.py:34
  28.4 19.5 %collective-permute-start.4 = (f32[2,8,4096]{2,1,0:T(8,128)S(1)}, f32[2,8,4096]{2,1,0:T(8,128)S(1)}, u32[]{:S(2)}, u32[]{:S(2)}) collective-permute-start(f32[2,8,4096]{2,1,0:T(8,128)S(1)} %get-tuple-element.52), channel_id=1, source_target_pairs={{0,1},{1,2},{2,3},{3,0},{4,5},{5,6},{6,7},{7,4},{8,9},{9,10},{10,1... | collective-permute-start | bytes 786440 | tf_op jit(solution)/shard_map/ppermute | solution.py:370
  29.9 17.9 %collective-permute-start.5 = (f32[2,8,4096]{2,1,0:T(8,128)S(1)}, f32[2,8,4096]{2,1,0:T(8,128)S(1)}, u32[]{:S(2)}, u32[]{:S(2)}) collective-permute-start(f32[2,8,4096]{2,1,0:T(8,128)S(1)} %get-tuple-element.53), channel_id=1, source_target_pairs={{0,2},{1,3},{2,0},{3,1},{4,6},{5,7},{6,4},{7,5},{8,10},{9,11},{10,... | collective-permute-start | bytes 786440 | tf_op jit(solution)/shard_map/ppermute | solution.py:370
  32.8 15.0 %collective-permute-start.6 = (f32[2,8,4096]{2,1,0:T(8,128)S(1)}, f32[2,8,4096]{2,1,0:T(8,128)S(1)}, u32[]{:S(2)}, u32[]{:S(2)}) collective-permute-start(f32[2,8,4096]{2,1,0:T(8,128)S(1)} %get-tuple-element.54), channel_id=1, source_target_pairs={{0,3},{1,0},{2,1},{3,2},{4,7},{5,4},{6,5},{7,6},{8,11},{9,8},{10,9... | collective-permute-start | bytes 786440 | tf_op jit(solution)/shard_map/ppermute | solution.py:370
  47.9 22.8 %collective-permute-start.7 = (f32[6,8,4096]{2,1,0:T(8,128)S(1)}, f32[6,8,4096]{2,1,0:T(8,128)S(1)}, u32[]{:S(2)}, u32[]{:S(2)}) collective-permute-start(f32[6,8,4096]{2,1,0:T(8,128)S(1)} %get-tuple-element.67), channel_id=1, source_target_pairs={{0,1},{1,2},{2,3},{3,0},{4,5},{5,6},{6,7},{7,4},{8,9},{9,10},{10,1... | collective-permute-start | bytes 2359304 | tf_op jit(solution)/shard_map/ppermute | solution.py:370
  49.5 38.2 %collective-permute-start.8 = (f32[6,8,4096]{2,1,0:T(8,128)S(1)}, f32[6,8,4096]{2,1,0:T(8,128)S(1)}, u32[]{:S(2)}, u32[]{:S(2)}) collective-permute-start(f32[6,8,4096]{2,1,0:T(8,128)S(1)} %get-tuple-element.68), channel_id=1, source_target_pairs={{0,2},{1,3},{2,0},{3,1},{4,6},{5,7},{6,4},{7,5},{8,10},{9,11},{10,... | collective-permute-start | bytes 2359304 | tf_op jit(solution)/shard_map/ppermute | solution.py:370
  52.4 35.3 %collective-permute-start.9 = (f32[6,8,4096]{2,1,0:T(8,128)S(1)}, f32[6,8,4096]{2,1,0:T(8,128)S(1)}, u32[]{:S(2)}, u32[]{:S(2)}) collective-permute-start(f32[6,8,4096]{2,1,0:T(8,128)S(1)} %get-tuple-element.69), channel_id=1, source_target_pairs={{0,3},{1,0},{2,1},{3,2},{4,7},{5,4},{6,5},{7,6},{8,11},{9,8},{10,9... | collective-permute-start | bytes 2359304 | tf_op jit(solution)/shard_map/ppermute | solution.py:370
  70.7 39.5 %collective-permute-start.10 = (f32[8,8,2048]{2,1,0:T(8,128)S(1)}, f32[8,8,2048]{2,1,0:T(8,128)S(1)}, u32[]{:S(2)}, u32[]{:S(2)}) collective-permute-start(f32[8,8,2048]{2,1,0:T(8,128)S(1)} %pad_maximum_fusion.5), channel_id=1, source_target_pairs={{0,1},{1,2},{2,3},{4,5},{5,6},{6,7},{8,9},{9,10},{10,11},{12,13},{... | collective-permute-start | bytes 1572872 | tf_op jit(solution)/shard_map/ppermute | solution.py:379
  80.1 30.0 %collective-permute-start.11 = (f32[8,8,2048]{2,1,0:T(8,128)S(1)}, f32[8,8,2048]{2,1,0:T(8,128)S(1)}, u32[]{:S(2)}, u32[]{:S(2)}) collective-permute-start(f32[8,8,2048]{2,1,0:T(8,128)S(1)} %pad_maximum_fusion.2), channel_id=1, source_target_pairs={{0,2},{1,3},{4,6},{5,7},{8,10},{9,11},{12,14},{13,15},{16,18},{17,... | collective-permute-start | bytes 1572872 | tf_op jit(solution)/shard_map/ppermute | solution.py:380
  85.0 25.1 %collective-permute-start.12 = (f32[8,8,2048]{2,1,0:T(8,128)S(1)}, f32[8,8,2048]{2,1,0:T(8,128)S(1)}, u32[]{:S(2)}, u32[]{:S(2)}) collective-permute-start(f32[8,8,2048]{2,1,0:T(8,128)S(1)} %pad_maximum_fusion.3), channel_id=1, source_target_pairs={{0,3},{4,7},{8,11},{12,15},{16,19},{20,23},{24,27},{28,31},{32,35}... | collective-permute-start | bytes 1572872 | tf_op jit(solution)/shard_map/ppermute | solution.py:381
  116.4 39.2 %collective-permute-start.13 = (f32[8,8,4096]{2,1,0:T(8,128)S(1)}, f32[8,8,4096]{2,1,0:T(8,128)S(1)}, u32[]{:S(2)}, u32[]{:S(2)}) collective-permute-start(f32[8,8,4096]{2,1,0:T(8,128)S(1)} %get-tuple-element.85), channel_id=1, source_target_pairs={{0,1},{1,2},{2,3},{3,0},{4,5},{5,6},{6,7},{7,4},{8,9},{9,10},{10,1... | collective-permute-start | bytes 3145736 | tf_op jit(solution)/shard_map/ppermute | solution.py:370
  116.5 39.1 %collective-permute-start.15 = (f32[8,8,4096]{2,1,0:T(8,128)S(1)}, f32[8,8,4096]{2,1,0:T(8,128)S(1)}, u32[]{:S(2)}, u32[]{:S(2)}) collective-permute-start(f32[8,8,4096]{2,1,0:T(8,128)S(1)} %get-tuple-element.87), channel_id=1, source_target_pairs={{0,3},{1,0},{2,1},{3,2},{4,7},{5,4},{6,5},{7,6},{8,11},{9,8},{10,9... | collective-permute-start | bytes 3145736 | tf_op jit(solution)/shard_map/ppermute | solution.py:370
  120.2 35.4 %collective-permute-start.14 = (f32[8,8,2048]{2,1,0:T(8,128)S(1)}, f32[8,8,2048]{2,1,0:T(8,128)S(1)}, u32[]{:S(2)}, u32[]{:S(2)}) collective-permute-start(f32[8,8,2048]{2,1,0:T(8,128)S(1)} %get-tuple-element.86), channel_id=1, source_target_pairs={{0,2},{1,3},{2,0},{3,1},{4,6},{5,7},{6,4},{7,5},{8,10},{9,11},{10,... | collective-permute-start | bytes 1572872 | tf_op jit(solution)/shard_map/ppermute | solution.py:370

commit v6 on v5

--- a/solution.py
+++ b/solution.py
@@ -387,7 +387,7 @@
 
 
 CHUNKS = (2, 6)
-NEAR = 2048
+NEAR = 2304
 
 
 def per_device(lattice_state, constant_field, tangents):

time: 158 us -> 159 us (level)
  blocking collectives: 20.5 us -> 23.4 us
  waiting for transfers between devices: 59.9 us -> 58.3 us
    all_to_all x1, blocking collectives: 20.5 us -> 23.4 us  [all_terms(): return lax.all_to_all(copies, ('rows', 'vec'), 0, 0, tiled=True)]
    ppermute x9, waiting for transfers between devices: 49.1 us -> 47.5 us  [shifted(): return lax.ppermute(block, 'vec', [(i, (i + shift) % 4) for i in range(4)])]
where the time goes in v6:
time: 159 us
  waiting for transfers between devices  58.3 us (37%)
  starting transfers between devices  39 us (25%)
  Pallas kernels  30.4 us (19%)
  blocking collectives  23.4 us (15%)
  local copies, waits for them, and re-layouts  6.17 us (4%)
    ppermute x9, waiting for transfers between devices, shifted(): return lax.ppermute(block, 'vec', [(i, (i + shift) % 4) for i in range(4)])  47.5 us
    all_to_all x1, blocking collectives, all_terms(): return lax.all_to_all(copies, ('rows', 'vec'), 0, 0, tiled=True)  23.4 us
    ppermute x9, starting transfers between devices, shifted(): return lax.ppermute(block, 'vec', [(i, (i + shift) % 4) for i in range(4)])  17 us
    pallas_call x1, Pallas kernels, push(): pl.pallas_call(tangent_kernel, grid=(count,), in_specs=[SMEM, pl.BlockSpe...  11.3 us
    ppermute x1, starting transfers between devices, opposite(): one = lax.ppermute(blocks[3], 'vec', [(0, 1), (1, 2), (2, 3)])  9.39 us
    ppermute x2, waiting for transfers between devices, neighbours(): above = lax.ppermute(last, 'rows', forward)  7.64 us
    pallas_call x1, Pallas kernels, push_first(): pl.pallas_call(first_kernel, grid=(count,), in_specs=[SMEM, pl.BlockSpec(...  6.42 us
    pallas_call x1, Pallas kernels, factorise(): pl.pallas_call(lambda *refs: factor_kernel(scale, *refs), in_specs=[SMEM]...  6.23 us
  transfers between devices with their start and end apart: 16, of which 6 were waited for; matrix products, arithmetic and copies ran while one was open for 2% of the time, Pallas kernels for 14%

profile of v6, /device:TPU:0, one launch (start us, length us, event | category | flops | bytes accessed | tf_op | source)
XLA Modules:
  0.0 158.8 jit_solution(13196276767054058243)
XLA Ops:
  0.7 1.4 fusion.1
  3.5 5.8 %collective-permute-start = (f32[4,2,4,4096]{3,2,1,0:T(4,128)S(1)}, f32[4,2,4,4096]{3,2,1,0:T(4,128)S(1)}, u32[]{:S(2)}, u32[]{:S(2)}) collective-permute-start(f32[4,2,4,4096]{3,2,1,0:T(4,128)S(1)} %pad_maximum_fusion.4), channel_id=1, source_target_pairs={{4,0},{8,4},{12,8},{16,12},{20,16},{24,20},{28,24},{32,28},{36,32}... | collective-permute-start | bytes 1572872 | tf_op jit(solution)/shard_map/ppermute | solution.py:35
  9.5 3.3 %fusion = (f32[6,2,4,4096]{3,2,1,0:T(4,128)}, f32[6,2,4,4096]{3,2,1,0:T(4,128)}) fusion(f32[8,2,16,4096]{3,2,1,0:T(8,128)} %u_ref.3), kind=kLoop, calls=%fused_computation.6 | loop fusion | bytes 3145728 | tf_op jit(solution)/shard_map/slice | solution.py:27
  12.8 3.2 %collective-permute-done.below_ref.fields_below = f32[4,2,4,4096]{3,2,1,0:T(4,128)S(1)} collective-permute-done((f32[4,2,4,4096]{3,2,1,0:T(4,128)S(1)}, f32[4,2,4,4096]{3,2,1,0:T(4,128)S(1)}, u32[]{:S(2)}, u32[]{:S(2)}) %collective-permute-start) | collective-permute-done | bytes 524320 | tf_op jit(solution)/shard_map/ppermute | solution.py:35
  16.0 5.4 %collective-permute-done.1.above_ref.fields_above = f32[4,2,4,4096]{3,2,1,0:T(4,128)S(1)} collective-permute-done((f32[4,2,4,4096]{3,2,1,0:T(4,128)S(1)}, f32[4,2,4,4096]{3,2,1,0:T(4,128)S(1)}, u32[]{:S(2)}, u32[]{:S(2)}) %collective-permute-start.1) | collective-permute-done | bytes 524320 | tf_op jit(solution)/shard_map/ppermute | solution.py:34
  21.9 6.4 %shard_map.58 = (f32[2,8,4096]{2,1,0:T(8,128)S(1)}, f32[2,8,4096]{2,1,0:T(8,128)S(1)}, f32[2,8,4096]{2,1,0:T(8,128)S(1)}, f32[2,8,4096]{2,1,0:T(8,128)S(1)}, f32...) custom-call(s32[1]{0:T(128)} %bitcast.me_ref.refs_0_, f32[8,2,16,4096]{3,2,1,0:T(8,128)} %u_ref.3, ...), custom_call_target="tpu_custom_call" | custom-call | flops 90000000 | bytes 18000000 | tf_op jit(solution)/shard_map/pallas_call | solution.py:108
  28.4 1.6 collective-permute-start.4
  29.9 2.9 %collective-permute-start.5 = (f32[2,8,4096]{2,1,0:T(8,128)S(1)}, f32[2,8,4096]{2,1,0:T(8,128)S(1)}, u32[]{:S(2)}, u32[]{:S(2)}) collective-permute-start(f32[2,8,4096]{2,1,0:T(8,128)S(1)} %get-tuple-element.53), channel_id=1, source_target_pairs={{0,2},{1,3},{2,0},{3,1},{4,6},{5,7},{6,4},{7,5},{8,10},{9,11},{10,... | collective-permute-start | bytes 786440 | tf_op jit(solution)/shard_map/ppermute | solution.py:370
  34.3 2.2 %collective-permute-done.3.above_ref = f32[6,2,4,4096]{3,2,1,0:T(4,128)} collective-permute-done((f32[6,2,4,4096]{3,2,1,0:T(4,128)}, f32[6,2,4,4096]{3,2,1,0:T(4,128)}, u32[]{:S(2)}, u32[]{:S(2)}) %collective-permute-start.3) | collective-permute-done | bytes 786464 | tf_op jit(solution)/shard_map/ppermute | solution.py:34
  36.5 11.3 %shard_map.59 = (f32[6,8,4096]{2,1,0:T(8,128)S(1)}, f32[6,8,4096]{2,1,0:T(8,128)S(1)}, f32[6,8,4096]{2,1,0:T(8,128)S(1)}, f32[6,8,4096]{2,1,0:T(8,128)S(1)}) custom-call(s32[1]{0:T(128)} %bitcast.me_ref.refs_0_, f32[8,2,16,4096]{3,2,1,0:T(8,128)} %u_ref.3, f32[6,2,4,4096]{3,2,1,0:T(4,128)S(1)} %collective-permute-done.2.below_ref, ...), custom_call_target="tpu_custom_call" | custom-call | flops 180000000 | bytes 36000000 | tf_op jit(solution)/shard_map/pallas_call | solution.py:146
  47.9 1.7 %collective-permute-start.7 = (f32[6,8,4096]{2,1,0:T(8,128)S(1)}, f32[6,8,4096]{2,1,0:T(8,128)S(1)}, u32[]{:S(2)}, u32[]{:S(2)}) collective-permute-start(f32[6,8,4096]{2,1,0:T(8,128)S(1)} %get-tuple-element.67), channel_id=1, source_target_pairs={{0,1},{1,2},{2,3},{3,0},{4,5},{5,6},{6,7},{7,4},{8,9},{9,10},{10,1... | collective-permute-start | bytes 2359304 | tf_op jit(solution)/shard_map/ppermute | solution.py:370
  49.6 3.0 %collective-permute-start.8 = (f32[6,8,4096]{2,1,0:T(8,128)S(1)}, f32[6,8,4096]{2,1,0:T(8,128)S(1)}, u32[]{:S(2)}, u32[]{:S(2)}) collective-permute-start(f32[6,8,4096]{2,1,0:T(8,128)S(1)} %get-tuple-element.68), channel_id=1, source_target_pairs={{0,2},{1,3},{2,0},{3,1},{4,6},{5,7},{6,4},{7,5},{8,10},{9,11},{10,... | collective-permute-start | bytes 2359304 | tf_op jit(solution)/shard_map/ppermute | solution.py:370
  54.2 16.5 %collective-permute-done.7.refs_6_ = f32[6,8,4096]{2,1,0:T(8,128)S(1)} collective-permute-done((f32[6,8,4096]{2,1,0:T(8,128)S(1)}, f32[6,8,4096]{2,1,0:T(8,128)S(1)}, u32[]{:S(2)}, u32[]{:S(2)}) %collective-permute-start.7) | collective-permute-done | bytes 786464 | tf_op jit(solution)/shard_map/ppermute | solution.py:370
  70.7 9.4 %collective-permute-start.10 = (f32[8,8,2304]{2,1,0:T(8,128)S(1)}, f32[8,8,2304]{2,1,0:T(8,128)S(1)}, u32[]{:S(2)}, u32[]{:S(2)}) collective-permute-start(f32[8,8,2304]{2,1,0:T(8,128)S(1)} %pad_maximum_fusion.3), channel_id=1, source_target_pairs={{0,1},{1,2},{2,3},{4,5},{5,6},{6,7},{8,9},{9,10},{10,11},{12,13},{... | collective-permute-start | bytes 1769480 | tf_op jit(solution)/shard_map/ppermute | solution.py:379
  80.1 4.9 %collective-permute-start.11 = (f32[8,8,2304]{2,1,0:T(8,128)S(1)}, f32[8,8,2304]{2,1,0:T(8,128)S(1)}, u32[]{:S(2)}, u32[]{:S(2)}) collective-permute-start(f32[8,8,2304]{2,1,0:T(8,128)S(1)} %pad_maximum_fusion), channel_id=1, source_target_pairs={{0,2},{1,3},{4,6},{5,7},{8,10},{9,11},{12,14},{13,15},{16,18},{17,... | collective-permute-start | bytes 1769480 | tf_op jit(solution)/shard_map/ppermute | solution.py:380
  86.4 1.4 collective-permute-done.8.refs_7_
  87.8 1.9 %shard_map.60 = (bf16[256,4096]{1,0:T(8,128)(2,1)S(1)}, bf16[256,4096]{1,0:T(8,128)(2,1)S(1)}, f32[1024,128]{1,0:T(8,128)S(1)}) custom-call(s32[1]{0:T(128)} %bitcast.me_ref.refs_0_, f32[2,8,4096]{2,1,0:T(8,128)S(1)} %get-tuple-element.62.refs_1_, f32[2,8,4096]{2,1,0:T(8,128)S(1)} %collective-permute-done.4.refs_2_, ...), custom_call_target="tpu_custom_call" | custom-call | tf_op jit(solution)/shard_map/pallas_call | solution.py:215
  89.6 23.4 %all_to_all.12 = f32[128,8,128]{2,1,0:T(8,128)S(1)} all-to-all(f32[128,8,128]{2,1,0:T(8,128)S(1)} %bitcast.10), channel_id=1, replica_groups=mesh['rows'=32,'vec'=4] {'rows','vec'}, dimensions={0} | all-to-all | bytes 1048576 | tf_op jit(solution)/shard_map/all_to_all | solution.py:386
  113.1 6.2 %shard_map.61 = (f32[1,32]{1,0:T(1,128)}, bf16[256,256]{1,0:T(8,128)(2,1)S(1)}, bf16[256,256]{1,0:T(8,128)(2,1)S(1)}, f32[8,8,4096]{2,1,0:T(8,128)S(1)}, f32[8,8...) custom-call(s32[1]{0:T(128)} %bitcast.me_ref.refs_0_, f32[1024,128]{1,0:T(8,128)S(1)} %bitcast.7, ...), custom_call_target="tpu_custom_call" | custom-call | tf_op jit(solution)/shard_map/pallas_call | solution.py:282
  119.4 3.7 %collective-permute-start.15 = (f32[8,8,4096]{2,1,0:T(8,128)S(1)}, f32[8,8,4096]{2,1,0:T(8,128)S(1)}, u32[]{:S(2)}, u32[]{:S(2)}) collective-permute-start(f32[8,8,4096]{2,1,0:T(8,128)S(1)} %get-tuple-element.87), channel_id=1, source_target_pairs={{0,3},{1,0},{2,1},{3,2},{4,7},{5,4},{6,5},{7,6},{8,11},{9,8},{10,9... | collective-permute-start | bytes 3145736 | tf_op jit(solution)/shard_map/ppermute | solution.py:370
  123.1 1.4 collective-permute-start.14
  124.5 3.1 %shard_map.62.own_ref = f32[8,4,8,4096]{3,2,1,0:T(8,128)} custom-call(s32[1]{0:T(128)} %bitcast.me_ref.refs_0_, bf16[256,256]{1,0:T(8,128)(2,1)S(1)} %get-tuple-element.79.w_high, bf16[256,256]{1,0:T(8,128)(2,1)S(1)} %get-tuple-element.80.w_low, bf16[256,4096]{1,0:T(8,128)(2,1)S(1)} %get-tuple-element.77.refs_2_.high_ref, ...), custom_call_target="tpu_custom_call" | custom-call | tf_op jit(solution)/shard_map/pallas_call | solution.py:326
  127.6 29.5 %collective-permute-done.14.across_ref = f32[8,8,1792]{2,1,0:T(8,128)S(1)} collective-permute-done((f32[8,8,1792]{2,1,0:T(8,128)S(1)}, f32[8,8,1792]{2,1,0:T(8,128)S(1)}, u32[]{:S(2)}, u32[]{:S(2)}) %collective-permute-start.14) | collective-permute-done | bytes 458784 | tf_op jit(solution)/shard_map/ppermute | solution.py:370
  157.1 1.5 shard_map.63
  (36 shorter events, 6.6 us)
Async XLA Ops:
  0.6 21.3 %copy-start = (f32[2,16,4096]{2,1,0:T(8,128)S(1)}, f32[2,16,4096]{2,1,0:T(8,128)}, u32[]{:S(2)}) copy-start(f32[2,16,4096]{2,1,0:T(8,128)} %z_ref.1) | copy-start | bytes 1572868
  0.6 21.3 %copy-start.1 = (f32[2,16,4096]{2,1,0:T(8,128)S(1)}, f32[2,16,4096]{2,1,0:T(8,128)}, u32[]{:S(2)}) copy-start(f32[2,16,4096]{2,1,0:T(8,128)} %c_ref.1) | copy-start | bytes 1572868
  3.5 12.5 %collective-permute-start = (f32[4,2,4,4096]{3,2,1,0:T(4,128)S(1)}, f32[4,2,4,4096]{3,2,1,0:T(4,128)S(1)}, u32[]{:S(2)}, u32[]{:S(2)}) collective-permute-start(f32[4,2,4,4096]{3,2,1,0:T(4,128)S(1)} %pad_maximum_fusion.4), channel_id=1, source_target_pairs={{4,0},{8,4},{12,8},{16,12},{20,16},{24,20},{28,24},{32,28},{36,32}... | collective-permute-start | bytes 1572872 | tf_op jit(solution)/shard_map/ppermute | solution.py:35
  9.4 12.0 %collective-permute-start.1 = (f32[4,2,4,4096]{3,2,1,0:T(4,128)S(1)}, f32[4,2,4,4096]{3,2,1,0:T(4,128)S(1)}, u32[]{:S(2)}, u32[]{:S(2)}) collective-permute-start(f32[4,2,4,4096]{3,2,1,0:T(4,128)S(1)} %pad_maximum_fusion.5), channel_id=1, source_target_pairs={{0,4},{4,8},{8,12},{12,16},{16,20},{20,24},{24,28},{28,32},{32,36}... | collective-permute-start | bytes 1572872 | tf_op jit(solution)/shard_map/ppermute | solution.py:34
  21.4 12.8 %collective-permute-start.2 = (f32[6,2,4,4096]{3,2,1,0:T(4,128)}, f32[6,2,4,4096]{3,2,1,0:T(4,128)S(1)}, u32[]{:S(2)}, u32[]{:S(2)}) collective-permute-start(f32[6,2,4,4096]{3,2,1,0:T(4,128)} %get-tuple-element.49), channel_id=1, source_target_pairs={{4,0},{8,4},{12,8},{16,12},{20,16},{24,20},{28,24},{32,28},{36,32}... | collective-permute-start | bytes 2359304 | tf_op jit(solution)/shard_map/ppermute | solution.py:35
  21.4 15.1 %collective-permute-start.3 = (f32[6,2,4,4096]{3,2,1,0:T(4,128)}, f32[6,2,4,4096]{3,2,1,0:T(4,128)}, u32[]{:S(2)}, u32[]{:S(2)}) collective-permute-start(f32[6,2,4,4096]{3,2,1,0:T(4,128)} %get-tuple-element.50), channel_id=1, source_target_pairs={{0,4},{4,8},{8,12},{12,16},{16,20},{20,24},{24,28},{28,32},{32,36}... | collective-permute-start | bytes 2359304 | tf_op jit(solution)/shard_map/ppermute | solution.py:34
  28.4 19.5 %collective-permute-start.4 = (f32[2,8,4096]{2,1,0:T(8,128)S(1)}, f32[2,8,4096]{2,1,0:T(8,128)S(1)}, u32[]{:S(2)}, u32[]{:S(2)}) collective-permute-start(f32[2,8,4096]{2,1,0:T(8,128)S(1)} %get-tuple-element.52), channel_id=1, source_target_pairs={{0,1},{1,2},{2,3},{3,0},{4,5},{5,6},{6,7},{7,4},{8,9},{9,10},{10,1... | collective-permute-start | bytes 786440 | tf_op jit(solution)/shard_map/ppermute | solution.py:370
  29.9 17.9 %collective-permute-start.5 = (f32[2,8,4096]{2,1,0:T(8,128)S(1)}, f32[2,8,4096]{2,1,0:T(8,128)S(1)}, u32[]{:S(2)}, u32[]{:S(2)}) collective-permute-start(f32[2,8,4096]{2,1,0:T(8,128)S(1)} %get-tuple-element.53), channel_id=1, source_target_pairs={{0,2},{1,3},{2,0},{3,1},{4,6},{5,7},{6,4},{7,5},{8,10},{9,11},{10,... | collective-permute-start | bytes 786440 | tf_op jit(solution)/shard_map/ppermute | solution.py:370
  32.8 15.0 %collective-permute-start.6 = (f32[2,8,4096]{2,1,0:T(8,128)S(1)}, f32[2,8,4096]{2,1,0:T(8,128)S(1)}, u32[]{:S(2)}, u32[]{:S(2)}) collective-permute-start(f32[2,8,4096]{2,1,0:T(8,128)S(1)} %get-tuple-element.54), channel_id=1, source_target_pairs={{0,3},{1,0},{2,1},{3,2},{4,7},{5,4},{6,5},{7,6},{8,11},{9,8},{10,9... | collective-permute-start | bytes 786440 | tf_op jit(solution)/shard_map/ppermute | solution.py:370
  47.9 22.8 %collective-permute-start.7 = (f32[6,8,4096]{2,1,0:T(8,128)S(1)}, f32[6,8,4096]{2,1,0:T(8,128)S(1)}, u32[]{:S(2)}, u32[]{:S(2)}) collective-permute-start(f32[6,8,4096]{2,1,0:T(8,128)S(1)} %get-tuple-element.67), channel_id=1, source_target_pairs={{0,1},{1,2},{2,3},{3,0},{4,5},{5,6},{6,7},{7,4},{8,9},{9,10},{10,1... | collective-permute-start | bytes 2359304 | tf_op jit(solution)/shard_map/ppermute | solution.py:370
  49.6 38.2 %collective-permute-start.8 = (f32[6,8,4096]{2,1,0:T(8,128)S(1)}, f32[6,8,4096]{2,1,0:T(8,128)S(1)}, u32[]{:S(2)}, u32[]{:S(2)}) collective-permute-start(f32[6,8,4096]{2,1,0:T(8,128)S(1)} %get-tuple-element.68), channel_id=1, source_target_pairs={{0,2},{1,3},{2,0},{3,1},{4,6},{5,7},{6,4},{7,5},{8,10},{9,11},{10,... | collective-permute-start | bytes 2359304 | tf_op jit(solution)/shard_map/ppermute | solution.py:370
  52.6 35.2 %collective-permute-start.9 = (f32[6,8,4096]{2,1,0:T(8,128)S(1)}, f32[6,8,4096]{2,1,0:T(8,128)S(1)}, u32[]{:S(2)}, u32[]{:S(2)}) collective-permute-start(f32[6,8,4096]{2,1,0:T(8,128)S(1)} %get-tuple-element.69), channel_id=1, source_target_pairs={{0,3},{1,0},{2,1},{3,2},{4,7},{5,4},{6,5},{7,6},{8,11},{9,8},{10,9... | collective-permute-start | bytes 2359304 | tf_op jit(solution)/shard_map/ppermute | solution.py:370
  70.7 42.4 %collective-permute-start.10 = (f32[8,8,2304]{2,1,0:T(8,128)S(1)}, f32[8,8,2304]{2,1,0:T(8,128)S(1)}, u32[]{:S(2)}, u32[]{:S(2)}) collective-permute-start(f32[8,8,2304]{2,1,0:T(8,128)S(1)} %pad_maximum_fusion.3), channel_id=1, source_target_pairs={{0,1},{1,2},{2,3},{4,5},{5,6},{6,7},{8,9},{9,10},{10,11},{12,13},{... | collective-permute-start | bytes 1769480 | tf_op jit(solution)/shard_map/ppermute | solution.py:379
  80.1 33.0 %collective-permute-start.11 = (f32[8,8,2304]{2,1,0:T(8,128)S(1)}, f32[8,8,2304]{2,1,0:T(8,128)S(1)}, u32[]{:S(2)}, u32[]{:S(2)}) collective-permute-start(f32[8,8,2304]{2,1,0:T(8,128)S(1)} %pad_maximum_fusion), channel_id=1, source_target_pairs={{0,2},{1,3},{4,6},{5,7},{8,10},{9,11},{12,14},{13,15},{16,18},{17,... | collective-permute-start | bytes 1769480 | tf_op jit(solution)/shard_map/ppermute | solution.py:380
  85.0 28.0 %collective-permute-start.12 = (f32[8,8,2304]{2,1,0:T(8,128)S(1)}, f32[8,8,2304]{2,1,0:T(8,128)S(1)}, u32[]{:S(2)}, u32[]{:S(2)}) collective-permute-start(f32[8,8,2304]{2,1,0:T(8,128)S(1)} %pad_maximum_fusion.1), channel_id=1, source_target_pairs={{0,3},{4,7},{8,11},{12,15},{16,19},{20,23},{24,27},{28,31},{32,35}... | collective-permute-start | bytes 1769480 | tf_op jit(solution)/shard_map/ppermute | solution.py:381
  119.3 37.8 %collective-permute-start.13 = (f32[8,8,4096]{2,1,0:T(8,128)S(1)}, f32[8,8,4096]{2,1,0:T(8,128)S(1)}, u32[]{:S(2)}, u32[]{:S(2)}) collective-permute-start(f32[8,8,4096]{2,1,0:T(8,128)S(1)} %get-tuple-element.85), channel_id=1, source_target_pairs={{0,1},{1,2},{2,3},{3,0},{4,5},{5,6},{6,7},{7,4},{8,9},{9,10},{10,1... | collective-permute-start | bytes 3145736 | tf_op jit(solution)/shard_map/ppermute | solution.py:370
  119.4 37.7 %collective-permute-start.15 = (f32[8,8,4096]{2,1,0:T(8,128)S(1)}, f32[8,8,4096]{2,1,0:T(8,128)S(1)}, u32[]{:S(2)}, u32[]{:S(2)}) collective-permute-start(f32[8,8,4096]{2,1,0:T(8,128)S(1)} %get-tuple-element.87), channel_id=1, source_target_pairs={{0,3},{1,0},{2,1},{3,2},{4,7},{5,4},{6,5},{7,6},{8,11},{9,8},{10,9... | collective-permute-start | bytes 3145736 | tf_op jit(solution)/shard_map/ppermute | solution.py:370
  123.1 34.0 %collective-permute-start.14 = (f32[8,8,1792]{2,1,0:T(8,128)S(1)}, f32[8,8,1792]{2,1,0:T(8,128)S(1)}, u32[]{:S(2)}, u32[]{:S(2)}) collective-permute-start(f32[8,8,1792]{2,1,0:T(8,128)S(1)} %get-tuple-element.86), channel_id=1, source_target_pairs={{0,2},{1,3},{2,0},{3,1},{4,6},{5,7},{6,4},{7,5},{8,10},{9,11},{10,... | collective-permute-start | bytes 1376264 | tf_op jit(solution)/shard_map/ppermute | solution.py:370

commit v7 on v5

--- a/solution.py
+++ b/solution.py
@@ -11,7 +11,7 @@
 STEPS = 3
 COUPLING = 0.35
 HALO = 4
-VMEM = 24 * 1024 * 1024
+VMEM = 32 * 1024 * 1024
 HIGHEST = lax.Precision.HIGHEST
 FULL = pl.BlockSpec(memory_space=pltpu.VMEM)
 SMEM = pl.BlockSpec(memory_space=pltpu.SMEM)

time: 158 us -> 158 us (level)
  no operation moved by 1% of the time
where the time goes in v7:
time: 158 us; the launch traced here: 157 us
  waiting for transfers between devices  59.9 us (38%)
  starting transfers between devices  39 us (25%)
  Pallas kernels  30.3 us (19%)
  blocking collectives  20.5 us (13%)
  local copies, waits for them, and re-layouts  6.15 us (4%)
    ppermute x9, waiting for transfers between devices, shifted(): return lax.ppermute(block, 'vec', [(i, (i + shift) % 4) for i in range(4)])  49.1 us
    all_to_all x1, blocking collectives, all_terms(): return lax.all_to_all(copies, ('rows', 'vec'), 0, 0, tiled=True)  20.5 us
    ppermute x9, starting transfers between devices, shifted(): return lax.ppermute(block, 'vec', [(i, (i + shift) % 4) for i in range(4)])  16.9 us
    pallas_call x1, Pallas kernels, push(): pl.pallas_call(tangent_kernel, grid=(count,), in_specs=[SMEM, pl.BlockSpe...  11.3 us
    ppermute x1, starting transfers between devices, opposite(): one = lax.ppermute(blocks[3], 'vec', [(0, 1), (1, 2), (2, 3)])  9.42 us
    ppermute x2, waiting for transfers between devices, neighbours(): above = lax.ppermute(last, 'rows', forward)  7.64 us
    pallas_call x1, Pallas kernels, push_first(): pl.pallas_call(first_kernel, grid=(count,), in_specs=[SMEM, pl.BlockSpec(...  6.42 us
    pallas_call x1, Pallas kernels, factorise(): pl.pallas_call(lambda *refs: factor_kernel(scale, *refs), in_specs=[SMEM]...  6.27 us
  transfers between devices with their start and end apart: 16, of which 6 were waited for; matrix products, arithmetic and copies ran while one was open for 2% of the time, Pallas kernels for 14%

profile of v7, /device:TPU:0, one launch (start us, length us, event | category | flops | bytes accessed | tf_op | source)
XLA Modules:
  0.0 157.3 jit_solution(5903636593279753503)
XLA Ops:
  0.7 1.4 fusion.1
  3.5 5.8 %collective-permute-start = (f32[4,2,4,4096]{3,2,1,0:T(4,128)S(1)}, f32[4,2,4,4096]{3,2,1,0:T(4,128)S(1)}, u32[]{:S(2)}, u32[]{:S(2)}) collective-permute-start(f32[4,2,4,4096]{3,2,1,0:T(4,128)S(1)} %pad_maximum_fusion), channel_id=1, source_target_pairs={{4,0},{8,4},{12,8},{16,12},{20,16},{24,20},{28,24},{32,28},{36,32}... | collective-permute-start | bytes 1572872 | tf_op jit(solution)/shard_map/ppermute | solution.py:35
  9.5 3.3 %fusion = (f32[6,2,4,4096]{3,2,1,0:T(4,128)}, f32[6,2,4,4096]{3,2,1,0:T(4,128)}) fusion(f32[8,2,16,4096]{3,2,1,0:T(8,128)} %u_ref.3), kind=kLoop, calls=%fused_computation.6 | loop fusion | bytes 3145728 | tf_op jit(solution)/shard_map/slice | solution.py:27
  12.8 3.2 %collective-permute-done.below_ref.fields_below = f32[4,2,4,4096]{3,2,1,0:T(4,128)S(1)} collective-permute-done((f32[4,2,4,4096]{3,2,1,0:T(4,128)S(1)}, f32[4,2,4,4096]{3,2,1,0:T(4,128)S(1)}, u32[]{:S(2)}, u32[]{:S(2)}) %collective-permute-start) | collective-permute-done | bytes 524320 | tf_op jit(solution)/shard_map/ppermute | solution.py:35
  16.0 5.4 %collective-permute-done.1.above_ref.fields_above = f32[4,2,4,4096]{3,2,1,0:T(4,128)S(1)} collective-permute-done((f32[4,2,4,4096]{3,2,1,0:T(4,128)S(1)}, f32[4,2,4,4096]{3,2,1,0:T(4,128)S(1)}, u32[]{:S(2)}, u32[]{:S(2)}) %collective-permute-start.1) | collective-permute-done | bytes 524320 | tf_op jit(solution)/shard_map/ppermute | solution.py:34
  21.9 6.4 %shard_map.58 = (f32[2,8,4096]{2,1,0:T(8,128)S(1)}, f32[2,8,4096]{2,1,0:T(8,128)S(1)}, f32[2,8,4096]{2,1,0:T(8,128)S(1)}, f32[2,8,4096]{2,1,0:T(8,128)S(1)}, f32...) custom-call(s32[1]{0:T(128)} %bitcast.me_ref.refs_0_, f32[8,2,16,4096]{3,2,1,0:T(8,128)} %u_ref.3, ...), custom_call_target="tpu_custom_call" | custom-call | flops 90000000 | bytes 18000000 | tf_op jit(solution)/shard_map/pallas_call | solution.py:108
  28.4 1.6 %collective-permute-start.4 = (f32[2,8,4096]{2,1,0:T(8,128)S(1)}, f32[2,8,4096]{2,1,0:T(8,128)S(1)}, u32[]{:S(2)}, u32[]{:S(2)}) collective-permute-start(f32[2,8,4096]{2,1,0:T(8,128)S(1)} %get-tuple-element.52), channel_id=1, source_target_pairs={{0,1},{1,2},{2,3},{3,0},{4,5},{5,6},{6,7},{7,4},{8,9},{9,10},{10,1... | collective-permute-start | bytes 786440 | tf_op jit(solution)/shard_map/ppermute | solution.py:370
  29.9 2.9 %collective-permute-start.5 = (f32[2,8,4096]{2,1,0:T(8,128)S(1)}, f32[2,8,4096]{2,1,0:T(8,128)S(1)}, u32[]{:S(2)}, u32[]{:S(2)}) collective-permute-start(f32[2,8,4096]{2,1,0:T(8,128)S(1)} %get-tuple-element.53), channel_id=1, source_target_pairs={{0,2},{1,3},{2,0},{3,1},{4,6},{5,7},{6,4},{7,5},{8,10},{9,11},{10,... | collective-permute-start | bytes 786440 | tf_op jit(solution)/shard_map/ppermute | solution.py:370
  34.3 2.2 %collective-permute-done.3.above_ref = f32[6,2,4,4096]{3,2,1,0:T(4,128)} collective-permute-done((f32[6,2,4,4096]{3,2,1,0:T(4,128)}, f32[6,2,4,4096]{3,2,1,0:T(4,128)}, u32[]{:S(2)}, u32[]{:S(2)}) %collective-permute-start.3) | collective-permute-done | bytes 786464 | tf_op jit(solution)/shard_map/ppermute | solution.py:34
  36.5 11.3 %shard_map.59 = (f32[6,8,4096]{2,1,0:T(8,128)S(1)}, f32[6,8,4096]{2,1,0:T(8,128)S(1)}, f32[6,8,4096]{2,1,0:T(8,128)S(1)}, f32[6,8,4096]{2,1,0:T(8,128)S(1)}) custom-call(s32[1]{0:T(128)} %bitcast.me_ref.refs_0_, f32[8,2,16,4096]{3,2,1,0:T(8,128)} %u_ref.3, f32[6,2,4,4096]{3,2,1,0:T(4,128)S(1)} %collective-permute-done.2.below_ref, ...), custom_call_target="tpu_custom_call" | custom-call | flops 180000000 | bytes 36000000 | tf_op jit(solution)/shard_map/pallas_call | solution.py:146
  47.9 1.7 %collective-permute-start.7 = (f32[6,8,4096]{2,1,0:T(8,128)S(1)}, f32[6,8,4096]{2,1,0:T(8,128)S(1)}, u32[]{:S(2)}, u32[]{:S(2)}) collective-permute-start(f32[6,8,4096]{2,1,0:T(8,128)S(1)} %get-tuple-element.67), channel_id=1, source_target_pairs={{0,1},{1,2},{2,3},{3,0},{4,5},{5,6},{6,7},{7,4},{8,9},{9,10},{10,1... | collective-permute-start | bytes 2359304 | tf_op jit(solution)/shard_map/ppermute | solution.py:370
  49.5 2.9 %collective-permute-start.8 = (f32[6,8,4096]{2,1,0:T(8,128)S(1)}, f32[6,8,4096]{2,1,0:T(8,128)S(1)}, u32[]{:S(2)}, u32[]{:S(2)}) collective-permute-start(f32[6,8,4096]{2,1,0:T(8,128)S(1)} %get-tuple-element.68), channel_id=1, source_target_pairs={{0,2},{1,3},{2,0},{3,1},{4,6},{5,7},{6,4},{7,5},{8,10},{9,11},{10,... | collective-permute-start | bytes 2359304 | tf_op jit(solution)/shard_map/ppermute | solution.py:370
  54.1 16.6 %collective-permute-done.7.refs_6_ = f32[6,8,4096]{2,1,0:T(8,128)S(1)} collective-permute-done((f32[6,8,4096]{2,1,0:T(8,128)S(1)}, f32[6,8,4096]{2,1,0:T(8,128)S(1)}, u32[]{:S(2)}, u32[]{:S(2)}) %collective-permute-start.7) | collective-permute-done | bytes 786464 | tf_op jit(solution)/shard_map/ppermute | solution.py:370
  70.7 9.4 %collective-permute-start.10 = (f32[8,8,2048]{2,1,0:T(8,128)S(1)}, f32[8,8,2048]{2,1,0:T(8,128)S(1)}, u32[]{:S(2)}, u32[]{:S(2)}) collective-permute-start(f32[8,8,2048]{2,1,0:T(8,128)S(1)} %pad_maximum_fusion.5), channel_id=1, source_target_pairs={{0,1},{1,2},{2,3},{4,5},{5,6},{6,7},{8,9},{9,10},{10,11},{12,13},{... | collective-permute-start | bytes 1572872 | tf_op jit(solution)/shard_map/ppermute | solution.py:379
  80.1 4.9 %collective-permute-start.11 = (f32[8,8,2048]{2,1,0:T(8,128)S(1)}, f32[8,8,2048]{2,1,0:T(8,128)S(1)}, u32[]{:S(2)}, u32[]{:S(2)}) collective-permute-start(f32[8,8,2048]{2,1,0:T(8,128)S(1)} %pad_maximum_fusion.2), channel_id=1, source_target_pairs={{0,2},{1,3},{4,6},{5,7},{8,10},{9,11},{12,14},{13,15},{16,18},{17,... | collective-permute-start | bytes 1572872 | tf_op jit(solution)/shard_map/ppermute | solution.py:380
  86.4 1.4 collective-permute-done.8.refs_7_
  87.8 1.9 %shard_map.60 = (bf16[256,4096]{1,0:T(8,128)(2,1)S(1)}, bf16[256,4096]{1,0:T(8,128)(2,1)S(1)}, f32[1024,128]{1,0:T(8,128)S(1)}) custom-call(s32[1]{0:T(128)} %bitcast.me_ref.refs_0_, f32[2,8,4096]{2,1,0:T(8,128)S(1)} %get-tuple-element.62.refs_1_, f32[2,8,4096]{2,1,0:T(8,128)S(1)} %collective-permute-done.4.refs_2_, ...), custom_call_target="tpu_custom_call" | custom-call | tf_op jit(solution)/shard_map/pallas_call | solution.py:215
  89.6 20.5 %all_to_all.12 = f32[128,8,128]{2,1,0:T(8,128)S(1)} all-to-all(f32[128,8,128]{2,1,0:T(8,128)S(1)} %bitcast.10), channel_id=1, replica_groups=mesh['rows'=32,'vec'=4] {'rows','vec'}, dimensions={0} | all-to-all | bytes 1048576 | tf_op jit(solution)/shard_map/all_to_all | solution.py:386
  110.1 6.3 %shard_map.61 = (f32[1,32]{1,0:T(1,128)}, bf16[256,256]{1,0:T(8,128)(2,1)S(1)}, bf16[256,256]{1,0:T(8,128)(2,1)S(1)}, f32[8,8,4096]{2,1,0:T(8,128)S(1)}, f32[8,8...) custom-call(s32[1]{0:T(128)} %bitcast.me_ref.refs_0_, f32[1024,128]{1,0:T(8,128)S(1)} %bitcast.7, ...), custom_call_target="tpu_custom_call" | custom-call | tf_op jit(solution)/shard_map/pallas_call | solution.py:282
  116.5 3.7 %collective-permute-start.15 = (f32[8,8,4096]{2,1,0:T(8,128)S(1)}, f32[8,8,4096]{2,1,0:T(8,128)S(1)}, u32[]{:S(2)}, u32[]{:S(2)}) collective-permute-start(f32[8,8,4096]{2,1,0:T(8,128)S(1)} %get-tuple-element.87), channel_id=1, source_target_pairs={{0,3},{1,0},{2,1},{3,2},{4,7},{5,4},{6,5},{7,6},{8,11},{9,8},{10,9... | collective-permute-start | bytes 3145736 | tf_op jit(solution)/shard_map/ppermute | solution.py:370
  120.2 1.4 collective-permute-start.14
  121.6 2.9 %shard_map.62.own_ref = f32[8,4,8,4096]{3,2,1,0:T(8,128)} custom-call(s32[1]{0:T(128)} %bitcast.me_ref.refs_0_, bf16[256,256]{1,0:T(8,128)(2,1)S(1)} %get-tuple-element.79.w_high, bf16[256,256]{1,0:T(8,128)(2,1)S(1)} %get-tuple-element.80.w_low, bf16[256,4096]{1,0:T(8,128)(2,1)S(1)} %get-tuple-element.77.refs_2_.high_ref, ...), custom_call_target="tpu_custom_call" | custom-call | tf_op jit(solution)/shard_map/pallas_call | solution.py:326
  124.5 31.1 %collective-permute-done.14.across_ref = f32[8,8,2048]{2,1,0:T(8,128)S(1)} collective-permute-done((f32[8,8,2048]{2,1,0:T(8,128)S(1)}, f32[8,8,2048]{2,1,0:T(8,128)S(1)}, u32[]{:S(2)}, u32[]{:S(2)}) %collective-permute-start.14) | collective-permute-done | bytes 524320 | tf_op jit(solution)/shard_map/ppermute | solution.py:370
  155.6 1.5 shard_map.63
  (36 shorter events, 6.6 us)
Async XLA Ops:
  0.6 21.3 %copy-start = (f32[2,16,4096]{2,1,0:T(8,128)S(1)}, f32[2,16,4096]{2,1,0:T(8,128)}, u32[]{:S(2)}) copy-start(f32[2,16,4096]{2,1,0:T(8,128)} %z_ref.1) | copy-start | bytes 1572868
  0.6 21.3 %copy-start.1 = (f32[2,16,4096]{2,1,0:T(8,128)S(1)}, f32[2,16,4096]{2,1,0:T(8,128)}, u32[]{:S(2)}) copy-start(f32[2,16,4096]{2,1,0:T(8,128)} %c_ref.1) | copy-start | bytes 1572868
  3.5 12.5 %collective-permute-start = (f32[4,2,4,4096]{3,2,1,0:T(4,128)S(1)}, f32[4,2,4,4096]{3,2,1,0:T(4,128)S(1)}, u32[]{:S(2)}, u32[]{:S(2)}) collective-permute-start(f32[4,2,4,4096]{3,2,1,0:T(4,128)S(1)} %pad_maximum_fusion), channel_id=1, source_target_pairs={{4,0},{8,4},{12,8},{16,12},{20,16},{24,20},{28,24},{32,28},{36,32}... | collective-permute-start | bytes 1572872 | tf_op jit(solution)/shard_map/ppermute | solution.py:35
  9.4 12.0 %collective-permute-start.1 = (f32[4,2,4,4096]{3,2,1,0:T(4,128)S(1)}, f32[4,2,4,4096]{3,2,1,0:T(4,128)S(1)}, u32[]{:S(2)}, u32[]{:S(2)}) collective-permute-start(f32[4,2,4,4096]{3,2,1,0:T(4,128)S(1)} %pad_maximum_fusion.1), channel_id=1, source_target_pairs={{0,4},{4,8},{8,12},{12,16},{16,20},{20,24},{24,28},{28,32},{32,36}... | collective-permute-start | bytes 1572872 | tf_op jit(solution)/shard_map/ppermute | solution.py:34
  21.4 12.8 %collective-permute-start.2 = (f32[6,2,4,4096]{3,2,1,0:T(4,128)}, f32[6,2,4,4096]{3,2,1,0:T(4,128)S(1)}, u32[]{:S(2)}, u32[]{:S(2)}) collective-permute-start(f32[6,2,4,4096]{3,2,1,0:T(4,128)} %get-tuple-element.49), channel_id=1, source_target_pairs={{4,0},{8,4},{12,8},{16,12},{20,16},{24,20},{28,24},{32,28},{36,32}... | collective-permute-start | bytes 2359304 | tf_op jit(solution)/shard_map/ppermute | solution.py:35
  21.4 15.1 %collective-permute-start.3 = (f32[6,2,4,4096]{3,2,1,0:T(4,128)}, f32[6,2,4,4096]{3,2,1,0:T(4,128)}, u32[]{:S(2)}, u32[]{:S(2)}) collective-permute-start(f32[6,2,4,4096]{3,2,1,0:T(4,128)} %get-tuple-element.50), channel_id=1, source_target_pairs={{0,4},{4,8},{8,12},{12,16},{16,20},{20,24},{24,28},{28,32},{32,36}... | collective-permute-start | bytes 2359304 | tf_op jit(solution)/shard_map/ppermute | solution.py:34
  28.4 19.5 %collective-permute-start.4 = (f32[2,8,4096]{2,1,0:T(8,128)S(1)}, f32[2,8,4096]{2,1,0:T(8,128)S(1)}, u32[]{:S(2)}, u32[]{:S(2)}) collective-permute-start(f32[2,8,4096]{2,1,0:T(8,128)S(1)} %get-tuple-element.52), channel_id=1, source_target_pairs={{0,1},{1,2},{2,3},{3,0},{4,5},{5,6},{6,7},{7,4},{8,9},{9,10},{10,1... | collective-permute-start | bytes 786440 | tf_op jit(solution)/shard_map/ppermute | solution.py:370
  29.9 17.9 %collective-permute-start.5 = (f32[2,8,4096]{2,1,0:T(8,128)S(1)}, f32[2,8,4096]{2,1,0:T(8,128)S(1)}, u32[]{:S(2)}, u32[]{:S(2)}) collective-permute-start(f32[2,8,4096]{2,1,0:T(8,128)S(1)} %get-tuple-element.53), channel_id=1, source_target_pairs={{0,2},{1,3},{2,0},{3,1},{4,6},{5,7},{6,4},{7,5},{8,10},{9,11},{10,... | collective-permute-start | bytes 786440 | tf_op jit(solution)/shard_map/ppermute | solution.py:370
  32.8 15.0 %collective-permute-start.6 = (f32[2,8,4096]{2,1,0:T(8,128)S(1)}, f32[2,8,4096]{2,1,0:T(8,128)S(1)}, u32[]{:S(2)}, u32[]{:S(2)}) collective-permute-start(f32[2,8,4096]{2,1,0:T(8,128)S(1)} %get-tuple-element.54), channel_id=1, source_target_pairs={{0,3},{1,0},{2,1},{3,2},{4,7},{5,4},{6,5},{7,6},{8,11},{9,8},{10,9... | collective-permute-start | bytes 786440 | tf_op jit(solution)/shard_map/ppermute | solution.py:370
  47.9 22.8 %collective-permute-start.7 = (f32[6,8,4096]{2,1,0:T(8,128)S(1)}, f32[6,8,4096]{2,1,0:T(8,128)S(1)}, u32[]{:S(2)}, u32[]{:S(2)}) collective-permute-start(f32[6,8,4096]{2,1,0:T(8,128)S(1)} %get-tuple-element.67), channel_id=1, source_target_pairs={{0,1},{1,2},{2,3},{3,0},{4,5},{5,6},{6,7},{7,4},{8,9},{9,10},{10,1... | collective-permute-start | bytes 2359304 | tf_op jit(solution)/shard_map/ppermute | solution.py:370
  49.5 38.2 %collective-permute-start.8 = (f32[6,8,4096]{2,1,0:T(8,128)S(1)}, f32[6,8,4096]{2,1,0:T(8,128)S(1)}, u32[]{:S(2)}, u32[]{:S(2)}) collective-permute-start(f32[6,8,4096]{2,1,0:T(8,128)S(1)} %get-tuple-element.68), channel_id=1, source_target_pairs={{0,2},{1,3},{2,0},{3,1},{4,6},{5,7},{6,4},{7,5},{8,10},{9,11},{10,... | collective-permute-start | bytes 2359304 | tf_op jit(solution)/shard_map/ppermute | solution.py:370
  52.4 35.3 %collective-permute-start.9 = (f32[6,8,4096]{2,1,0:T(8,128)S(1)}, f32[6,8,4096]{2,1,0:T(8,128)S(1)}, u32[]{:S(2)}, u32[]{:S(2)}) collective-permute-start(f32[6,8,4096]{2,1,0:T(8,128)S(1)} %get-tuple-element.69), channel_id=1, source_target_pairs={{0,3},{1,0},{2,1},{3,2},{4,7},{5,4},{6,5},{7,6},{8,11},{9,8},{10,9... | collective-permute-start | bytes 2359304 | tf_op jit(solution)/shard_map/ppermute | solution.py:370
  70.7 39.5 %collective-permute-start.10 = (f32[8,8,2048]{2,1,0:T(8,128)S(1)}, f32[8,8,2048]{2,1,0:T(8,128)S(1)}, u32[]{:S(2)}, u32[]{:S(2)}) collective-permute-start(f32[8,8,2048]{2,1,0:T(8,128)S(1)} %pad_maximum_fusion.5), channel_id=1, source_target_pairs={{0,1},{1,2},{2,3},{4,5},{5,6},{6,7},{8,9},{9,10},{10,11},{12,13},{... | collective-permute-start | bytes 1572872 | tf_op jit(solution)/shard_map/ppermute | solution.py:379
  80.1 30.0 %collective-permute-start.11 = (f32[8,8,2048]{2,1,0:T(8,128)S(1)}, f32[8,8,2048]{2,1,0:T(8,128)S(1)}, u32[]{:S(2)}, u32[]{:S(2)}) collective-permute-start(f32[8,8,2048]{2,1,0:T(8,128)S(1)} %pad_maximum_fusion.2), channel_id=1, source_target_pairs={{0,2},{1,3},{4,6},{5,7},{8,10},{9,11},{12,14},{13,15},{16,18},{17,... | collective-permute-start | bytes 1572872 | tf_op jit(solution)/shard_map/ppermute | solution.py:380
  85.0 25.1 %collective-permute-start.12 = (f32[8,8,2048]{2,1,0:T(8,128)S(1)}, f32[8,8,2048]{2,1,0:T(8,128)S(1)}, u32[]{:S(2)}, u32[]{:S(2)}) collective-permute-start(f32[8,8,2048]{2,1,0:T(8,128)S(1)} %pad_maximum_fusion.3), channel_id=1, source_target_pairs={{0,3},{4,7},{8,11},{12,15},{16,19},{20,23},{24,27},{28,31},{32,35}... | collective-permute-start | bytes 1572872 | tf_op jit(solution)/shard_map/ppermute | solution.py:381
  116.4 39.2 %collective-permute-start.13 = (f32[8,8,4096]{2,1,0:T(8,128)S(1)}, f32[8,8,4096]{2,1,0:T(8,128)S(1)}, u32[]{:S(2)}, u32[]{:S(2)}) collective-permute-start(f32[8,8,4096]{2,1,0:T(8,128)S(1)} %get-tuple-element.85), channel_id=1, source_target_pairs={{0,1},{1,2},{2,3},{3,0},{4,5},{5,6},{6,7},{7,4},{8,9},{9,10},{10,1... | collective-permute-start | bytes 3145736 | tf_op jit(solution)/shard_map/ppermute | solution.py:370
  116.5 39.1 %collective-permute-start.15 = (f32[8,8,4096]{2,1,0:T(8,128)S(1)}, f32[8,8,4096]{2,1,0:T(8,128)S(1)}, u32[]{:S(2)}, u32[]{:S(2)}) collective-permute-start(f32[8,8,4096]{2,1,0:T(8,128)S(1)} %get-tuple-element.87), channel_id=1, source_target_pairs={{0,3},{1,0},{2,1},{3,2},{4,7},{5,4},{6,5},{7,6},{8,11},{9,8},{10,9... | collective-permute-start | bytes 3145736 | tf_op jit(solution)/shard_map/ppermute | solution.py:370
  120.2 35.4 %collective-permute-start.14 = (f32[8,8,2048]{2,1,0:T(8,128)S(1)}, f32[8,8,2048]{2,1,0:T(8,128)S(1)}, u32[]{:S(2)}, u32[]{:S(2)}) collective-permute-start(f32[8,8,2048]{2,1,0:T(8,128)S(1)} %get-tuple-element.86), channel_id=1, source_target_pairs={{0,2},{1,3},{2,0},{3,1},{4,6},{5,7},{6,4},{7,5},{8,10},{9,11},{10,... | collective-permute-start | bytes 1572872 | tf_op jit(solution)/shard_map/ppermute | solution.py:370
